TPU v7x, 32 devices: a whole 2x2x4 slice. The times are simulated.
32 devices in a mesh: dp: 4 (over y, x), expert: 8 (over z, core).
Axes of the slice: x: 2, y: 2, z: 4, core: 2. Of those that a mesh axis runs over, the one named last changes fastest.
Arguments:
- tokens: bfloat16 [31520, 512], P(('dp', 'expert')), may hold values from -6 to 6
- targets: bfloat16 [31520, 512], P(('dp', 'expert')), may hold values from -6 to 6
- valid_mask: int32 [31520], P(('dp', 'expert')), may hold values from 0 to 1
- routes: int32 [31520, 2], P(('dp', 'expert')), may hold values from 0 to 7, as said below
- slot_ids: int32 [31520, 2], P(('dp', 'expert')), may hold values from 0 to 312, as said below
- ln1_gain: bfloat16 [512], P(('dp', 'expert')), may hold values from 0.5 to 1.5
- qkv_weight: bfloat16 [512, 1536], P(('dp', 'expert')), may hold values from -0.25 to 0.25
- out_weight: bfloat16 [512, 512], P(('dp', 'expert')), may hold values from -0.5 to 0.5
- ln2_gain: bfloat16 [512], P(('dp', 'expert')), may hold values from 0.5 to 1.5
- router_weight: bfloat16 [512, 8], P(('dp', 'expert')), may hold values from -0.1875 to 0.1875
- expert_in: bfloat16 [8, 512, 2048], P('expert', 'dp'), may hold values from -0.25 to 0.25
- expert_out: bfloat16 [8, 2048, 512], P('expert', 'dp'), may hold values from -0.1875 to 0.1875
Outputs:
- block_out: bfloat16 [31520, 512], P(('dp', 'expert'))
- loss: float32 [], replicated
- tokens_grad: float32 [31520, 512], P(('dp', 'expert'))
- ln1_gain_grad: float32 [512], P(('dp', 'expert'))
- qkv_grad: float32 [512, 1536], P(('dp', 'expert'))
- out_grad: float32 [512, 512], P(('dp', 'expert'))
- ln2_gain_grad: float32 [512], P(('dp', 'expert'))
- router_grad: float32 [512, 8], P(('dp', 'expert'))
- expert_in_grad: float32 [8, 512, 2048], P('expert', 'dp')
- expert_out_grad: float32 [8, 2048, 512], P('expert', 'dp')
Inputs may be any that keep to these rules, and one draw needn't show every extreme that they name: `routes`: the two experts of a token differ. `slot_ids`: within each block of 985 rows (one device's tokens) the kept pairs routed to one expert have distinct slots; 312 marks a dropped pair. In every draw one expert holds all 312 slots from every block.
All inputs are finite; a program needn't handle non-finite values.
Results may differ from a plain program's by a relative error of at most 0.009.
Values may be sent and summed in bfloat16 or wider, within the bound.
A program may use at most 192 MiB of HBM per device.

v0:
```python
import jax
import jax.numpy as jnp
from jax import lax
from jax.sharding import PartitionSpec as P

HEADS = 8
IMG_DEV = 5


HIGH = lax.Precision.HIGHEST
EPS = 1e-06


def layer_norm(values, scale_gain):
    row_mean = jnp.mean(values, axis=-1, keepdims=True)
    centered = values - row_mean
    variance = jnp.mean(centered * centered, axis=-1, keepdims=True)
    inverse = lax.rsqrt(variance + EPS)
    normed = centered * inverse
    return (normed * scale_gain, normed, inverse)


def layer_norm_back(grad_in, normed, inverse, scale_gain):
    scaled = grad_in * scale_gain
    gain_grad = jnp.sum(grad_in * normed, axis=0)
    inner_term = (
        scaled
        - jnp.mean(scaled, axis=-1, keepdims=True)
        - normed * jnp.mean(scaled * normed, axis=-1, keepdims=True)
    )
    return (inverse * inner_term, gain_grad)


def contract_rows(left_side, right_side):
    return lax.dot_general(
        left_side, right_side, (((0,), (0,)), ((), ())), preferred_element_type=jnp.float32
    )


def contract_cols(left_side, right_side):
    return lax.dot_general(
        left_side, right_side, (((1,), (1,)), ((), ())), preferred_element_type=jnp.float32
    )


def exact_gelu(values):
    return jax.nn.gelu(values, approximate=False)


def split_heads(qkv_low, images, head_count):
    row_count, triple_width = qkv_low.shape
    head_dim = triple_width // (3 * head_count)
    pieces = qkv_low.reshape(images, row_count // images, 3, head_count, head_dim)
    return (pieces[:, :, 0], pieces[:, :, 1], pieces[:, :, 2], head_dim ** (-0.5))


def attention_forward(qkv_low, images, head_count):
    queries, key_rows, values, score_scale = split_heads(qkv_low, images, head_count)
    scores = (
        jnp.einsum("ilhd,imhd->ihlm", queries, key_rows, preferred_element_type=jnp.float32)
        * score_scale
    )
    row_max = jnp.max(scores, axis=-1, keepdims=True)
    exp_scores = jnp.exp(scores - row_max)
    row_sum = jnp.sum(exp_scores, axis=-1, keepdims=True)
    weights_low = (exp_scores / row_sum).astype(jnp.bfloat16)
    log_total = row_max + jnp.log(row_sum)
    mixed_rows = jnp.einsum(
        "ihlm,imhd->ilhd", weights_low, values, preferred_element_type=jnp.float32
    )
    return (mixed_rows.reshape(qkv_low.shape[0], -1).astype(jnp.bfloat16), log_total)


def attention_back(qkv_low, log_total, grad_mixed, images, head_count):
    queries, key_rows, values, score_scale = split_heads(qkv_low, images, head_count)
    scores = (
        jnp.einsum("ilhd,imhd->ihlm", queries, key_rows, preferred_element_type=jnp.float32)
        * score_scale
    )
    weights_full = jnp.exp(scores - log_total)
    weights_low = weights_full.astype(jnp.bfloat16)
    grad_heads = grad_mixed.reshape(queries.shape)
    grad_weights = jnp.einsum(
        "ilhd,imhd->ihlm", grad_heads, values, preferred_element_type=jnp.float32
    )
    grad_values = jnp.einsum(
        "ihlm,ilhd->imhd", weights_low, grad_heads, preferred_element_type=jnp.float32
    )
    grad_scores = weights_full * (
        grad_weights - jnp.sum(weights_full * grad_weights, axis=-1, keepdims=True)
    )
    grad_low = grad_scores.astype(jnp.bfloat16)
    grad_queries = (
        jnp.einsum("ihlm,imhd->ilhd", grad_low, key_rows, preferred_element_type=jnp.float32)
        * score_scale
    )
    grad_keys = (
        jnp.einsum("ihlm,ilhd->imhd", grad_low, queries, preferred_element_type=jnp.float32)
        * score_scale
    )
    stacked = jnp.stack([grad_queries, grad_keys, grad_values], axis=2)
    return stacked.reshape(qkv_low.shape).astype(jnp.bfloat16)


def expert_forward(rows_in, weight_in, weight_out, block_size):
    result = jnp.zeros((rows_in.shape[0], weight_out.shape[1]), jnp.float32)
    for offset in range(0, weight_in.shape[1], block_size):
        pre_act = jnp.dot(
            rows_in, weight_in[:, offset : offset + block_size], preferred_element_type=jnp.float32
        )
        hidden = exact_gelu(pre_act).astype(jnp.bfloat16)
        result = result + jnp.dot(
            hidden, weight_out[offset : offset + block_size], preferred_element_type=jnp.float32
        )
    return result


def expert_back(rows_in, weight_in, weight_out, grad_rows_out, block_size):
    grad_rows = jnp.zeros(rows_in.shape, jnp.float32)
    grads_first = []
    grads_second = []
    for offset in range(0, weight_in.shape[1], block_size):
        slice_in = weight_in[:, offset : offset + block_size]
        slice_out = weight_out[offset : offset + block_size]
        pre_act = jnp.dot(rows_in, slice_in, preferred_element_type=jnp.float32)
        hidden, gelu_back = jax.vjp(exact_gelu, pre_act)
        grads_second.append(contract_rows(hidden.astype(jnp.bfloat16), grad_rows_out))
        grad_hidden = contract_cols(grad_rows_out, slice_out)
        grad_pre = gelu_back(grad_hidden)[0].astype(jnp.bfloat16)
        grads_first.append(contract_rows(rows_in, grad_pre))
        grad_rows = grad_rows + contract_cols(grad_pre, slice_in)
    return (grad_rows, jnp.concatenate(grads_first, axis=1), jnp.concatenate(grads_second, axis=0))


def shards(
    tokens,
    targets,
    valid_mask,
    routes,
    slot_ids,
    ln1_gain,
    qkv_weight,
    out_weight,
    ln2_gain,
    router_weight,
    expert_in,
    expert_out,
):
    tok_rows, model_width = tokens.shape
    experts = lax.axis_size("expert")
    total_tokens = tok_rows * lax.axis_size("dp") * experts
    capacity = (5 * tok_rows // 2 // experts + 7) // 8 * 8
    dense_full = (
        lax.all_gather(ln1_gain, ("dp", "expert"), axis=0, tiled=True),
        lax.all_gather(qkv_weight, ("dp", "expert"), axis=0, tiled=True),
        lax.all_gather(out_weight, ("dp", "expert"), axis=0, tiled=True),
        lax.all_gather(ln2_gain, ("dp", "expert"), axis=0, tiled=True),
        lax.all_gather(router_weight, ("dp", "expert"), axis=0, tiled=True),
    )
    gain_one, qkv_full, out_full, gain_two, router_full = dense_full
    expert_full = (
        lax.all_gather(expert_in, "dp", axis=1, tiled=True),
        lax.all_gather(expert_out, "dp", axis=1, tiled=True),
    )
    weight_in = expert_full[0][0]
    weight_out = expert_full[1][0]
    valid_f = valid_mask.astype(jnp.float32)
    valid_count = lax.psum(jnp.sum(valid_f), ("dp", "expert"))
    inputs_f = tokens.astype(jnp.float32)
    gain_one_f = gain_one.astype(jnp.float32)
    gain_two_f = gain_two.astype(jnp.float32)
    norm_one, normed_one, inverse_one = layer_norm(inputs_f, gain_one_f)
    act_one = norm_one.astype(jnp.bfloat16)
    qkv_low = jnp.dot(act_one, qkv_full, preferred_element_type=jnp.float32).astype(jnp.bfloat16)
    mixed_low, log_total = attention_forward(qkv_low, IMG_DEV, HEADS)
    residual = inputs_f + jnp.dot(mixed_low, out_full, preferred_element_type=jnp.float32)
    norm_two, normed_two, inverse_two = layer_norm(residual, gain_two_f)
    act_two = norm_two.astype(jnp.bfloat16)
    gate_probs = jax.nn.softmax(
        jnp.dot(act_two, router_full, preferred_element_type=jnp.float32), axis=-1
    )
    expert_ids = lax.broadcasted_iota(jnp.int32, (1, experts), 1)
    first_pick = (routes[:, 0:1] == expert_ids).astype(jnp.float32)
    second_pick = (routes[:, 1:2] == expert_ids).astype(jnp.float32)
    gate_first = jnp.sum(gate_probs * first_pick, axis=-1, keepdims=True)
    gate_second = jnp.sum(gate_probs * second_pick, axis=-1, keepdims=True)
    target_slot = jnp.where(slot_ids < capacity, routes * capacity + slot_ids, -1)
    slot_columns = lax.broadcasted_iota(jnp.int32, (1, experts * capacity), 1)
    first_hot = (target_slot[:, 0:1] == slot_columns).astype(jnp.bfloat16)
    second_hot = (target_slot[:, 1:2] == slot_columns).astype(jnp.bfloat16)
    both_hot = first_hot + second_hot
    outgoing = contract_rows(both_hot, act_two).astype(jnp.bfloat16)
    arrived = lax.all_to_all(
        outgoing.reshape(experts, capacity, model_width),
        "expert",
        split_axis=0,
        concat_axis=0,
        tiled=True,
    ).reshape(-1, model_width)
    hidden_block = min(512, weight_in.shape[1])
    produced = expert_forward(arrived, weight_in, weight_out, hidden_block).astype(jnp.bfloat16)
    returned = lax.all_to_all(
        produced.reshape(experts, capacity, model_width),
        "expert",
        split_axis=0,
        concat_axis=0,
        tiled=True,
    ).reshape(-1, model_width)
    from_first = jnp.dot(first_hot, returned, preferred_element_type=jnp.float32)
    from_second = jnp.dot(second_hot, returned, preferred_element_type=jnp.float32)
    output = residual + gate_first * from_first + gate_second * from_second
    residue = output - targets.astype(jnp.float32)
    local_loss = jnp.sum(valid_f * jnp.mean(residue * residue, axis=-1))
    loss_sum = lax.psum(local_loss, ("dp", "expert"))
    loss_value = loss_sum / valid_count
    grad_out = total_tokens / valid_count * valid_f[:, None] * residue
    dense_back = (
        lax.all_gather(ln1_gain, ("dp", "expert"), axis=0, tiled=True),
        lax.all_gather(qkv_weight, ("dp", "expert"), axis=0, tiled=True),
        lax.all_gather(out_weight, ("dp", "expert"), axis=0, tiled=True),
        lax.all_gather(ln2_gain, ("dp", "expert"), axis=0, tiled=True),
        lax.all_gather(router_weight, ("dp", "expert"), axis=0, tiled=True),
    )
    expert_back_full = (
        lax.all_gather(expert_in, "dp", axis=1, tiled=True),
        lax.all_gather(expert_out, "dp", axis=1, tiled=True),
    )
    qkv_back = dense_back[1]
    out_back = dense_back[2]
    router_back = dense_back[4]
    weight_in_back = expert_back_full[0][0]
    weight_out_back = expert_back_full[1][0]
    slot_grads = (
        contract_rows(first_hot, (gate_first * grad_out).astype(jnp.bfloat16))
        + contract_rows(second_hot, (gate_second * grad_out).astype(jnp.bfloat16))
    ).astype(jnp.bfloat16)
    expert_grad_rows = lax.all_to_all(
        slot_grads.reshape(experts, capacity, model_width),
        "expert",
        split_axis=0,
        concat_axis=0,
        tiled=True,
    ).reshape(-1, model_width)
    grad_rows, grad_first_weight, grad_second_weight = expert_back(
        arrived, weight_in_back, weight_out_back, expert_grad_rows, hidden_block
    )
    grad_back = lax.all_to_all(
        grad_rows.astype(jnp.bfloat16).reshape(experts, capacity, model_width),
        "expert",
        split_axis=0,
        concat_axis=0,
        tiled=True,
    ).reshape(-1, model_width)
    grad_act_two = jnp.dot(both_hot, grad_back, preferred_element_type=jnp.float32)
    gate_grad = first_pick * jnp.sum(
        grad_out * from_first, axis=-1, keepdims=True
    ) + second_pick * jnp.sum(grad_out * from_second, axis=-1, keepdims=True)
    logit_grad = gate_probs * (gate_grad - jnp.sum(gate_probs * gate_grad, axis=-1, keepdims=True))
    router_f = router_back.astype(jnp.float32)
    grad_act_two = grad_act_two + lax.dot_general(
        logit_grad,
        router_f,
        (((1,), (1,)), ((), ())),
        precision=HIGH,
        preferred_element_type=jnp.float32,
    )
    router_grad = lax.dot_general(
        act_two.astype(jnp.float32),
        logit_grad,
        (((0,), (0,)), ((), ())),
        precision=HIGH,
        preferred_element_type=jnp.float32,
    )
    grad_norm_two, gain_two_grad = layer_norm_back(
        grad_act_two, normed_two, inverse_two, gain_two_f
    )
    grad_resid = grad_out + grad_norm_two
    branch_grad = grad_resid.astype(jnp.bfloat16)
    out_weight_grad = contract_rows(mixed_low, branch_grad)
    grad_mixed = contract_cols(branch_grad, out_back).astype(jnp.bfloat16)
    qkv_grad_low = attention_back(qkv_low, log_total, grad_mixed, IMG_DEV, HEADS)
    qkv_weight_grad = contract_rows(act_one, qkv_grad_low)
    grad_act_one = contract_cols(qkv_grad_low, qkv_back)
    grad_norm_one, gain_one_grad = layer_norm_back(
        grad_act_one, normed_one, inverse_one, gain_one_f
    )
    tokens_grad = grad_resid + grad_norm_one
    dense_grads = (
        lax.psum_scatter(gain_one_grad, ("dp", "expert"), scatter_dimension=0, tiled=True),
        lax.psum_scatter(qkv_weight_grad, ("dp", "expert"), scatter_dimension=0, tiled=True),
        lax.psum_scatter(out_weight_grad, ("dp", "expert"), scatter_dimension=0, tiled=True),
        lax.psum_scatter(gain_two_grad, ("dp", "expert"), scatter_dimension=0, tiled=True),
        lax.psum_scatter(router_grad, ("dp", "expert"), scatter_dimension=0, tiled=True),
    )
    expert_grads = (
        lax.psum_scatter(
            grad_first_weight[None].astype(jnp.bfloat16), "dp", scatter_dimension=1, tiled=True
        ).astype(jnp.float32),
        lax.psum_scatter(
            grad_second_weight[None].astype(jnp.bfloat16), "dp", scatter_dimension=1, tiled=True
        ).astype(jnp.float32),
    )
    first_result = expert_grads[0]
    second_result = expert_grads[1]
    return (
        output.astype(jnp.bfloat16),
        loss_value,
        tokens_grad,
        dense_grads[0],
        dense_grads[1],
        dense_grads[2],
        dense_grads[3],
        dense_grads[4],
        first_result,
        second_result,
    )


def solution(mesh):
    in_specs = (
        P(("dp", "expert"), None),
        P(("dp", "expert"), None),
        P(("dp", "expert")),
        P(("dp", "expert"), None),
        P(("dp", "expert"), None),
        P(("dp", "expert")),
        P(("dp", "expert"), None),
        P(("dp", "expert"), None),
        P(("dp", "expert")),
        P(("dp", "expert"), None),
        P("expert", "dp", None),
        P("expert", "dp", None),
    )
    out_specs = (
        P(("dp", "expert"), None),
        P(),
        P(("dp", "expert"), None),
        P(("dp", "expert")),
        P(("dp", "expert"), None),
        P(("dp", "expert"), None),
        P(("dp", "expert")),
        P(("dp", "expert"), None),
        P("expert", "dp", None),
        P("expert", "dp", None),
    )
    return jax.shard_map(shards, mesh=mesh, in_specs=in_specs, out_specs=out_specs, check_vma=False)
```

profile of v0, /device:TPU:0, one launch (start us, length us, event | category | flops | bytes accessed | tf_op | source)
XLA Modules:
  0.0 898.8 jit_solution(4426230858950665184)
XLA Ops:
  10.5 42.2 %all-reduce.5 = (bf16[512]{0:T(512)(128)(2,1)S(1)}, bf16[512]{0:T(512)(128)(2,1)S(1)}) all-reduce(bf16[512]{0:T(512)(128)(2,1)S(1)} %dynamic-update-slice, bf16[512]{0:T(512)(128)(2,1)S(1)} %dynamic-update-slice.1), channel_id=1, replica_groups=mesh['dp'=4,'expert'=8] {'dp','expert'}, use_global_device_ids=true, to_apply=%add | all-reduce | flops 1024 | bytes 4096
  56.6 45.3 %all_gather.28 = bf16[512,512]{1,0:T(8,128)(2,1)} all-gather(bf16[16,512]{1,0:T(8,128)(2,1)} %param.19), channel_id=1, replica_groups=mesh['dp'=4,'expert'=8] {'dp','expert'}, dimensions={0}, use_global_device_ids=true | all-gather | bytes 540672 | tf_op jit(solution)/shard_map/all_gather | solution.py:156
  155.8 36.7 %all-gather.7.cloned.1.call-done = bf16[1,512,2048]{2,1,0:T(8,128)(2,1)} async-done(((bf16[1,128,2048]{2,1,0:T(8,128)(2,1)}), bf16[1,512,2048]{2,1,0:T(8,128)(2,1)}) %all-gather.7.cloned.1.call-update) | async-done | bytes 2097168 | tf_op jit(solution)/shard_map/all_gather | solution.py:162
  192.5 20.9 %all-to-all-done = bf16[8,312,512]{2,1,0:T(8,128)(2,1)S(1)} async-done(((bf16[8,312,512]{2,1,0:T(8,128)(2,1)}), bf16[8,312,512]{2,1,0:T(8,128)(2,1)S(1)}, u32[]{:S(2)}, u32[]{:S(2)}) %all-to-all-start) | async-done | bytes 2555936 | tf_op jit(solution)/shard_map/all_to_all | solution.py:193
  214.9 15.7 %multiply_convert_fusion.2 = (bf16[2496,512]{1,0:T(8,128)(2,1)S(1)}, f32[2496,512]{1,0:T(8,128)}, f32[2496,512]{1,0:T(8,128)}) fusion(bf16[2496,512]{1,0:T(8,128)(2,1)} %bitcast.160, bf16[512,2048]{1,0:T(8,128)(2,1)} %bitcast.170), kind=kOutput, calls=%fused_computation.44 | convolution fusion | flops 1391689728 | bytes 15859712 | tf_op jit(solution)/shard_map/dot_general | solution.py:108
  230.6 13.6 %multiply_convert_fusion.4 = (bf16[2496,512]{1,0:T(8,128)(2,1)}, f32[2496,512]{1,0:T(8,128)}, f32[2496,512]{1,0:T(8,128)}) fusion(bf16[2496,512]{1,0:T(8,128)(2,1)S(1)} %bitcast.161, bf16[512,2048]{1,0:T(8,128)(2,1)S(1)} %bitcast.172), kind=kOutput, calls=%fused_computation.70 | convolution fusion | flops 1391689728 | bytes 15859712 | tf_op jit(solution)/shard_map/dot_general | solution.py:108
  244.2 13.5 %multiply_convert_fusion.3 = (bf16[2496,512]{1,0:T(8,128)(2,1)}, f32[2496,512]{1,0:T(8,128)}, f32[2496,512]{1,0:T(8,128)}) fusion(bf16[2496,512]{1,0:T(8,128)(2,1)S(1)} %bitcast.162, bf16[512,2048]{1,0:T(8,128)(2,1)S(1)} %bitcast.173), kind=kOutput, calls=%fused_computation.57 | convolution fusion | flops 1391689728 | bytes 15859712 | tf_op jit(solution)/shard_map/dot_general | solution.py:108
  257.7 14.0 %multiply_convert_fusion.1 = (bf16[2496,512]{1,0:T(8,128)(2,1)}, f32[2496,512]{1,0:T(8,128)}, f32[2496,512]{1,0:T(8,128)}) fusion(bf16[2496,512]{1,0:T(8,128)(2,1)S(1)} %bitcast.163, bf16[512,2048]{1,0:T(8,128)(2,1)S(1)} %bitcast.174), kind=kOutput, calls=%fused_computation.31 | convolution fusion | flops 1391689728 | bytes 15859712 | tf_op jit(solution)/shard_map/dot_general | solution.py:108
  286.5 77.5 %psum.15 = f32[]{:T(128)} all-reduce(f32[]{:T(128)} %convert_reduce_fusion.1), channel_id=1, replica_groups=mesh['dp'=4,'expert'=8] {'dp','expert'}, use_global_device_ids=true, to_apply=%region_14.15 | all-reduce | flops 1 | bytes 8 | tf_op jit(solution)/shard_map/psum | solution.py:168
  364.0 41.6 %all-gather = bf16[32,16,8]{1,2,0:T(8,128)(2,1)S(1)} all-gather(bf16[1,16,8]{1,2,0:T(8,128)(2,1)S(1)} %bitcast.194), channel_id=1, replica_groups=mesh['dp'=4,'expert'=8] {'dp','expert'}, dimensions={0}, use_global_device_ids=true | all-gather | bytes 8448 | tf_op jit(solution)/shard_map/all_gather | solution.py:158
  411.7 6.2 multiply_reduce_fusion.5
  434.1 58.0 %all-to-all-done.2 = bf16[8,312,512]{2,1,0:T(8,128)(2,1)} async-done(((bf16[8,312,512]{2,1,0:T(8,128)(2,1)}), bf16[8,312,512]{2,1,0:T(8,128)(2,1)}, u32[]{:S(2)}, u32[]{:S(2)}) %all-to-all-start.2) | async-done | bytes 2555936 | tf_op jit(solution)/shard_map/all_to_all | solution.py:237
  492.1 8.0 add_convert_fusion.2
  505.5 7.0 add_convert_fusion.3
  537.7 11.3 %copy.64 = bf16[1,512,2048]{2,0,1:T(2,128)(2,1)} copy(bf16[1,512,2048]{1,2,0:T(8,128)(2,1)} %pad_maximum_fusion.1) | data formatting | bytes 4194304
  553.8 9.6 %add_convert_fusion = bf16[2496,512]{1,0:T(8,128)(2,1)} fusion(f32[2496,512]{1,0:T(8,128)} %fusion.109, f32[2496,512]{1,0:T(8,128)} %fusion.117, f32[2496,512]{1,0:T(8,128)} %fusion.113, bf16[2496,512]{1,0:T(8,128)(2,1)} %copy-done.24, bf16[512,2048]{1,0:T(8,128)(2,1)} %bitcast.171), kind=kOutput, calls=%fused_computation.24 | convolution fusion | flops 1313734656 | bytes 20971520 | tf_op jit(solution)/shard_map/dot_general | solution.py:41
  584.1 42.6 %all-to-all-done.3 = bf16[8,312,512]{2,1,0:T(8,128)(2,1)} async-done(((bf16[8,312,512]{2,1,0:T(8,128)(2,1)}), bf16[8,312,512]{2,1,0:T(8,128)(2,1)}, u32[]{:S(2)}, u32[]{:S(2)}) %all-to-all-start.3) | async-done | bytes 2555936 | tf_op jit(solution)/shard_map/all_to_all | solution.py:247
  645.2 9.0 %multiply_reduce_fusion = (f32[5,8,197]{2,1,0:T(8,128)S(1)}, f32[5,8,197,197]{2,3,1,0:T(8,128)}) fusion(f32[5,8,197,197]{2,3,1,0:T(8,128)} %copy-done, f32[5,8,197]{2,1,0:T(8,128)S(1)} %log_add_fusion, bf16[5,197,8,64]{1,3,2,0:T(8,128)(2,1)S(1)} %copy.51, bf16[5,197,1,8,64]{1,4,3,0,2:T(8,128)(2,1)} %copy.67), kind=kOutput, calls=%fused_computation.9 | convolution fusion | flops 204903648 | bytes 14499200 | tf_op jit(solution)/shard_map/ilhd,imhd->ihlm/dot_general | solution.py:83
  654.3 7.0 multiply_convert_fusion
  669.3 9.1 %copy.56 = bf16[5,197,3,8,64]{4,3,2,1,0:T(8,128)(2,1)} copy(bf16[5,197,3,8,64]{1,4,3,0,2:T(8,128)(2,1)} %pad_maximum_fusion) | data formatting | bytes 6051840 | tf_op jit(solution)/shard_map/stack | solution.py:101
  678.5 9.0 %convert_element_type.168 = bf16[985,1536]{1,0:T(8,128)(2,1)} reshape(bf16[5,197,3,8,64]{4,3,2,1,0:T(8,128)(2,1)} %copy.56) | data formatting | bytes 6051840 | tf_op jit(solution)/shard_map/convert_element_type | solution.py:102
  711.0 37.2 %all-reduce.4 = (f32[]{:T(128)}, f32[512]{0:T(512)S(1)}, f32[512]{0:T(512)S(1)}) all-reduce(f32[]{:T(128)} %multiply_reduce_fusion.11, f32[512]{0:T(512)S(1)} %get-tuple-element.42, f32[512]{0:T(512)S(1)} %get-tuple-element.40), channel_id=1, replica_groups=mesh['dp'=4,'expert'=8] {'dp','expert'}, use_global_device_ids=true, to_apply=%region_12.13 | all-reduce | flops 1025 | bytes 8200 | tf_op jit(solution)/shard_map/psum | solution.py:214
  753.8 32.8 %reduce-scatter.12.cloned.1.call-done = f32[16,512]{1,0:T(8,128)} async-done(((f32[512,512]{1,0:T(8,128)}), f32[16,512]{1,0:T(8,128)}) %reduce-scatter.12.cloned.1.call-update) | async-done | bytes 32784 | tf_op jit(solution)/shard_map/reduce_scatter | solution.py:291
  786.6 103.4 %reduce-scatter.10.cloned.1.call-done = f32[16,1536]{1,0:T(8,128)} async-done(((f32[512,1536]{1,0:T(8,128)}), f32[16,1536]{1,0:T(8,128)}) %reduce-scatter.10.cloned.1.call-update) | async-done | bytes 98320 | tf_op jit(solution)/shard_map/reduce_scatter | solution.py:290
  (250 shorter events, 207.6 us)
Async XLA Ops:
  8.0 93.9 %all-gather.5.cloned.1.call-start = ((), (), s32[]{:S(2)}) async-start(), calls=%async_computation.9 | async-start | bytes 1622016 | tf_op jit(solution)/shard_map/all_gather | solution.py:155
  52.6 52.8 %copy-start.44 = (f32[512]{0:T(512)}, f32[512]{0:T(512)S(1)}, u32[]{:S(2)}) copy-start(f32[512]{0:T(512)S(1)} %convert_element_type.136) | copy-start | bytes 6148
  52.6 91.3 %copy-start.50 = (f32[512]{0:T(512)}, f32[512]{0:T(512)S(1)}, u32[]{:S(2)}) copy-start(f32[512]{0:T(512)S(1)} %convert_element_type.143) | copy-start | bytes 6148
  54.1 51.3 %copy-start.36 = (f32[985]{0:T(1024)}, f32[985]{0:T(1024)S(1)}, u32[]{:S(2)}) copy-start(f32[985]{0:T(1024)S(1)} %broadcast_multiply_fusion.5) | copy-start | bytes 11824
  55.8 49.6 %copy-start.40 = (f32[985]{0:T(1024)}, f32[985]{0:T(1024)S(1)}, u32[]{:S(2)}) copy-start(f32[985]{0:T(1024)S(1)} %add_rsqrt_fusion.1) | copy-start | bytes 11824
  56.6 88.8 %copy-start.52 = (s32[985,1]{0,1:T(1,128)}, s32[985,1]{0,1:T(1,128)S(1)}, u32[]{:S(2)}) copy-start(s32[985,1]{0,1:T(1,128)S(1)} %get-tuple-element.71) | copy-start | bytes 11824
  56.6 88.8 %copy-start.54 = (s32[985,1]{0,1:T(1,128)}, s32[985,1]{0,1:T(1,128)S(1)}, u32[]{:S(2)}) copy-start(s32[985,1]{0,1:T(1,128)S(1)} %get-tuple-element.72) | copy-start | bytes 11824
  151.0 62.4 %all-to-all-start = ((bf16[8,312,512]{2,1,0:T(8,128)(2,1)}), bf16[8,312,512]{2,1,0:T(8,128)(2,1)S(1)}, u32[]{:S(2)}, u32[]{:S(2)}) async-start(bf16[8,312,512]{2,1,0:T(8,128)(2,1)} %bitcast.168), calls=%async_computation | async-start | bytes 5111808 | tf_op jit(solution)/shard_map/all_to_all | solution.py:193
  154.6 37.9 %all-gather.7.cloned.1.call-start = ((), (), s32[]{:S(2)}) async-start(), calls=%async_computation.10 | async-start | bytes 2621440 | tf_op jit(solution)/shard_map/all_gather | solution.py:162
  155.2 116.6 %all-gather.9.cloned.1.call-start = ((), (), s32[]{:S(2)}) async-start(), calls=%async_computation.11 | async-start | bytes 2621440 | tf_op jit(solution)/shard_map/all_gather | solution.py:163
  214.9 15.7 %copy-start.30 = (bf16[1,512,2048]{2,1,0:T(8,128)(2,1)S(1)}, bf16[1,512,2048]{2,1,0:T(8,128)(2,1)}, u32[]{:S(2)}) copy-start(bf16[1,512,2048]{2,1,0:T(8,128)(2,1)} %all-gather.7.cloned.1.call-done) | copy-start | bytes 6291460
  230.6 41.2 %copy-start.17 = (bf16[2496,512]{1,0:T(8,128)(2,1)}, bf16[2496,512]{1,0:T(8,128)(2,1)S(1)}, u32[]{:S(2)}) copy-start(bf16[2496,512]{1,0:T(8,128)(2,1)S(1)} %get-tuple-element.64) | copy-start | bytes 7667716
  281.3 82.7 %copy-start.56 = (bf16[16,8]{0,1:T(8,128)(2,1)S(1)}, bf16[16,8]{0,1:T(8,128)(2,1)}, u32[]{:S(2)}) copy-start(bf16[16,8]{0,1:T(8,128)(2,1)} %param.21) | copy-start | bytes 772
  281.3 125.1 %copy-start.49 = (s32[985,2]{0,1:T(2,128)S(1)}, s32[985,2]{0,1:T(2,128)}, u32[]{:S(2)}) copy-start(s32[985,2]{0,1:T(2,128)} %param.15) | copy-start | bytes 23644
  281.3 125.2 %copy-start.12 = (bf16[985,512]{1,0:T(8,128)(2,1)S(1)}, bf16[985,512]{1,0:T(8,128)(2,1)}, u32[]{:S(2)}) copy-start(bf16[985,512]{1,0:T(8,128)(2,1)} %copy-done.11) | copy-start | bytes 3025924
  281.3 125.7 %copy-start.55 = (s32[985,1]{0,1:T(1,128)S(1)}, s32[985,1]{0,1:T(1,128)}, u32[]{:S(2)}) copy-start(s32[985,1]{0,1:T(1,128)} %copy-done.54) | copy-start | bytes 11824
  281.3 125.6 %all-to-all-start.1 = ((bf16[8,312,512]{2,1,0:T(8,128)(2,1)}), bf16[8,312,512]{2,1,0:T(8,128)(2,1)}, u32[]{:S(2)}, u32[]{:S(2)}) async-start(bf16[8,312,512]{2,1,0:T(8,128)(2,1)} %bitcast.15), calls=%async_computation.1 | async-start | bytes 5111808 | tf_op jit(solution)/shard_map/all_to_all | solution.py:202
  427.6 64.5 %all-to-all-start.2 = ((bf16[8,312,512]{2,1,0:T(8,128)(2,1)}), bf16[8,312,512]{2,1,0:T(8,128)(2,1)}, u32[]{:S(2)}, u32[]{:S(2)}) async-start(bf16[8,312,512]{2,1,0:T(8,128)(2,1)} %bitcast.169), calls=%async_computation.2 | async-start | bytes 5111808 | tf_op jit(solution)/shard_map/all_to_all | solution.py:237
  432.0 261.6 %reduce-scatter.16.cloned.1.call-start = ((), (), s32[]{:S(2)}) async-start(), calls=%async_computation.15 | async-start | bytes 270336
  434.0 260.9 %reduce-scatter.18.cloned.1.call-start = ((), (), s32[]{:S(2)}) async-start(), calls=%async_computation.16 | async-start | bytes 2621440
  563.4 63.3 %all-to-all-start.3 = ((bf16[8,312,512]{2,1,0:T(8,128)(2,1)}), bf16[8,312,512]{2,1,0:T(8,128)(2,1)}, u32[]{:S(2)}, u32[]{:S(2)}) async-start(bf16[8,312,512]{2,1,0:T(8,128)(2,1)} %bitcast.158), calls=%async_computation.3 | async-start | bytes 5111808 | tf_op jit(solution)/shard_map/all_to_all | solution.py:247
  567.8 135.5 %reduce-scatter.14.cloned.1.call-start = ((), (), s32[]{:S(2)}) async-start(), calls=%async_computation.14 | async-start | bytes 2621440 | tf_op jit(solution)/shard_map/reduce_scatter | solution.py:299
  584.0 202.6 %reduce-scatter.12.cloned.1.call-start = ((), (), s32[]{:S(2)}) async-start(), calls=%async_computation.13 | async-start | bytes 1081344 | tf_op jit(solution)/shard_map/reduce_scatter | solution.py:291
  654.3 235.8 %reduce-scatter.10.cloned.1.call-start = ((), (), s32[]{:S(2)}) async-start(), calls=%async_computation.12 | async-start | bytes 3244032 | tf_op jit(solution)/shard_map/reduce_scatter | solution.py:290
  (54 other events, 286.4 us)
Sparse Core Ops, SparseCore 0:
  11.9 57.9 all-gather.4
  435.7 134.5 reduce-scatter.15
  573.5 31.5 reduce-scatter.17
  607.9 35.1 reduce-scatter.13
  654.4 132.2 reduce-scatter.11
  792.5 97.5 reduce-scatter.9
Sparse Core Ops, SparseCore 1:
  156.9 35.5 all-gather.6
  194.2 35.1 all-gather.8
where the time goes:
time: 907 us; the launch traced here: 899 us
  waiting for transfers between devices  296 us (33%)
  blocking collectives  244 us (27%)
  matrix products  204 us (22%)
  local copies, waits for them, and re-layouts  91 us (10%)
  other arithmetic  26.5 us (3%)
  between operations  20.1 us (2%)
  starting transfers between devices  17.3 us (2%)
    reduce_scatter x1, waiting for transfers between devices, shards(): lax.psum_scatter(qkv_weight_grad, ('dp', 'expert'), scatter_dimension=0,...  103 us
    psum x1, blocking collectives, shards(): valid_count = lax.psum(jnp.sum(valid_f), ('dp', 'expert'))  77.5 us
    all_to_all x1, waiting for transfers between devices, shards(): lax.all_to_all(slot_grads.reshape(experts, capacity, model_width), 'exper...  58 us
    dot_general x4, matrix products, expert_forward(): jnp.dot(rows_in, weight_in[:, offset:offset + block_size], preferred_elem...  56.8 us
    dot_general x10, matrix products, contract_cols(): lax.dot_general(left_side, right_side, (((1,), (1,)), ((), ())), preferre...  52.1 us
    unnamed x148, local copies, waits for them, and re-layouts  49 us
    all_gather x1, blocking collectives, shards(): lax.all_gather(out_weight, ('dp', 'expert'), axis=0, tiled=True)  45.3 us
    dot_general x13, matrix products, contract_rows(): lax.dot_general(left_side, right_side, (((0,), (0,)), ((), ())), preferre...  44.6 us
  transfers between devices with their start and end apart: 12, of which 6 were waited for; matrix products, arithmetic and copies ran while one was open for 26% of the time, Pallas kernels for 0%

commit v1 on v0

--- a/solution.py
+++ b/solution.py
@@ -1,6 +1,8 @@
 import jax
 import jax.numpy as jnp
 from jax import lax
+from jax.experimental import pallas as pl
+from jax.experimental.pallas import tpu as pltpu
 from jax.sharding import PartitionSpec as P
 
 HEADS = 8
@@ -316,6 +318,580 @@
     )
 
 
+F32 = jnp.float32
+BF16 = jnp.bfloat16
+MB = 2**20
+
+
+def round_up(value, unit):
+    return (value + unit - 1) // unit * unit
+
+
+def dot(left_side, right_side):
+    return jnp.dot(left_side, right_side, preferred_element_type=F32)
+
+
+def lane_ids(shape):
+    return lax.broadcasted_iota(jnp.int32, shape, len(shape) - 1)
+
+
+def row_ids(shape):
+    return lax.broadcasted_iota(jnp.int32, shape, len(shape) - 2)
+
+
+def normalize(values):
+    centered = values - jnp.mean(values, axis=-1, keepdims=True)
+    inverse = lax.rsqrt(jnp.mean(centered * centered, axis=-1, keepdims=True) + EPS)
+    return centered * inverse, inverse
+
+
+def gelu_pair(values):
+    size = jnp.abs(values)
+    inv = 1.0 / (1.0 + 0.2316419 * size)
+    density = 0.3989422804014327 * jnp.exp(-0.5 * values * values)
+    series = inv * (
+        0.319381530
+        + inv * (-0.356563782 + inv * (1.781477937 + inv * (-1.821255978 + inv * 1.330274429)))
+    )
+    tail = density * series
+    cumulative = jnp.where(values >= 0, 1.0 - tail, tail)
+    return values * cumulative, cumulative + values * density
+
+
+def forward_kernel(
+    real_rows,
+    experts,
+    tok_ref,
+    wqkv_ref,
+    wout_ref,
+    gain_ref,
+    router_ref,
+    router_t_ref,
+    cols_ref,
+    rows_ref,
+    qkv_ref,
+    probs_ref,
+    mixed_ref,
+    resid_ref,
+    act_ref,
+    gates_ref,
+    grow_ref,
+):
+    inputs = tok_ref[...].astype(F32)
+    normed, _ = normalize(inputs)
+    act_one = (normed * gain_ref[0:1, :]).astype(BF16)
+    qkv = dot(act_one, wqkv_ref[...]).astype(BF16)
+    qkv_ref[...] = qkv
+    width = inputs.shape[1]
+    rows = inputs.shape[0]
+    low_half = lane_ids((1, 128)) < 64
+    key_bias = jnp.where(lane_ids((1, rows)) < real_rows, 0.0, -1e30)
+    parts = []
+    for pair in range(width // 128):
+        lanes = slice(128 * pair, 128 * (pair + 1))
+        queries = qkv[:, lanes]
+        key_rows = qkv[:, width + 128 * pair : width + 128 * (pair + 1)]
+        values = qkv[:, 2 * width + 128 * pair : 2 * width + 128 * (pair + 1)]
+        outs = []
+        for side in range(2):
+            mask = low_half if side == 0 else jnp.logical_not(low_half)
+            masked = jnp.where(mask, queries, jnp.zeros_like(queries))
+            scores = contract_cols(masked, key_rows) * 0.125 + key_bias
+            exped = jnp.exp(scores - jnp.max(scores, axis=-1, keepdims=True))
+            probs = (exped * (1.0 / jnp.sum(exped, axis=-1, keepdims=True))).astype(BF16)
+            probs_ref[2 * pair + side] = probs
+            outs.append(dot(probs, values))
+        parts.append(jnp.where(low_half, outs[0], outs[1]).astype(BF16))
+    mixed = jnp.concatenate(parts, axis=1)
+    mixed_ref[...] = mixed
+    resid = inputs + dot(mixed, wout_ref[...])
+    resid_ref[...] = resid
+    normed_two, _ = normalize(resid)
+    act_two = (normed_two * gain_ref[1:2, :]).astype(BF16)
+    act_ref[...] = act_two
+    lanes = lane_ids((1, 128))
+    logits = jnp.where(lanes < experts, dot(act_two, router_ref[...]), -1e30)
+    exped = jnp.exp(logits - jnp.max(logits, axis=-1, keepdims=True))
+    gates = exped / jnp.sum(exped, axis=-1, keepdims=True)
+    cols = cols_ref[...]
+    first = jnp.sum(jnp.where(lanes == cols[:, 2:3], gates, 0.0), axis=-1, keepdims=True)
+    second = jnp.sum(jnp.where(lanes == cols[:, 3:4], gates, 0.0), axis=-1, keepdims=True)
+    gates_ref[...] = jnp.where(lanes == experts, first, jnp.where(lanes == experts + 1, second, gates))
+    logits_t = contract_cols(router_t_ref[...], act_two)[:experts]
+    exped_t = jnp.exp(logits_t - jnp.max(logits_t, axis=0, keepdims=True))
+    gates_t = exped_t / jnp.sum(exped_t, axis=0, keepdims=True)
+    ids_t = row_ids(gates_t.shape)
+    first_t = jnp.sum(jnp.where(ids_t == rows_ref[2:3, :], gates_t, 0.0), axis=0, keepdims=True)
+    second_t = jnp.sum(jnp.where(ids_t == rows_ref[3:4, :], gates_t, 0.0), axis=0, keepdims=True)
+    grow_ref[...] = jnp.where(row_ids((8, rows)) == 0, first_t, second_t)
+
+
+def hot_rows(codes, start, count):
+    slots = row_ids((count, codes.shape[1])) + start
+    return (slots == codes[0:1, :]) | (slots == codes[1:2, :])
+
+
+def expert_forward_kernel(
+    cap, group, act_ref, codes_ref, win_ref, wout_ref, rows_out_ref, hidden_ref, slope_ref, out_ref
+):
+    which, half = pl.program_id(0), pl.program_id(1)
+    blocks, images = act_ref.shape[0], act_ref.shape[1]
+    hidden_width = win_ref.shape[1]
+    pieces = []
+    for block in range(blocks):
+        start = (which * group + half * blocks + block) * cap
+        total = None
+        for image in range(images):
+            hot = jnp.where(hot_rows(codes_ref[block, image], start, cap), 1.0, 0.0).astype(BF16)
+            term = dot(hot, act_ref[block, image])
+            total = term if total is None else total + term
+        pieces.append(total.astype(BF16))
+    rows_in = jnp.concatenate(pieces, axis=0)
+    rows_out_ref[...] = rows_in.reshape(rows_out_ref.shape)
+    step = 512
+    result = None
+    for offset in range(0, hidden_width, step):
+        act, slope = gelu_pair(dot(rows_in, win_ref[:, offset : offset + step]))
+        act = act.astype(BF16)
+        hidden_ref[:, :, offset : offset + step] = act.reshape(blocks, cap, step)
+        slope_ref[:, :, offset : offset + step] = slope.astype(BF16).reshape(blocks, cap, step)
+        term = dot(act, wout_ref[offset : offset + step, :])
+        result = term if result is None else result + term
+    out_ref[...] = result.astype(BF16).reshape(out_ref.shape)
+
+
+def hot_cols(codes, count):
+    return lane_ids((codes.shape[0], count)) == codes
+
+
+def combine_kernel(
+    experts, scale_ref, resid_ref, back_ref, cols_ref, gates_ref, target_ref, valid_ref,
+    out_ref, dout_ref, dlow_ref, dlogit_ref, loss_ref,
+):
+    count = back_ref.shape[0]
+    cols = cols_ref[...]
+    rows = cols.shape[0]
+    hot = jnp.concatenate(
+        [
+            jnp.where(hot_cols(cols[:, 0:1], count), 1.0, 0.0).astype(BF16),
+            jnp.where(hot_cols(cols[:, 1:2], count), 1.0, 0.0).astype(BF16),
+        ],
+        axis=0,
+    )
+    both = dot(hot, back_ref[...])
+    from_first, from_second = both[:rows], both[rows:]
+    gates = gates_ref[...]
+    first, second = gates[:, experts : experts + 1], gates[:, experts + 1 : experts + 2]
+    output = resid_ref[...] + first * from_first + second * from_second
+    out_ref[...] = output.astype(BF16)
+    residue = output - target_ref[...].astype(F32)
+    valid = valid_ref[...]
+    square = jnp.mean(residue * residue, axis=-1, keepdims=True) * valid[:, 0:1]
+
+    @pl.when(pl.program_id(0) == 0)
+    def _():
+        loss_ref[...] = jnp.zeros_like(loss_ref)
+
+    loss_ref[...] += jnp.sum(square)
+    dout = (scale_ref[0, 0] * valid[:, 0:1]) * residue
+    dout_ref[...] = dout
+    dlow_ref[...] = dout.astype(BF16)
+    lanes = lane_ids((1, 128))
+    grad = jnp.where(
+        lanes == cols[:, 2:3], jnp.sum(dout * from_first, axis=-1, keepdims=True), 0.0
+    ) + jnp.where(lanes == cols[:, 3:4], jnp.sum(dout * from_second, axis=-1, keepdims=True), 0.0)
+    real = jnp.where(lanes < experts, gates, 0.0)
+    dlogit_ref[...] = real * (grad - jnp.sum(real * grad, axis=-1, keepdims=True))
+
+
+def expert_back_kernel(
+    cap, group, dlow_ref, codes_ref, grow_ref, rows_ref, hidden_ref, slope_ref, win_ref, wout_ref,
+    back_ref, gin_ref, gout_ref, acc_in, acc_out,
+):
+    which, half = pl.program_id(0), pl.program_id(1)
+    blocks, images = dlow_ref.shape[0], dlow_ref.shape[1]
+    hidden_width = win_ref.shape[1]
+    pieces = []
+    for block in range(blocks):
+        start = (which * group + half * blocks + block) * cap
+        total = None
+        slot_gate = None
+        for image in range(images):
+            codes = codes_ref[block, image]
+            slots = row_ids((cap, codes.shape[1])) + start
+            is_first = slots == codes[0:1, :]
+            is_second = slots == codes[1:2, :]
+            hot = jnp.where(is_first | is_second, 1.0, 0.0).astype(BF16)
+            term = dot(hot, dlow_ref[block, image])
+            gain = grow_ref[block, image]
+            picked = jnp.where(is_first, gain[0:1, :], jnp.where(is_second, gain[1:2, :], 0.0))
+            picked = jnp.sum(picked, axis=-1, keepdims=True)
+            total = term if total is None else total + term
+            slot_gate = picked if slot_gate is None else slot_gate + picked
+        pieces.append((total * slot_gate).astype(BF16))
+    grads = jnp.concatenate(pieces, axis=0)
+    grads_t = grads.T
+    rows_in_t = rows_ref[...].reshape(blocks * cap, -1).T
+    step = 512
+    result = None
+    for offset in range(0, hidden_width, step):
+        cut = slice(offset, offset + step)
+        hidden = hidden_ref[:, :, cut].reshape(blocks * cap, step)
+        slope = slope_ref[:, :, cut].reshape(blocks * cap, step).astype(F32)
+        dpre = (contract_cols(grads, wout_ref[cut, :]) * slope).astype(BF16)
+        gin = dot(rows_in_t, dpre)
+        gout = dot(grads_t, hidden)
+        term = contract_cols(dpre, win_ref[:, cut])
+        result = term if result is None else result + term
+
+        @pl.when(half == 0)
+        def _():
+            acc_in[:, cut] = gin
+            acc_out[:, cut] = gout
+
+        @pl.when(half == 1)
+        def _():
+            gin_ref[:, cut] = (acc_in[:, cut] + gin).astype(BF16)
+            gout_ref[:, cut] = (acc_out[:, cut] + gout).astype(BF16)
+
+    back_ref[...] = result.astype(BF16).reshape(back_ref.shape)
+
+
+def back_kernel(
+    tok_ref, wqkv_ref, wout_ref, gain_ref, router_t_ref, cols_ref, back_ref, dlogit_ref, resid_ref,
+    dout_ref, qkv_ref, probs_ref, mixed_ref,
+    tgrad_ref, gqkv_ref, gout_ref, gmisc_ref,
+):
+    count = back_ref.shape[0]
+    cols = cols_ref[...]
+    hot = jnp.where(hot_cols(cols[:, 0:1], count) | hot_cols(cols[:, 1:2], count), 1.0, 0.0)
+    dlogits = dlogit_ref[...]
+    dact = dot(hot.astype(BF16), back_ref[...])
+    dlogits_high = dlogits.astype(BF16)
+    dlogits_low = (dlogits - dlogits_high.astype(F32)).astype(BF16)
+    dact = dact + dot(dlogits_high, router_t_ref[...]) + dot(dlogits_low, router_t_ref[...])
+
+    resid = resid_ref[...]
+    normed_two, inverse_two = normalize(resid)
+    gain_two = gain_ref[1:2, :]
+    act_two = (normed_two * gain_two).astype(BF16)
+    grouter = contract_rows(dlogits_high, act_two) + contract_rows(dlogits_low, act_two)
+
+    def norm_back(grad, normed, inverse, gain):
+        scaled = grad * gain
+        gain_grad = jnp.sum(grad * normed, axis=0, keepdims=True)
+        inner = (
+            scaled
+            - jnp.mean(scaled, axis=-1, keepdims=True)
+            - normed * jnp.mean(scaled * normed, axis=-1, keepdims=True)
+        )
+        return inverse * inner, gain_grad
+
+    grad_two, ggain_two = norm_back(dact, normed_two, inverse_two, gain_two)
+    dresid = dout_ref[...] + grad_two
+    branch = dresid.astype(BF16)
+    mixed = mixed_ref[...]
+    gout = contract_rows(mixed, branch)
+    dmixed = contract_cols(branch, wout_ref[...]).astype(BF16)
+    qkv = qkv_ref[...]
+    width = dmixed.shape[1]
+    low_half = lane_ids((1, 128)) < 64
+    dqs, dks, dvs = [], [], []
+    for pair in range(width // 128):
+        cut = slice(128 * pair, 128 * (pair + 1))
+        queries = qkv[:, cut]
+        key_rows = qkv[:, width + 128 * pair : width + 128 * (pair + 1)]
+        values = qkv[:, 2 * width + 128 * pair : 2 * width + 128 * (pair + 1)]
+        dmix = dmixed[:, cut]
+        dq = []
+        dk = dv = None
+        for side in range(2):
+            mask = low_half if side == 0 else jnp.logical_not(low_half)
+            dmask = jnp.where(mask, dmix, jnp.zeros_like(dmix))
+            qmask = jnp.where(mask, queries, jnp.zeros_like(queries))
+            probs_low = probs_ref[2 * pair + side]
+            probs = probs_low.astype(F32)
+            dprobs = contract_cols(dmask, values)
+            dscore = probs * (dprobs - jnp.sum(probs * dprobs, axis=-1, keepdims=True))
+            dscore = dscore.astype(BF16)
+            dq.append(dot(dscore, key_rows))
+            dk_term = contract_rows(dscore, qmask)
+            dv_term = contract_rows(probs_low, dmask)
+            dk = dk_term if dk is None else dk + dk_term
+            dv = dv_term if dv is None else dv + dv_term
+        dqs.append((jnp.where(low_half, dq[0], dq[1]) * 0.125).astype(BF16))
+        dks.append((dk * 0.125).astype(BF16))
+        dvs.append(dv.astype(BF16))
+    dqkv = jnp.concatenate(dqs + dks + dvs, axis=1)
+    inputs = tok_ref[...].astype(F32)
+    normed_one, inverse_one = normalize(inputs)
+    gain_one = gain_ref[0:1, :]
+    act_one = (normed_one * gain_one).astype(BF16)
+    gqkv = contract_rows(act_one, dqkv)
+    dact_one = contract_cols(dqkv, wqkv_ref[...])
+    grad_one, ggain_one = norm_back(dact_one, normed_one, inverse_one, gain_one)
+    tgrad_ref[...] = dresid + grad_one
+    gmisc = jnp.concatenate(
+        [
+            grouter[:8],
+            jnp.where(row_ids((8, width)) == 0, ggain_one, jnp.where(row_ids((8, width)) == 1, ggain_two, 0.0)),
+        ],
+        axis=0,
+    )
+
+    @pl.when(pl.program_id(0) == 0)
+    def _():
+        gqkv_ref[...] = gqkv
+        gout_ref[...] = gout
+        gmisc_ref[...] = gmisc
+
+    @pl.when(pl.program_id(0) > 0)
+    def _():
+        gqkv_ref[...] += gqkv
+        gout_ref[...] += gout
+        gmisc_ref[...] += gmisc
+
+
+def shape(dims, kind):
+    return jax.ShapeDtypeStruct(dims, kind)
+
+
+def whole(dims):
+    return pl.BlockSpec(dims, lambda *_: (0,) * len(dims))
+
+
+def per_image(*dims):
+    return pl.BlockSpec((None,) + dims, lambda i: (i,) + (0,) * len(dims))
+
+
+def params():
+    return pltpu.CompilerParams(vmem_limit_bytes=56 * MB)
+
+
+def fast_shards(
+    tokens, targets, valid_mask, routes, slot_ids, ln1_gain, qkv_weight, out_weight, ln2_gain,
+    router_weight, expert_in, expert_out,
+):
+    axes = ("dp", "expert")
+    tok_rows, width = tokens.shape
+    experts = lax.axis_size("expert")
+    group = experts // 2
+    dp = lax.axis_size("dp")
+    total_tokens = tok_rows * dp * experts
+    hidden_width = expert_in.shape[2]
+    capacity = (5 * tok_rows // 2 // experts + 7) // 8 * 8
+    cap = round_up(capacity, 16)
+    images = IMG_DEV
+    real_rows = tok_rows // images
+    rows = round_up(real_rows, 16)
+    me = lax.axis_index("expert")
+
+    def pad_rows(array, value=0):
+        array = array.reshape(images, real_rows, -1)
+        return jnp.pad(array, ((0, 0), (0, rows - real_rows), (0, 0)), constant_values=value)
+
+    valid_f = valid_mask.astype(F32)
+    my_count = jnp.sum(valid_f)
+    count_high = jnp.floor(my_count / 128.0)
+    count_low = my_count - 128.0 * count_high
+    shard = qkv_weight.shape[0]
+    extra = jnp.concatenate(
+        [
+            router_weight,
+            ln1_gain[:, None],
+            ln2_gain[:, None],
+            jnp.broadcast_to(count_high.astype(BF16), (shard, 1)),
+            jnp.broadcast_to(count_low.astype(BF16), (shard, 1)),
+            jnp.zeros((shard, 128 - experts - 4), BF16),
+        ],
+        axis=1,
+    )
+    dense = lax.all_gather(
+        jnp.concatenate([qkv_weight, out_weight, extra], axis=1), axes, axis=0, tiled=True
+    )
+    qkv_full = dense[:, : 3 * width]
+    out_full = dense[:, 3 * width : 4 * width]
+    extra_full = dense[:, 4 * width :]
+    router_full = jnp.where(lane_ids((1, 128)) < experts, extra_full, 0)
+    extra_t = extra_full.T
+    router_t = jnp.where(row_ids((128, 1)) < experts, extra_t, 0)
+    gains = extra_t[experts : experts + 2].astype(F32)
+    counts = extra_full[::shard].astype(F32)
+    valid_count = jnp.sum(counts[:, experts + 2] * 128.0 + counts[:, experts + 3])
+    scale = (total_tokens / valid_count).reshape(1, 1)
+
+    far = [(i, i ^ group) for i in range(experts)]
+    w_in = [expert_in[0]]
+    w_out = [expert_out[0]]
+    w_in.append(lax.ppermute(w_in[0], "expert", far))
+    w_out.append(lax.ppermute(w_out[0], "expert", far))
+    win_full = jnp.stack([lax.all_gather(w, "dp", axis=0, tiled=True) for w in w_in])
+    wout_full = jnp.stack([lax.all_gather(w, "dp", axis=0, tiled=True) for w in w_out])
+
+    def exchange(blocks):
+        out = [blocks[0]]
+        for k in range(1, group):
+            out.append(lax.ppermute(blocks[k], "expert", [(i, i ^ k) for i in range(experts)]))
+        return out
+
+    code = jnp.where(slot_ids < capacity, (routes ^ me) * cap + slot_ids, -1)
+    cols = pad_rows(jnp.concatenate([code, routes], axis=1), -1)
+    row_codes = jnp.pad(cols.transpose(0, 2, 1), ((0, 0), (0, 4), (0, 0)))
+    cols = jnp.pad(cols, ((0, 0), (0, 0), (0, 4)))
+    tok_p = pad_rows(tokens)
+    target_p = pad_rows(targets)
+    valid_p = pad_rows(jnp.broadcast_to(valid_f[:, None], (tok_rows, 8)))
+
+    gate_lanes = 128
+    qkv_p, probs, mixed, resid, act_two, gates, grow = pl.pallas_call(
+        lambda *refs: forward_kernel(real_rows, experts, *refs),
+        grid=(images,),
+        in_specs=[
+            per_image(rows, width), whole((width, 3 * width)), whole((width, width)), whole((2, width)),
+            whole((width, 128)), whole((128, width)), per_image(rows, 8), per_image(8, rows),
+        ],
+        out_specs=[
+            per_image(rows, 3 * width), per_image(HEADS, rows, rows), per_image(rows, width),
+            per_image(rows, width), per_image(rows, width), per_image(rows, gate_lanes), per_image(8, rows),
+        ],
+        out_shape=[
+            shape((images, rows, 3 * width), BF16), shape((images, HEADS, rows, rows), BF16),
+            shape((images, rows, width), BF16), shape((images, rows, width), F32),
+            shape((images, rows, width), BF16), shape((images, rows, gate_lanes), F32),
+            shape((images, 8, rows), F32),
+        ],
+        compiler_params=params(),
+        cost_estimate=pl.CostEstimate(flops=int(5e9), bytes_accessed=int(2e7), transcendentals=0),
+        name="attention_forward",
+    )(tok_p, qkv_full, out_full, gains, router_full, router_t, cols, row_codes)
+
+    act_all = jnp.stack(exchange([act_two] * group))
+    code_all = jnp.stack(exchange([row_codes] * group))
+
+    half_blocks = group // 2
+    def by_half(*dims):
+        return pl.BlockSpec((half_blocks,) + dims, lambda q, h: (h,) + (0,) * len(dims))
+    def by_expert(*dims):
+        return pl.BlockSpec((None,) + dims, lambda q, h: (q,) + (0,) * len(dims))
+    def by_both(*dims):
+        return pl.BlockSpec((None, half_blocks) + dims, lambda q, h: (q, h) + (0,) * len(dims))
+
+    rows_in, hidden, slope, produced = pl.pallas_call(
+        lambda *refs: expert_forward_kernel(cap, group, *refs),
+        grid=(2, 2),
+        in_specs=[
+            by_half(images, rows, width), by_half(images, 8, rows), by_expert(width, hidden_width),
+            by_expert(hidden_width, width),
+        ],
+        out_specs=[by_both(cap, width), by_both(cap, hidden_width), by_both(cap, hidden_width), by_both(cap, width)],
+        out_shape=[
+            shape((2, group, cap, width), BF16), shape((2, group, cap, hidden_width), BF16),
+            shape((2, group, cap, hidden_width), BF16), shape((2, group, cap, width), BF16),
+        ],
+        compiler_params=params(),
+        cost_estimate=pl.CostEstimate(flops=int(14e9), bytes_accessed=int(4e7), transcendentals=0),
+        name="expert_forward",
+    )(act_all, code_all, win_full, wout_full)
+
+    def give_back(array):
+        came = exchange([array[:, k] for k in range(group)])
+        return jnp.stack(came, axis=1).reshape(2 * group * cap, width)
+
+    returned = give_back(produced)
+    block_out, dout, dlow, dlogits, loss_part = pl.pallas_call(
+        lambda *refs: combine_kernel(experts, *refs),
+        grid=(images,),
+        in_specs=[
+            pl.BlockSpec(memory_space=pltpu.SMEM), per_image(rows, width), whole((2 * group * cap, width)),
+            per_image(rows, 8), per_image(rows, gate_lanes), per_image(rows, width), per_image(rows, 8),
+        ],
+        out_specs=[
+            per_image(rows, width), per_image(rows, width), per_image(rows, width), per_image(rows, gate_lanes),
+            whole((8, 128)),
+        ],
+        out_shape=[
+            shape((images, rows, width), BF16), shape((images, rows, width), F32),
+            shape((images, rows, width), BF16), shape((images, rows, gate_lanes), F32), shape((8, 128), F32),
+        ],
+        compiler_params=params(),
+        cost_estimate=pl.CostEstimate(flops=int(5e9), bytes_accessed=int(1e7), transcendentals=0),
+        name="combine_and_loss",
+    )(scale, resid, returned, cols, gates, target_p, valid_p)
+
+    dlow_all = jnp.stack(exchange([dlow] * group))
+    grow_all = jnp.stack(exchange([grow] * group))
+    drows, gin, gout_t = pl.pallas_call(
+        lambda *refs: expert_back_kernel(cap, group, *refs),
+        grid=(2, 2),
+        in_specs=[
+            by_half(images, rows, width), by_half(images, 8, rows), by_half(images, 8, rows),
+            by_both(cap, width), by_both(cap, hidden_width), by_both(cap, hidden_width),
+            by_expert(width, hidden_width), by_expert(hidden_width, width),
+        ],
+        out_specs=[by_both(cap, width), by_expert(width, hidden_width), by_expert(width, hidden_width)],
+        out_shape=[
+            shape((2, group, cap, width), BF16), shape((2, width, hidden_width), BF16),
+            shape((2, width, hidden_width), BF16),
+        ],
+        scratch_shapes=[pltpu.VMEM((width, hidden_width), F32), pltpu.VMEM((width, hidden_width), F32)],
+        compiler_params=params(),
+        cost_estimate=pl.CostEstimate(flops=int(24e9), bytes_accessed=int(4e7), transcendentals=0),
+        name="expert_backward",
+    )(dlow_all, code_all, grow_all, rows_in, hidden, slope, win_full, wout_full)
+    grad_back = give_back(drows)
+
+    tgrad, gqkv, gout_w, gmisc = pl.pallas_call(
+        back_kernel,
+        grid=(images,),
+        in_specs=[
+            per_image(rows, width), whole((width, 3 * width)), whole((width, width)), whole((2, width)),
+            whole((128, width)), per_image(rows, 8), whole((2 * group * cap, width)),
+            per_image(rows, gate_lanes), per_image(rows, width), per_image(rows, width),
+            per_image(rows, 3 * width), per_image(HEADS, rows, rows), per_image(rows, width),
+        ],
+        out_specs=[per_image(rows, width), whole((width, 3 * width)), whole((width, width)), whole((16, width))],
+        out_shape=[
+            shape((images, rows, width), F32), shape((width, 3 * width), F32), shape((width, width), F32),
+            shape((16, width), F32),
+        ],
+        compiler_params=params(),
+        cost_estimate=pl.CostEstimate(flops=int(10e9), bytes_accessed=int(3e7), transcendentals=0),
+        name="attention_backward",
+    )(tok_p, qkv_full, out_full, gains, router_t, cols, grad_back, dlogits, resid, dout, qkv_p, probs, mixed)
+
+    gin_sums = [lax.psum_scatter(gin[q], "dp", scatter_dimension=0, tiled=True) for q in (1, 0)]
+    gout_sums = [lax.psum_scatter(gout_t[q], "dp", scatter_dimension=1, tiled=True) for q in (1, 0)]
+    gin_own = gin_sums[1].astype(F32) + lax.ppermute(gin_sums[0], "expert", far).astype(F32)
+    gout_own = (gout_sums[1].astype(F32) + lax.ppermute(gout_sums[0], "expert", far).astype(F32)).T
+
+    dense_grad = jnp.concatenate(
+        [
+            gqkv, gout_w, gmisc.T,
+            jnp.broadcast_to(loss_part[0:1, 0:1] / 16.0, (width, 1)), jnp.zeros((width, 111), F32),
+        ],
+        axis=1,
+    )
+    mine = lax.psum_scatter(dense_grad, axes, scatter_dimension=0, tiled=True)
+    misc = mine[:, 4 * width :]
+    loss_value = jnp.sum(misc[:, 16]) * (16.0 / shard) / valid_count
+
+    def unpad(array):
+        return array[:, :real_rows].reshape(tok_rows, width)
+
+    return (
+        unpad(block_out),
+        loss_value,
+        unpad(tgrad),
+        misc[:, 8],
+        mine[:, : 3 * width],
+        mine[:, 3 * width : 4 * width],
+        misc[:, 9],
+        misc[:, :experts],
+        gin_own[None],
+        gout_own[None],
+    )
+
+
 def solution(mesh):
     in_specs = (
         P(("dp", "expert"), None),
@@ -343,4 +919,6 @@
         P("expert", "dp", None),
         P("expert", "dp", None),
     )
-    return jax.shard_map(shards, mesh=mesh, in_specs=in_specs, out_specs=out_specs, check_vma=False)
+    halves = mesh.shape["expert"] == 8 and mesh.shape["dp"] == 4
+    body = fast_shards if halves else shards
+    return jax.shard_map(body, mesh=mesh, in_specs=in_specs, out_specs=out_specs, check_vma=False)

time: 907 us -> 749 us (0.83)
  blocking collectives: 244 us -> 0 us
  matrix products: 204 us -> 0 us
  waiting for transfers between devices: 296 us -> 491 us
  Pallas kernels: 0 us -> 134 us
  local copies, waits for them, and re-layouts: 91 us -> 54.8 us
    dot_general x44 -> x0, matrix products: 202 us -> none  [the longest x4 56.8 us: expert_forward(): jnp.dot(rows_in, weight_in[:, offset:offset + block_size], preferred_elem...]
    ppermute x0 -> x22, waiting for transfers between devices: none -> 202 us  [the longest x18 145 us: exchange(): lax.ppermute(blocks[k], 'expert', [(i, i ^ k) for i in range(experts)])]
    pallas_call x0 -> x5, Pallas kernels: none -> 134 us  [the longest x1 42.2 us: fast_shards(): pl.pallas_call(lambda *refs: expert_back_kernel(cap, group, *refs), grid=...]
    all_to_all x4 -> x0, waiting for transfers between devices: 121 us -> none  [the longest x1 58 us: shards(): lax.all_to_all(slot_grads.reshape(experts, capacity, model_width), 'exper...]
    psum x2 -> x0, blocking collectives: 115 us -> none  [the longest x1 77.5 us: shards(): valid_count = lax.psum(jnp.sum(valid_f), ('dp', 'expert'))]
    all_gather x2 -> x0, blocking collectives: 86.9 us -> none  [the longest x1 45.3 us: shards(): lax.all_gather(out_weight, ('dp', 'expert'), axis=0, tiled=True)]
    reduce_scatter x3 -> x5, waiting for transfers between devices: 136 us -> 203 us  [the longest x1 143 us: fast_shards(): mine = lax.psum_scatter(dense_grad, axes, scatter_dimension=0, tiled=True)]
    all_gather x3 -> x5, waiting for transfers between devices: 36.8 us -> 84 us  [the longest x4 69.1 us: fast_shards(): lax.all_gather(w, 'dp', axis=0, tiled=True)]
  transfers between devices with their start and end apart: 12 -> 32, of which waited for: 6 -> 19; matrix products, arithmetic and copies ran while one was open for 26% -> 7% of each run, Pallas kernels for 0% -> 6%
where the time goes in v1:
time: 749 us; the launch traced here: 748 us
  waiting for transfers between devices  491 us (66%)
  Pallas kernels  134 us (18%)
  local copies, waits for them, and re-layouts  54.8 us (7%)
  other arithmetic  27.7 us (4%)
  starting transfers between devices  21 us (3%)
  between operations  19.6 us (3%)
    ppermute x18, waiting for transfers between devices, exchange(): lax.ppermute(blocks[k], 'expert', [(i, i ^ k) for i in range(experts)])  145 us
    reduce_scatter x1, waiting for transfers between devices, fast_shards(): mine = lax.psum_scatter(dense_grad, axes, scatter_dimension=0, tiled=True)  143 us
    all_gather x4, waiting for transfers between devices, fast_shards(): lax.all_gather(w, 'dp', axis=0, tiled=True)  69.1 us
    pallas_call x1, Pallas kernels, fast_shards(): pl.pallas_call(lambda *refs: expert_back_kernel(cap, group, *refs), grid=...  42.2 us
    pallas_call x1, Pallas kernels, fast_shards(): pl.pallas_call(lambda *refs: expert_forward_kernel(cap, group, *refs), gr...  33.5 us
    reduce_scatter x2, waiting for transfers between devices, fast_shards(): lax.psum_scatter(gin[q], 'dp', scatter_dimension=0, tiled=True)  32.5 us
    pallas_call x1, Pallas kernels, fast_shards(): pl.pallas_call(back_kernel, grid=(images,), in_specs=[per_image(rows, wid...  30.6 us
    ppermute x1, waiting for transfers between devices, fast_shards(): w_out.append(lax.ppermute(w_out[0], 'expert', far))  28.5 us
  transfers between devices with their start and end apart: 32, of which 19 were waited for; matrix products, arithmetic and copies ran while one was open for 7% of the time, Pallas kernels for 6%

profile of v1, /device:TPU:0, one launch (start us, length us, event | category | flops | bytes accessed | tf_op | source)
XLA Modules:
  0.0 747.9 jit_solution(10476772941024469062)
XLA Ops:
  18.6 24.9 %collective-permute-done.6 = bf16[128,2048]{1,0:T(8,128)(2,1)S(1)} collective-permute-done((bf16[128,2048]{1,0:T(8,128)(2,1)}, bf16[128,2048]{1,0:T(8,128)(2,1)S(1)}, u32[]{:S(2)}, u32[]{:S(2)}) %collective-permute-start.6) | collective-permute-done | bytes 524320 | tf_op jit(solution)/shard_map/ppermute | solution.py:726
  45.1 28.5 %collective-permute-done.7 = bf16[512,512]{1,0:T(8,128)(2,1)S(1)} collective-permute-done((bf16[512,512]{1,0:T(8,128)(2,1)}, bf16[512,512]{1,0:T(8,128)(2,1)S(1)}, u32[]{:S(2)}, u32[]{:S(2)}) %collective-permute-start.7) | collective-permute-done | bytes 524320 | tf_op jit(solution)/shard_map/ppermute | solution.py:727
  78.0 14.9 %all-gather.8.cloned.1.call-done = bf16[512,2176]{1,0:T(8,128)(2,1)} async-done(((bf16[16,2176]{1,0:T(8,128)(2,1)}), bf16[512,2176]{1,0:T(8,128)(2,1)}) %all-gather.8.cloned.1.call-update) | async-done | bytes 2228240 | tf_op jit(solution)/shard_map/all_gather | solution.py:709
  100.7 15.2 %attention_forward.1 = (bf16[5,208,1536]{2,1,0:T(8,128)(2,1)}, bf16[5,8,208,208]{3,2,1,0:T(8,128)(2,1)}, bf16[5,208,512]{2,1,0:T(8,128)(2,1)}, f32[5,208,512]{2,...) custom-call(bf16[5,208,512]{2,1,0:T(8,128)(2,1)} %pad.23.refs_0_.tok_ref, ...), custom_call_target="tpu_custom_call" | custom-call | flops 5000000000 | bytes 20000000 | tf_op jit(solution)/shard_map/attention_forward/pallas_call | solution.py:746
  120.0 45.3 %collective-permute-done.5 = s32[5,8,208]{2,1,0:T(8,128)S(1)} collective-permute-done((s32[5,8,208]{2,1,0:T(8,128)S(1)}, s32[5,8,208]{2,1,0:T(8,128)S(1)}, u32[]{:S(2)}, u32[]{:S(2)}) %collective-permute-start.5) | collective-permute-done | bytes 33312 | tf_op jit(solution)/shard_map/ppermute | solution.py:734
  167.8 4.6 pad_maximum_fusion.2.refs_2_.refs_6_
  172.4 31.5 %all-gather.16.cloned.1.call-done = bf16[1,2048,512]{2,1,0:T(8,128)(2,1)} async-done(((bf16[1,512,512]{2,1,0:T(8,128)(2,1)}), bf16[1,2048,512]{2,1,0:T(8,128)(2,1)}) %all-gather.16.cloned.1.call-update) | async-done | bytes 2097168 | tf_op jit(solution)/shard_map/all_gather | solution.py:729
  203.9 37.6 %all-gather.12.cloned.1.call-done = bf16[2048,512]{1,0:T(8,128)(2,1)} async-done(((bf16[512,512]{1,0:T(8,128)(2,1)}), bf16[2048,512]{1,0:T(8,128)(2,1)}) %all-gather.12.cloned.1.call-update) | async-done | bytes 2097168 | tf_op jit(solution)/shard_map/all_gather | solution.py:729
  241.5 4.8 pad_maximum_fusion.3.refs_3_.refs_7_
  249.8 33.5 %expert_forward.1 = (bf16[2,4,320,512]{3,2,1,0:T(8,128)(2,1)}, bf16[2,4,320,2048]{3,2,1,0:T(8,128)(2,1)}, bf16[2,4,320,2048]{3,2,1,0:T(8,128)(2,1)}, bf16[2,4,320,512]{3,2,1,0:T(8,128)(2,1)}) custom-call(bf16[4,5,208,512]{3,2,1,0:T(8,128)(2,1)} %pad_maximum_fusion.refs_0_, s32[4,5,8,208]{3,2,1,0:T(8,128)} %pad_add_fusion.refs_1_, ...), custom_call_target="tpu_custom_call" | custom-call | flops 14000000000 | bytes 40000000 | tf_op jit(solution)/shard_map/expert_forward/pallas_call | solution.py:779
  294.3 11.1 %collective-permute-done.10 = bf16[2,320,512]{2,1,0:T(8,128)(2,1)S(1)} collective-permute-done((bf16[2,320,512]{2,1,0:T(8,128)(2,1)}, bf16[2,320,512]{2,1,0:T(8,128)(2,1)S(1)}, u32[]{:S(2)}, u32[]{:S(2)}) %collective-permute-start.10) | collective-permute-done | bytes 655392 | tf_op jit(solution)/shard_map/ppermute | solution.py:734
  305.4 14.2 %collective-permute-done.9 = bf16[2,320,512]{2,1,0:T(8,128)(2,1)} collective-permute-done((bf16[2,320,512]{2,1,0:T(8,128)(2,1)}, bf16[2,320,512]{2,1,0:T(8,128)(2,1)}, u32[]{:S(2)}, u32[]{:S(2)}) %collective-permute-start.9) | collective-permute-done | bytes 655392 | tf_op jit(solution)/shard_map/ppermute | solution.py:734
  322.9 12.2 %combine_and_loss.1 = (bf16[5,208,512]{2,1,0:T(8,128)(2,1)}, f32[5,208,512]{2,1,0:T(8,128)}, bf16[5,208,512]{2,1,0:T(8,128)(2,1)}, f32[5,208,128]{2,1,0:T(8,128)}, f32[8,128]{1,0:T(8,128)}) custom-call(f32[1,1]{1,0:T(1,128)} %bitcast.2.refs_0_, f32[5,208,512]{2,1,0:T(8,128)} %get-tuple-element.33.refs_1_.resid_ref, bf16[2560,512]{1,0:T(8,128)(2,1)} %bitcast.67, ...), custom_call_target="tpu_custom_call" | custom-call | flops 5000000000 | bytes 10000000 | tf_op jit(solution)/shard_map/combine_and_loss/pallas_call | solution.py:801
  338.9 45.6 %collective-permute-done.16 = f32[5,8,208]{2,1,0:T(8,128)S(1)} collective-permute-done((f32[5,8,208]{2,1,0:T(8,128)S(1)}, f32[5,8,208]{2,1,0:T(8,128)S(1)}, u32[]{:S(2)}, u32[]{:S(2)}) %collective-permute-start.16) | collective-permute-done | bytes 33312 | tf_op jit(solution)/shard_map/ppermute | solution.py:734
  389.8 42.2 %expert_backward.1 = (bf16[2,4,320,512]{3,2,1,0:T(8,128)(2,1)}, bf16[2,512,2048]{2,1,0:T(8,128)(2,1)}, bf16[2,512,2048]{2,1,0:T(8,128)(2,1)}) custom-call(bf16[4,5,208,512]{3,2,1,0:T(8,128)(2,1)} %pad_maximum_fusion.1.refs_0_, s32[4,5,8,208]{3,2,1,0:T(8,128)} %pad_add_fusion.refs_1_, f32[4,5,8,208]{3,2,1,0:T(8,128)} %pad_maximum_fusion.6.refs_2_, ...), custom_call_target="tpu_custom_call" | custom-call | flops 24000000000 | bytes 40000000 | tf_op jit(solution)/shard_map/expert_backward/pallas_call | solution.py:823
  432.1 4.9 slice_bitcast_fusion.1
  437.0 4.8 slice_bitcast_fusion.3
  447.7 12.6 %collective-permute-done.19 = bf16[2,320,512]{2,1,0:T(8,128)(2,1)S(1)} collective-permute-done((bf16[2,320,512]{2,1,0:T(8,128)(2,1)S(1)}, bf16[2,320,512]{2,1,0:T(8,128)(2,1)S(1)}, u32[]{:S(2)}, u32[]{:S(2)}) %collective-permute-start.19) | collective-permute-done | bytes 655392 | tf_op jit(solution)/shard_map/ppermute | solution.py:734
  460.3 14.5 %collective-permute-done.18 = bf16[2,320,512]{2,1,0:T(8,128)(2,1)S(1)} collective-permute-done((bf16[2,320,512]{2,1,0:T(8,128)(2,1)S(1)}, bf16[2,320,512]{2,1,0:T(8,128)(2,1)S(1)}, u32[]{:S(2)}, u32[]{:S(2)}) %collective-permute-start.18) | collective-permute-done | bytes 655392 | tf_op jit(solution)/shard_map/ppermute | solution.py:734
  476.7 30.6 %attention_backward.1 = (f32[5,208,512]{2,1,0:T(8,128)}, f32[512,1536]{1,0:T(8,128)}, f32[512,512]{1,0:T(8,128)}, f32[16,512]{1,0:T(8,128)}) custom-call(bf16[5,208,512]{2,1,0:T(8,128)(2,1)} %pad.23.refs_0_.tok_ref, bf16[512,1536]{1,0:T(8,128)(2,1)} %slice.120.refs_1_.wqkv_ref, bf16[512,512]{1,0:T(8,128)(2,1)} %slice.121.refs_2_.wout_ref, ...), custom_call_target="tpu_custom_call" | custom-call | flops 10000000000 | bytes 30000000 | tf_op jit(solution)/shard_map/attention_backward/pallas_call | solution.py:843
  508.3 5.9 concatenate.11
  521.8 27.2 %reduce-scatter.12.cloned.1.call-done = bf16[512,512]{1,0:T(8,128)(2,1)} async-done(((bf16[512,2048]{1,0:T(8,128)(2,1)}), bf16[512,512]{1,0:T(8,128)(2,1)}) %reduce-scatter.12.cloned.1.call-update) | async-done | bytes 524304 | tf_op jit(solution)/shard_map/reduce_scatter | solution.py:863
  555.0 32.5 %reduce-scatter.8.cloned.1.call-done = bf16[128,2048]{1,0:T(8,128)(2,1)} async-done(((bf16[512,2048]{1,0:T(8,128)(2,1)}), bf16[128,2048]{1,0:T(8,128)(2,1)}) %reduce-scatter.8.cloned.1.call-update) | async-done | bytes 524304 | tf_op jit(solution)/shard_map/reduce_scatter | solution.py:862
  589.6 143.1 %reduce-scatter.6.cloned.1.call-done = f32[16,2176]{1,0:T(8,128)} async-done(((f32[512,2176]{1,0:T(8,128)}), f32[16,2176]{1,0:T(8,128)}) %reduce-scatter.6.cloned.1.call-update) | async-done | bytes 139280 | tf_op jit(solution)/shard_map/reduce_scatter | solution.py:874
  (150 shorter events, 86.1 us)
Async XLA Ops:
  7.2 85.8 %all-gather.8.cloned.1.call-start = ((), (), s32[]{:S(2)}) async-start(), calls=%async_computation.5 | async-start | bytes 2297856 | tf_op jit(solution)/shard_map/all_gather | solution.py:709
  13.7 154.1 %all-gather.14.cloned.1.call-start = ((), (), s32[]{:S(2)}) async-start(), calls=%async_computation.13 | async-start | bytes 2621440 | tf_op jit(solution)/shard_map/all_gather | solution.py:728
  14.5 153.3 %all-gather.10.cloned.1.call-start = ((), (), s32[]{:S(2)}) async-start(), calls=%async_computation.6 | async-start | bytes 2621440 | tf_op jit(solution)/shard_map/all_gather | solution.py:728
  44.4 159.6 %all-gather.16.cloned.1.call-start = ((), (), s32[]{:S(2)}) async-start(), calls=%async_computation.14 | async-start | bytes 2621440 | tf_op jit(solution)/shard_map/all_gather | solution.py:729
  44.9 196.6 %all-gather.12.cloned.1.call-start = ((), (), s32[]{:S(2)}) async-start(), calls=%async_computation.7 | async-start | bytes 2621440 | tf_op jit(solution)/shard_map/all_gather | solution.py:729
  74.4 439.8 %reduce-scatter.14.cloned.1.call-start = ((), (), s32[]{:S(2)}) async-start(), calls=%async_computation.12 | async-start | bytes 2621440 | tf_op jit(solution)/shard_map/reduce_scatter | solution.py:863
  115.9 130.4 %collective-permute-start.2 = (bf16[5,208,512]{2,1,0:T(8,128)(2,1)}, bf16[5,208,512]{2,1,0:T(8,128)(2,1)S(1)}, u32[]{:S(2)}, u32[]{:S(2)}) collective-permute-start(bf16[5,208,512]{2,1,0:T(8,128)(2,1)} %get-tuple-element.34), channel_id=1, source_target_pairs={{0,3},{1,2},{2,1},{3,0},{4,7},{5,6},{6,5},{7,4},{8,11},{9,10},{10,... | collective-permute-start | bytes 3194888 | tf_op jit(solution)/shard_map/ppermute | solution.py:734
  116.4 129.9 %collective-permute-start.1 = (bf16[5,208,512]{2,1,0:T(8,128)(2,1)}, bf16[5,208,512]{2,1,0:T(8,128)(2,1)}, u32[]{:S(2)}, u32[]{:S(2)}) collective-permute-start(bf16[5,208,512]{2,1,0:T(8,128)(2,1)} %get-tuple-element.34), channel_id=1, source_target_pairs={{0,2},{1,3},{2,0},{3,1},{4,6},{5,7},{6,4},{7,5},{8,10},{9,11},{10,... | collective-permute-start | bytes 3194888 | tf_op jit(solution)/shard_map/ppermute | solution.py:734
  117.9 128.5 %collective-permute-start = (bf16[5,208,512]{2,1,0:T(8,128)(2,1)}, bf16[5,208,512]{2,1,0:T(8,128)(2,1)}, u32[]{:S(2)}, u32[]{:S(2)}) collective-permute-start(bf16[5,208,512]{2,1,0:T(8,128)(2,1)} %get-tuple-element.34), channel_id=1, source_target_pairs={{0,1},{1,0},{2,3},{3,2},{4,5},{5,4},{6,7},{7,6},{8,9},{9,8},{10,11... | collective-permute-start | bytes 3194888 | tf_op jit(solution)/shard_map/ppermute | solution.py:734
  117.9 47.5 %collective-permute-start.5 = (s32[5,8,208]{2,1,0:T(8,128)S(1)}, s32[5,8,208]{2,1,0:T(8,128)S(1)}, u32[]{:S(2)}, u32[]{:S(2)}) collective-permute-start(s32[5,8,208]{2,1,0:T(8,128)S(1)} %copy-done.8), channel_id=1, source_target_pairs={{0,3},{1,2},{2,1},{3,0},{4,7},{5,6},{6,5},{7,4},{8,11},{9,10},{10,... | collective-permute-start | bytes 99848 | tf_op jit(solution)/shard_map/ppermute | solution.py:734
  118.6 48.0 %collective-permute-start.4 = (s32[5,8,208]{2,1,0:T(8,128)S(1)}, s32[5,8,208]{2,1,0:T(8,128)S(1)}, u32[]{:S(2)}, u32[]{:S(2)}) collective-permute-start(s32[5,8,208]{2,1,0:T(8,128)S(1)} %copy-done.8), channel_id=1, source_target_pairs={{0,2},{1,3},{2,0},{3,1},{4,6},{5,7},{6,4},{7,5},{8,10},{9,11},{10,... | collective-permute-start | bytes 99848 | tf_op jit(solution)/shard_map/ppermute | solution.py:734
  289.1 30.5 %collective-permute-start.9 = (bf16[2,320,512]{2,1,0:T(8,128)(2,1)}, bf16[2,320,512]{2,1,0:T(8,128)(2,1)}, u32[]{:S(2)}, u32[]{:S(2)}) collective-permute-start(bf16[2,320,512]{2,1,0:T(8,128)(2,1)} %get-tuple-element.97), channel_id=1, source_target_pairs={{0,2},{1,3},{2,0},{3,1},{4,6},{5,7},{6,4},{7,5},{8,10},{9,11},{10,... | collective-permute-start | bytes 1966088 | tf_op jit(solution)/shard_map/ppermute | solution.py:734
  289.7 29.9 %collective-permute-start.8 = (bf16[2,320,512]{2,1,0:T(8,128)(2,1)}, bf16[2,320,512]{2,1,0:T(8,128)(2,1)}, u32[]{:S(2)}, u32[]{:S(2)}) collective-permute-start(bf16[2,320,512]{2,1,0:T(8,128)(2,1)} %get-tuple-element.98), channel_id=1, source_target_pairs={{0,1},{1,0},{2,3},{3,2},{4,5},{5,4},{6,7},{7,6},{8,9},{9,8},{10,11... | collective-permute-start | bytes 1966088 | tf_op jit(solution)/shard_map/ppermute | solution.py:734
  335.1 51.4 %collective-permute-start.13 = (bf16[5,208,512]{2,1,0:T(8,128)(2,1)}, bf16[5,208,512]{2,1,0:T(8,128)(2,1)S(1)}, u32[]{:S(2)}, u32[]{:S(2)}) collective-permute-start(bf16[5,208,512]{2,1,0:T(8,128)(2,1)} %get-tuple-element.38), channel_id=1, source_target_pairs={{0,3},{1,2},{2,1},{3,0},{4,7},{5,6},{6,5},{7,4},{8,11},{9,10},{10,... | collective-permute-start | bytes 3194888 | tf_op jit(solution)/shard_map/ppermute | solution.py:734
  336.3 50.2 %collective-permute-start.12 = (bf16[5,208,512]{2,1,0:T(8,128)(2,1)}, bf16[5,208,512]{2,1,0:T(8,128)(2,1)S(1)}, u32[]{:S(2)}, u32[]{:S(2)}) collective-permute-start(bf16[5,208,512]{2,1,0:T(8,128)(2,1)} %get-tuple-element.38), channel_id=1, source_target_pairs={{0,2},{1,3},{2,0},{3,1},{4,6},{5,7},{6,4},{7,5},{8,10},{9,11},{10,... | collective-permute-start | bytes 3194888 | tf_op jit(solution)/shard_map/ppermute | solution.py:734
  336.8 49.7 %collective-permute-start.11 = (bf16[5,208,512]{2,1,0:T(8,128)(2,1)}, bf16[5,208,512]{2,1,0:T(8,128)(2,1)S(1)}, u32[]{:S(2)}, u32[]{:S(2)}) collective-permute-start(bf16[5,208,512]{2,1,0:T(8,128)(2,1)} %get-tuple-element.38), channel_id=1, source_target_pairs={{0,1},{1,0},{2,3},{3,2},{4,5},{5,4},{6,7},{7,6},{8,9},{9,8},{10,11... | collective-permute-start | bytes 3194888 | tf_op jit(solution)/shard_map/ppermute | solution.py:734
  337.0 47.6 %collective-permute-start.16 = (f32[5,8,208]{2,1,0:T(8,128)S(1)}, f32[5,8,208]{2,1,0:T(8,128)S(1)}, u32[]{:S(2)}, u32[]{:S(2)}) collective-permute-start(f32[5,8,208]{2,1,0:T(8,128)S(1)} %copy-done.7), channel_id=1, source_target_pairs={{0,3},{1,2},{2,1},{3,0},{4,7},{5,6},{6,5},{7,4},{8,11},{9,10},{10,... | collective-permute-start | bytes 99848 | tf_op jit(solution)/shard_map/ppermute | solution.py:734
  338.4 47.3 %collective-permute-start.15 = (f32[5,8,208]{2,1,0:T(8,128)S(1)}, f32[5,8,208]{2,1,0:T(8,128)S(1)}, u32[]{:S(2)}, u32[]{:S(2)}) collective-permute-start(f32[5,8,208]{2,1,0:T(8,128)S(1)} %copy-done.7), channel_id=1, source_target_pairs={{0,2},{1,3},{2,0},{3,1},{4,6},{5,7},{6,4},{7,5},{8,10},{9,11},{10,... | collective-permute-start | bytes 99848 | tf_op jit(solution)/shard_map/ppermute | solution.py:734
  436.9 79.8 %reduce-scatter.10.cloned.1.call-start = ((), (), s32[]{:S(2)}) async-start(), calls=%async_computation.10 | async-start | bytes 2621440 | tf_op jit(solution)/shard_map/reduce_scatter | solution.py:862
  441.8 107.2 %reduce-scatter.12.cloned.1.call-start = ((), (), s32[]{:S(2)}) async-start(), calls=%async_computation.11 | async-start | bytes 2621440 | tf_op jit(solution)/shard_map/reduce_scatter | solution.py:863
  442.6 144.9 %reduce-scatter.8.cloned.1.call-start = ((), (), s32[]{:S(2)}) async-start(), calls=%async_computation.9 | async-start | bytes 2621440 | tf_op jit(solution)/shard_map/reduce_scatter | solution.py:862
  443.3 289.4 %reduce-scatter.6.cloned.1.call-start = ((), (), s32[]{:S(2)}) async-start(), calls=%async_computation.8 | async-start | bytes 4595712 | tf_op jit(solution)/shard_map/reduce_scatter | solution.py:874
  514.2 38.2 %collective-permute-start.21 = (bf16[512,512]{1,0:T(8,128)(2,1)}, bf16[512,512]{1,0:T(8,128)(2,1)S(1)}, u32[]{:S(2)}, u32[]{:S(2)}) collective-permute-start(bf16[512,512]{1,0:T(8,128)(2,1)} %reduce-scatter.14.cloned.1.call-done), channel_id=1, source_target_pairs={{0,4},{1,5},{2,6},{3,7},{4,0},{5,1},{6,2},{7,3},{8,12},{9,13},{10,... | collective-permute-start | bytes 1572872 | tf_op jit(solution)/shard_map/ppermute | solution.py:865
  516.7 70.7 %collective-permute-start.20 = (bf16[128,2048]{1,0:T(8,128)(2,1)}, bf16[128,2048]{1,0:T(8,128)(2,1)S(1)}, u32[]{:S(2)}, u32[]{:S(2)}) collective-permute-start(bf16[128,2048]{1,0:T(8,128)(2,1)} %reduce-scatter.10.cloned.1.call-done), channel_id=1, source_target_pairs={{0,4},{1,5},{2,6},{3,7},{4,0},{5,1},{6,2},{7,3},{8,12},{9,13},{10,... | collective-permute-start | bytes 1572872 | tf_op jit(solution)/shard_map/ppermute | solution.py:864
  (20 other events, 339.1 us)
Sparse Core Ops, SparseCore 0:
  13.9 79.0 all-gather.7
  94.8 34.2 all-gather.13
  131.5 35.2 all-gather.9
  168.6 35.2 all-gather.15
  206.2 35.2 all-gather.11
  437.1 35.2 reduce-scatter.13
  475.6 35.1 reduce-scatter.9
  513.8 35.1 reduce-scatter.11
  552.2 35.1 reduce-scatter.7
  589.6 143.1 reduce-scatter.5

commit v2 on v1

--- a/solution.py
+++ b/solution.py
@@ -337,6 +337,37 @@
 
 def row_ids(shape):
     return lax.broadcasted_iota(jnp.int32, shape, len(shape) - 2)
+
+
+MESH = pl.DeviceIdType.MESH
+
+
+def flip(index, bit):
+    return index + bit * (1 - 2 * lax.rem(index // bit, 2))
+
+
+def send(src, dst, sems, slot, device):
+    return pltpu.make_async_remote_copy(
+        src_ref=src, dst_ref=dst, send_sem=sems[0].at[slot], recv_sem=sems[1].at[slot],
+        device_id=device, device_id_type=MESH,
+    )
+
+
+def greet(peers):
+    barrier = pltpu.get_barrier_semaphore()
+    for peer in peers:
+        pl.semaphore_signal(barrier, inc=1, device_id=peer, device_id_type=MESH)
+    pl.semaphore_wait(barrier, len(peers))
+
+
+def place():
+    dp_at, ex_at = lax.axis_index("dp"), lax.axis_index("expert")
+    near = [None, flip(dp_at, 1), flip(dp_at, 2), flip(flip(dp_at, 1), 2)]
+    return dp_at, ex_at, near
+
+
+def sem_pairs(count):
+    return [pltpu.SemaphoreType.DMA((count,)), pltpu.SemaphoreType.DMA((count,))]
 
 
 def normalize(values):
@@ -552,16 +583,82 @@
         @pl.when(half == 1)
         def _():
             gin_ref[:, cut] = (acc_in[:, cut] + gin).astype(BF16)
-            gout_ref[:, cut] = (acc_out[:, cut] + gout).astype(BF16)
+            gout_ref[offset // step] = (acc_out[:, cut] + gout).astype(BF16)
 
     back_ref[...] = result.astype(BF16).reshape(back_ref.shape)
 
 
 def back_kernel(
-    tok_ref, wqkv_ref, wout_ref, gain_ref, router_t_ref, cols_ref, back_ref, dlogit_ref, resid_ref,
-    dout_ref, qkv_ref, probs_ref, mixed_ref,
-    tgrad_ref, gqkv_ref, gout_ref, gmisc_ref,
+    images, tok_ref, wqkv_ref, wout_ref, gain_ref, router_t_ref, cols_ref, back_ref, dlogit_ref, resid_ref,
+    dout_ref, qkv_ref, probs_ref, mixed_ref, loss_ref, gin_ref, gex_ref,
+    tgrad_ref, dense_ref, misc_ref, gin_out, gex_out,
+    acc, acc_misc, part_in, part_ex, got_in, got_ex, sum_in, sum_ex, more_in, more_ex, far_in, far_ex, came_in, came_ex,
+    low, mate, low_mate, plane, low_plane, line, misc_got, local_sem, w_send, w_recv, d_send, d_recv, m_send, m_recv,
 ):
+    step_at = pl.program_id(0)
+    dp_at, ex_at, near = place()
+    core, floor = lax.rem(ex_at, 2), ex_at // 2
+    wsem, dsem, msem = (w_send, w_recv), (d_send, d_recv), (m_send, m_recv)
+    tensors = [
+        (gin_ref, part_in, got_in, sum_in, more_in, far_in, came_in, gin_out, 1, 2),
+        (gex_ref, part_ex, got_ex, sum_ex, more_ex, far_ex, came_ex, gex_out, 2, 1),
+    ]
+
+    def local_copies():
+        copies = []
+        for t, (grad, part, _, _, _, _, _, _, _, second) in enumerate(tensors):
+            for q in range(2):
+                for s in range(2):
+                    owner = dp_at if s == 0 else near[second]
+                    copies.append(
+                        pltpu.make_async_copy(grad.at[q, owner], part.at[q, s], local_sem.at[4 * t + 2 * q + s])
+                    )
+        return copies
+
+    def first_round(q):
+        copies = []
+        for t, (grad, _, got, _, _, _, _, _, first, _) in enumerate(tensors):
+            for s in range(2):
+                owner = near[first] if s == 0 else near[3]
+                copies.append(
+                    send(grad.at[q, owner], got.at[q, s], wsem, 8 * q + 4 * t + s, (near[first], ex_at))
+                )
+        return copies
+
+    def second_round(q):
+        return [
+            send(passed.at[q], more.at[q], wsem, 8 * q + 4 * t + 2, (near[second], ex_at))
+            for t, (_, _, _, passed, more, _, _, _, _, second) in enumerate(tensors)
+        ]
+
+    def far_round():
+        return [
+            send(far, came, wsem, 4 * t + 3, (dp_at, flip(ex_at, 4)))
+            for t, (_, _, _, _, _, far, came, _, _, _) in enumerate(tensors)
+        ]
+
+    def add_first(q):
+        for copy in first_round(q):
+            copy.wait_recv()
+        for _, part, got, passed, _, _, _, _, _, _ in tensors:
+            passed[q] = (part[q, 1].astype(F32) + got[q, 1].astype(F32)).astype(BF16)
+        for copy in second_round(q):
+            copy.start()
+
+    def total_of(tensor, q):
+        _, part, got, _, more, _, _, _, _, _ = tensor
+        return part[q, 0].astype(F32) + got[q, 0].astype(F32) + more[q].astype(F32)
+
+    @pl.when(step_at == 0)
+    def _():
+        greet(
+            [(near[k], ex_at) for k in (1, 2, 3)]
+            + [(dp_at, flip(ex_at, bit)) for bit in (1, 2, 4)]
+            + [(dp_at, flip(flip(ex_at, 2), 4))]
+        )
+        for copy in first_round(1) + first_round(0) + local_copies():
+            copy.start()
+
     count = back_ref.shape[0]
     cols = cols_ref[...]
     hot = jnp.where(hot_cols(cols[:, 0:1], count) | hot_cols(cols[:, 1:2], count), 1.0, 0.0)
@@ -631,25 +728,100 @@
     dact_one = contract_cols(dqkv, wqkv_ref[...])
     grad_one, ggain_one = norm_back(dact_one, normed_one, inverse_one, gain_one)
     tgrad_ref[...] = dresid + grad_one
+    ids = row_ids((8, width))
     gmisc = jnp.concatenate(
-        [
-            grouter[:8],
-            jnp.where(row_ids((8, width)) == 0, ggain_one, jnp.where(row_ids((8, width)) == 1, ggain_two, 0.0)),
-        ],
-        axis=0,
-    )
-
-    @pl.when(pl.program_id(0) == 0)
+        [grouter[:8], jnp.where(ids == 0, ggain_one, jnp.where(ids == 1, ggain_two, 0.0))], axis=0
+    )
+
+    @pl.when(step_at == 0)
     def _():
-        gqkv_ref[...] = gqkv
-        gout_ref[...] = gout
-        gmisc_ref[...] = gmisc
-
-    @pl.when(pl.program_id(0) > 0)
+        for copy in local_copies():
+            copy.wait()
+        acc[:, : 3 * width] = gqkv
+        acc[:, 3 * width :] = gout
+        loss_row = jnp.where(row_ids((8, 128)) == 2, loss_ref[...], 0.0)
+        acc_misc[...] = gmisc + jnp.concatenate(
+            [jnp.zeros((8, width), F32), jnp.concatenate([loss_row] * (width // 128), axis=1)], axis=0
+        )
+
+    @pl.when(step_at > 0)
     def _():
-        gqkv_ref[...] += gqkv
-        gout_ref[...] += gout
-        gmisc_ref[...] += gmisc
+        acc[:, : 3 * width] += gqkv
+        acc[:, 3 * width :] += gout
+        acc_misc[...] += gmisc
+
+    @pl.when(step_at == images - 2)
+    def _():
+        add_first(1)
+
+    @pl.when(step_at == images - 1)
+    def _():
+        lines, shard = low.shape[1], low.shape[3]
+        low[...] = acc[...].astype(BF16).reshape(low.shape)
+        other = lax.rem(core + 1, 2)
+        to_mate = send(low.at[:, :, other], mate, dsem, 0, (dp_at, flip(ex_at, 1)))
+        to_mate.start()
+        misc_peers = [
+            (dp_at, flip(ex_at, 1)), (near[1], ex_at), (near[2], ex_at), (dp_at, flip(ex_at, 2)), (dp_at, flip(ex_at, 4)),
+        ]
+        misc = [send(acc_misc.at[...] if k == 0 else misc_got.at[5 + k - 1], misc_got.at[k], msem, k, misc_peers[k]) for k in range(5)]
+        misc[0].start()
+        add_first(0)
+
+        for copy in second_round(1):
+            copy.wait_recv()
+        for tensor in tensors:
+            tensor[5][...] = total_of(tensor, 1).astype(BF16)
+        for copy in far_round():
+            copy.start()
+
+        def misc_step(k):
+            misc[k].wait_recv()
+            before = acc_misc[...] if k == 0 else misc_got[5 + k - 1]
+            misc_got[5 + k] = before + misc_got[k]
+            if k < 4:
+                misc[k + 1].start()
+
+        to_mate.wait_recv()
+        low_mate[...] = (low[:, :, core].astype(F32) + mate[...].astype(F32)).astype(BF16)
+        to_plane = [send(low_mate.at[near[k]], plane.at[k - 1], dsem, k, (near[k], ex_at)) for k in (1, 2, 3)]
+        for copy in to_plane:
+            copy.start()
+        misc_step(0)
+        misc_step(1)
+        misc_step(2)
+        for copy in to_plane:
+            copy.wait_recv()
+        summed = low_mate[dp_at].astype(F32)
+        for k in range(3):
+            summed = summed + plane[k].astype(F32)
+        low_plane[...] = summed.astype(BF16)
+        floors = [flip(floor, 1), flip(floor, 2), flip(flip(floor, 1), 2)]
+        to_line = [
+            send(low_plane.at[floors[k]], line.at[k], dsem, 4 + k, (dp_at, 2 * floors[k] + core)) for k in range(3)
+        ]
+        for copy in to_line:
+            copy.start()
+        misc_step(3)
+        misc_step(4)
+        misc_ref[...] = misc_got[9]
+        for copy in to_line:
+            copy.wait_recv()
+        result = low_plane[floor].astype(F32)
+        for k in range(3):
+            result = result + line[k].astype(F32)
+        dense_ref[...] = result
+
+        for copy in second_round(0):
+            copy.wait_recv()
+        for copy in far_round():
+            copy.wait_recv()
+        for tensor in tensors:
+            tensor[7][...] = total_of(tensor, 0) + tensor[6][...].astype(F32)
+        for copy in [to_mate] + misc + to_plane + to_line + first_round(0) + first_round(1):
+            copy.wait_send()
+        for copy in second_round(0) + second_round(1) + far_round():
+            copy.wait_send()
 
 
 def shape(dims, kind):
@@ -828,10 +1000,12 @@
             by_both(cap, width), by_both(cap, hidden_width), by_both(cap, hidden_width),
             by_expert(width, hidden_width), by_expert(hidden_width, width),
         ],
-        out_specs=[by_both(cap, width), by_expert(width, hidden_width), by_expert(width, hidden_width)],
+        out_specs=[
+            by_both(cap, width), by_expert(width, hidden_width), by_expert(dp, width, hidden_width // dp),
+        ],
         out_shape=[
             shape((2, group, cap, width), BF16), shape((2, width, hidden_width), BF16),
-            shape((2, width, hidden_width), BF16),
+            shape((2, dp, width, hidden_width // dp), BF16),
         ],
         scratch_shapes=[pltpu.VMEM((width, hidden_width), F32), pltpu.VMEM((width, hidden_width), F32)],
         compiler_params=params(),
@@ -840,40 +1014,52 @@
     )(dlow_all, code_all, grow_all, rows_in, hidden, slope, win_full, wout_full)
     grad_back = give_back(drows)
 
-    tgrad, gqkv, gout_w, gmisc = pl.pallas_call(
-        back_kernel,
+    floors = experts // 2
+    in_part, ex_part = (width // dp, hidden_width), (width, hidden_width // dp)
+    any_space = pl.BlockSpec(memory_space=pl.ANY)
+
+    def vmem(*dims):
+        return pltpu.VMEM(dims, BF16)
+
+    tgrad, dense_grad, misc, gin_own, gex_own = pl.pallas_call(
+        lambda *refs: back_kernel(images, *refs),
         grid=(images,),
         in_specs=[
             per_image(rows, width), whole((width, 3 * width)), whole((width, width)), whole((2, width)),
             whole((128, width)), per_image(rows, 8), whole((2 * group * cap, width)),
             per_image(rows, gate_lanes), per_image(rows, width), per_image(rows, width),
-            per_image(rows, 3 * width), per_image(HEADS, rows, rows), per_image(rows, width),
-        ],
-        out_specs=[per_image(rows, width), whole((width, 3 * width)), whole((width, width)), whole((16, width))],
+            per_image(rows, 3 * width), per_image(HEADS, rows, rows), per_image(rows, width), whole((8, 128)),
+            any_space, any_space,
+        ],
+        out_specs=[
+            per_image(rows, width), whole((shard, 4 * width)), whole((16, width)), whole(in_part), whole(ex_part),
+        ],
         out_shape=[
-            shape((images, rows, width), F32), shape((width, 3 * width), F32), shape((width, width), F32),
-            shape((16, width), F32),
-        ],
-        compiler_params=params(),
+            shape((images, rows, width), F32), shape((shard, 4 * width), F32), shape((16, width), F32),
+            shape(in_part, F32), shape(ex_part, F32),
+        ],
+        scratch_shapes=[
+            pltpu.VMEM((width, 4 * width), F32), pltpu.VMEM((16, width), F32),
+            vmem(2, 2, *in_part), vmem(2, 2, *ex_part), vmem(2, 2, *in_part), vmem(2, 2, *ex_part),
+            vmem(2, *in_part), vmem(2, *ex_part), vmem(2, *in_part), vmem(2, *ex_part),
+            vmem(*in_part), vmem(*ex_part), vmem(*in_part), vmem(*ex_part),
+            vmem(dp, floors, 2, shard, 4 * width), vmem(dp, floors, shard, 4 * width), vmem(dp, floors, shard, 4 * width),
+            vmem(3, floors, shard, 4 * width), vmem(floors, shard, 4 * width), vmem(3, shard, 4 * width),
+            pltpu.VMEM((10, 16, width), F32), pltpu.SemaphoreType.DMA((8,)),
+            *sem_pairs(16), *sem_pairs(8), *sem_pairs(5),
+        ],
+        compiler_params=pltpu.CompilerParams(
+            vmem_limit_bytes=60 * MB, collective_id=1, has_side_effects=True
+        ),
         cost_estimate=pl.CostEstimate(flops=int(10e9), bytes_accessed=int(3e7), transcendentals=0),
         name="attention_backward",
-    )(tok_p, qkv_full, out_full, gains, router_t, cols, grad_back, dlogits, resid, dout, qkv_p, probs, mixed)
-
-    gin_sums = [lax.psum_scatter(gin[q], "dp", scatter_dimension=0, tiled=True) for q in (1, 0)]
-    gout_sums = [lax.psum_scatter(gout_t[q], "dp", scatter_dimension=1, tiled=True) for q in (1, 0)]
-    gin_own = gin_sums[1].astype(F32) + lax.ppermute(gin_sums[0], "expert", far).astype(F32)
-    gout_own = (gout_sums[1].astype(F32) + lax.ppermute(gout_sums[0], "expert", far).astype(F32)).T
-
-    dense_grad = jnp.concatenate(
-        [
-            gqkv, gout_w, gmisc.T,
-            jnp.broadcast_to(loss_part[0:1, 0:1] / 16.0, (width, 1)), jnp.zeros((width, 111), F32),
-        ],
-        axis=1,
-    )
-    mine = lax.psum_scatter(dense_grad, axes, scatter_dimension=0, tiled=True)
-    misc = mine[:, 4 * width :]
-    loss_value = jnp.sum(misc[:, 16]) * (16.0 / shard) / valid_count
+    )(
+        tok_p, qkv_full, out_full, gains, router_t, cols, grad_back, dlogits, resid, dout, qkv_p, probs, mixed,
+        loss_part, gin.reshape(2, dp, *in_part), gout_t,
+    )
+    flat = lax.axis_index("dp") * experts + me
+    mine = lax.dynamic_slice_in_dim(misc, flat * shard, shard, axis=1)
+    loss_value = misc[10, 0] / valid_count
 
     def unpad(array):
         return array[:, :real_rows].reshape(tok_rows, width)
@@ -882,13 +1068,13 @@
         unpad(block_out),
         loss_value,
         unpad(tgrad),
-        misc[:, 8],
-        mine[:, : 3 * width],
-        mine[:, 3 * width : 4 * width],
-        misc[:, 9],
-        misc[:, :experts],
+        mine[8],
+        dense_grad[:, : 3 * width],
+        dense_grad[:, 3 * width :],
+        mine[9],
+        mine[:experts].T,
         gin_own[None],
-        gout_own[None],
+        gex_own.T[None],
     )
 
 

time: 749 us -> 616 us (0.82)
  waiting for transfers between devices: 491 us -> 285 us
  Pallas kernels: 134 us -> 224 us
  local copies, waits for them, and re-layouts: 54.8 us -> 46.2 us
    reduce_scatter x5 -> x0, waiting for transfers between devices: 203 us -> none  [the longest x1 143 us: fast_shards(): mine = lax.psum_scatter(dense_grad, axes, scatter_dimension=0, tiled=True)]
    pallas_call x1, Pallas kernels: 30.6 us -> 120 us  [fast_shards(): pl.pallas_call(lambda *refs: back_kernel(images, *refs), grid=(images,),...]
    squeeze x2 -> x1, local copies, waits for them, and re-layouts: 9.67 us -> 1.35 us  [fast_shards(): mine[9]]
  transfers between devices with their start and end apart: 32 -> 25, of which waited for: 19 -> 15; matrix products, arithmetic and copies ran while one was open for 7% -> 4% of each run, Pallas kernels for 6% -> 2%
where the time goes in v2:
time: 616 us; the launch traced here: 615 us
  waiting for transfers between devices  285 us (46%)
  Pallas kernels  224 us (36%)
  local copies, waits for them, and re-layouts  46.2 us (8%)
  other arithmetic  24.3 us (4%)
  between operations  18.5 us (3%)
  starting transfers between devices  17.4 us (3%)
    ppermute x18, waiting for transfers between devices, exchange(): lax.ppermute(blocks[k], 'expert', [(i, i ^ k) for i in range(experts)])  146 us
    pallas_call x1, Pallas kernels, fast_shards(): pl.pallas_call(lambda *refs: back_kernel(images, *refs), grid=(images,),...  120 us
    all_gather x4, waiting for transfers between devices, fast_shards(): lax.all_gather(w, 'dp', axis=0, tiled=True)  69.2 us
    pallas_call x1, Pallas kernels, fast_shards(): pl.pallas_call(lambda *refs: expert_back_kernel(cap, group, *refs), grid=...  42.2 us
    pallas_call x1, Pallas kernels, fast_shards(): pl.pallas_call(lambda *refs: expert_forward_kernel(cap, group, *refs), gr...  33.6 us
    ppermute x1, waiting for transfers between devices, fast_shards(): w_out.append(lax.ppermute(w_out[0], 'expert', far))  28.5 us
    ppermute x1, waiting for transfers between devices, fast_shards(): w_in.append(lax.ppermute(w_in[0], 'expert', far))  24.9 us
    pallas_call x1, Pallas kernels, fast_shards(): pl.pallas_call(lambda *refs: forward_kernel(real_rows, experts, *refs), g...  15.2 us
  transfers between devices with their start and end apart: 25, of which 15 were waited for; matrix products, arithmetic and copies ran while one was open for 4% of the time, Pallas kernels for 2%

profile of v2, /device:TPU:0, one launch (start us, length us, event | category | flops | bytes accessed | tf_op | source)
XLA Modules:
  0.0 614.7 jit_solution(7849218713714337271)
XLA Ops:
  14.5 4.1 collective-permute-start.6
  18.6 24.9 %collective-permute-done.6 = bf16[128,2048]{1,0:T(8,128)(2,1)S(1)} collective-permute-done((bf16[128,2048]{1,0:T(8,128)(2,1)}, bf16[128,2048]{1,0:T(8,128)(2,1)S(1)}, u32[]{:S(2)}, u32[]{:S(2)}) %collective-permute-start.6) | collective-permute-done | bytes 524320 | tf_op jit(solution)/shard_map/ppermute | solution.py:898
  45.1 28.5 %collective-permute-done.7 = bf16[512,512]{1,0:T(8,128)(2,1)S(1)} collective-permute-done((bf16[512,512]{1,0:T(8,128)(2,1)}, bf16[512,512]{1,0:T(8,128)(2,1)S(1)}, u32[]{:S(2)}, u32[]{:S(2)}) %collective-permute-start.7) | collective-permute-done | bytes 524320 | tf_op jit(solution)/shard_map/ppermute | solution.py:899
  78.0 15.0 %all-gather.8.cloned.1.call-done = bf16[512,2176]{1,0:T(8,128)(2,1)} async-done(((bf16[16,2176]{1,0:T(8,128)(2,1)}), bf16[512,2176]{1,0:T(8,128)(2,1)}) %all-gather.8.cloned.1.call-update) | async-done | bytes 2228240 | tf_op jit(solution)/shard_map/all_gather | solution.py:881
  94.9 2.7 slice.95.refs_1_
  100.7 15.2 %attention_forward.1 = (bf16[5,208,1536]{2,1,0:T(8,128)(2,1)}, bf16[5,8,208,208]{3,2,1,0:T(8,128)(2,1)}, bf16[5,208,512]{2,1,0:T(8,128)(2,1)}, f32[5,208,512]{2,...) custom-call(bf16[5,208,512]{2,1,0:T(8,128)(2,1)} %pad.23.refs_0_, ...), custom_call_target="tpu_custom_call" | custom-call | flops 5000000000 | bytes 20000000 | tf_op jit(solution)/shard_map/attention_forward/pallas_call | solution.py:918
  120.0 45.3 %collective-permute-done.5 = s32[5,8,208]{2,1,0:T(8,128)S(1)} collective-permute-done((s32[5,8,208]{2,1,0:T(8,128)S(1)}, s32[5,8,208]{2,1,0:T(8,128)S(1)}, u32[]{:S(2)}, u32[]{:S(2)}) %collective-permute-start.5) | collective-permute-done | bytes 33312 | tf_op jit(solution)/shard_map/ppermute | solution.py:906
  167.8 4.5 pad_maximum_fusion.2.refs_2_.refs_6_
  172.4 31.5 %all-gather.16.cloned.1.call-done = bf16[1,2048,512]{2,1,0:T(8,128)(2,1)} async-done(((bf16[1,512,512]{2,1,0:T(8,128)(2,1)}), bf16[1,2048,512]{2,1,0:T(8,128)(2,1)}) %all-gather.16.cloned.1.call-update) | async-done | bytes 2097168 | tf_op jit(solution)/shard_map/all_gather | solution.py:901
  203.9 37.6 %all-gather.12.cloned.1.call-done = bf16[2048,512]{1,0:T(8,128)(2,1)} async-done(((bf16[512,512]{1,0:T(8,128)(2,1)}), bf16[2048,512]{1,0:T(8,128)(2,1)}) %all-gather.12.cloned.1.call-update) | async-done | bytes 2097168 | tf_op jit(solution)/shard_map/all_gather | solution.py:901
  241.5 4.8 pad_maximum_fusion.3.refs_3_.refs_7_
  246.3 3.6 pad_maximum_fusion.refs_0_
  249.9 33.6 %expert_forward.1 = (bf16[2,4,320,512]{3,2,1,0:T(8,128)(2,1)}, bf16[2,4,320,2048]{3,2,1,0:T(8,128)(2,1)}, bf16[2,4,320,2048]{3,2,1,0:T(8,128)(2,1)}, bf16[2,4,320,512]{3,2,1,0:T(8,128)(2,1)}) custom-call(bf16[4,5,208,512]{3,2,1,0:T(8,128)(2,1)} %pad_maximum_fusion.refs_0_, s32[4,5,8,208]{3,2,1,0:T(8,128)} %pad_add_fusion.refs_1_, ...), custom_call_target="tpu_custom_call" | custom-call | flops 14000000000 | bytes 40000000 | tf_op jit(solution)/shard_map/expert_forward/pallas_call | solution.py:951
  285.6 2.7 fusion.2
  294.4 11.1 %collective-permute-done.10 = bf16[2,320,512]{2,1,0:T(8,128)(2,1)S(1)} collective-permute-done((bf16[2,320,512]{2,1,0:T(8,128)(2,1)}, bf16[2,320,512]{2,1,0:T(8,128)(2,1)S(1)}, u32[]{:S(2)}, u32[]{:S(2)}) %collective-permute-start.10) | collective-permute-done | bytes 655392 | tf_op jit(solution)/shard_map/ppermute | solution.py:906
  305.5 14.2 %collective-permute-done.9 = bf16[2,320,512]{2,1,0:T(8,128)(2,1)} collective-permute-done((bf16[2,320,512]{2,1,0:T(8,128)(2,1)}, bf16[2,320,512]{2,1,0:T(8,128)(2,1)}, u32[]{:S(2)}, u32[]{:S(2)}) %collective-permute-start.9) | collective-permute-done | bytes 655392 | tf_op jit(solution)/shard_map/ppermute | solution.py:906
  323.0 12.2 %combine_and_loss.1 = (bf16[5,208,512]{2,1,0:T(8,128)(2,1)}, f32[5,208,512]{2,1,0:T(8,128)}, bf16[5,208,512]{2,1,0:T(8,128)(2,1)}, f32[5,208,128]{2,1,0:T(8,128)}, f32[8,128]{1,0:T(8,128)}) custom-call(f32[1,1]{1,0:T(1,128)} %bitcast.2.refs_0_, f32[5,208,512]{2,1,0:T(8,128)} %get-tuple-element.34.refs_1_.refs_8_, bf16[2560,512]{1,0:T(8,128)(2,1)} %bitcast.63, ...), custom_call_target="tpu_custom_call" | custom-call | flops 5000000000 | bytes 10000000 | tf_op jit(solution)/shard_map/combine_and_loss/pallas_call | solution.py:973
  339.0 45.6 %collective-permute-done.16 = f32[5,8,208]{2,1,0:T(8,128)S(1)} collective-permute-done((f32[5,8,208]{2,1,0:T(8,128)S(1)}, f32[5,8,208]{2,1,0:T(8,128)S(1)}, u32[]{:S(2)}, u32[]{:S(2)}) %collective-permute-start.16) | collective-permute-done | bytes 33312 | tf_op jit(solution)/shard_map/ppermute | solution.py:906
  386.6 3.4 pad_maximum_fusion.1.refs_0_
  390.0 42.2 %expert_backward.1 = (bf16[2,4,320,512]{3,2,1,0:T(8,128)(2,1)}, bf16[2,512,2048]{2,1,0:T(8,128)(2,1)}, bf16[2,4,512,512]{3,2,1,0:T(8,128)(2,1)}) custom-call(bf16[4,5,208,512]{3,2,1,0:T(8,128)(2,1)} %pad_maximum_fusion.1.refs_0_, s32[4,5,8,208]{3,2,1,0:T(8,128)} %pad_add_fusion.refs_1_, f32[4,5,8,208]{3,2,1,0:T(8,128)} %pad_maximum_fusion.6.refs_2_, ...), custom_call_target="tpu_custom_call" | custom-call | flops 24000000000 | bytes 40000000 | tf_op jit(solution)/shard_map/expert_backward/pallas_call | solution.py:995
  434.3 2.8 fusion.1
  440.3 13.5 %collective-permute-done.19 = bf16[2,320,512]{2,1,0:T(8,128)(2,1)S(1)} collective-permute-done((bf16[2,320,512]{2,1,0:T(8,128)(2,1)}, bf16[2,320,512]{2,1,0:T(8,128)(2,1)S(1)}, u32[]{:S(2)}, u32[]{:S(2)}) %collective-permute-start.19) | collective-permute-done | bytes 655392 | tf_op jit(solution)/shard_map/ppermute | solution.py:906
  453.9 14.6 %collective-permute-done.18 = bf16[2,320,512]{2,1,0:T(8,128)(2,1)} collective-permute-done((bf16[2,320,512]{2,1,0:T(8,128)(2,1)}, bf16[2,320,512]{2,1,0:T(8,128)(2,1)}, u32[]{:S(2)}, u32[]{:S(2)}) %collective-permute-start.18) | collective-permute-done | bytes 655392 | tf_op jit(solution)/shard_map/ppermute | solution.py:906
  471.7 120.4 %attention_backward.1 = (f32[5,208,512]{2,1,0:T(8,128)}, f32[16,2048]{1,0:T(8,128)}, f32[16,512]{1,0:T(8,128)}, f32[128,2048]{1,0:T(8,128)}, f32[512,512]{1,0:T(8,128)}) custom-call(bf16[5,208,512]{2,1,0:T(8,128)(2,1)} %pad.23.refs_0_, bf16[512,1536]{1,0:T(8,128)(2,1)} %slice.95.refs_1_, bf16[512,512]{1,0:T(8,128)(2,1)} %slice.96.refs_2_, ...), custom_call_target="tpu_custom_call" | custom-call | flops 10000000000 | bytes 30000000 | tf_op jit(solution)/shard_map/attention_backward/pallas_call | solution.py:1024
  (123 shorter events, 62.1 us)
Async XLA Ops:
  7.2 85.8 %all-gather.8.cloned.1.call-start = ((), (), s32[]{:S(2)}) async-start(), calls=%async_computation | async-start | bytes 2297856 | tf_op jit(solution)/shard_map/all_gather | solution.py:881
  13.7 154.1 %all-gather.14.cloned.1.call-start = ((), (), s32[]{:S(2)}) async-start(), calls=%async_computation.3 | async-start | bytes 2621440 | tf_op jit(solution)/shard_map/all_gather | solution.py:900
  14.5 153.3 %all-gather.10.cloned.1.call-start = ((), (), s32[]{:S(2)}) async-start(), calls=%async_computation.1 | async-start | bytes 2621440 | tf_op jit(solution)/shard_map/all_gather | solution.py:900
  14.5 29.0 %collective-permute-start.6 = (bf16[128,2048]{1,0:T(8,128)(2,1)}, bf16[128,2048]{1,0:T(8,128)(2,1)S(1)}, u32[]{:S(2)}, u32[]{:S(2)}) collective-permute-start(bf16[128,2048]{1,0:T(8,128)(2,1)} %bitcast.77), channel_id=1, source_target_pairs={{0,4},{1,5},{2,6},{3,7},{4,0},{5,1},{6,2},{7,3},{8,12},{9,13},{10,... | collective-permute-start | bytes 1572872 | tf_op jit(solution)/shard_map/ppermute | solution.py:898
  44.4 159.6 %all-gather.16.cloned.1.call-start = ((), (), s32[]{:S(2)}) async-start(), calls=%async_computation.4 | async-start | bytes 2621440 | tf_op jit(solution)/shard_map/all_gather | solution.py:901
  44.9 196.6 %all-gather.12.cloned.1.call-start = ((), (), s32[]{:S(2)}) async-start(), calls=%async_computation.2 | async-start | bytes 2621440 | tf_op jit(solution)/shard_map/all_gather | solution.py:901
  45.0 28.6 %collective-permute-start.7 = (bf16[512,512]{1,0:T(8,128)(2,1)}, bf16[512,512]{1,0:T(8,128)(2,1)S(1)}, u32[]{:S(2)}, u32[]{:S(2)}) collective-permute-start(bf16[512,512]{1,0:T(8,128)(2,1)} %bitcast.78), channel_id=1, source_target_pairs={{0,4},{1,5},{2,6},{3,7},{4,0},{5,1},{6,2},{7,3},{8,12},{9,13},{10,... | collective-permute-start | bytes 1572872 | tf_op jit(solution)/shard_map/ppermute | solution.py:899
  115.9 130.4 %collective-permute-start.2 = (bf16[5,208,512]{2,1,0:T(8,128)(2,1)}, bf16[5,208,512]{2,1,0:T(8,128)(2,1)S(1)}, u32[]{:S(2)}, u32[]{:S(2)}) collective-permute-start(bf16[5,208,512]{2,1,0:T(8,128)(2,1)} %get-tuple-element.35), channel_id=1, source_target_pairs={{0,3},{1,2},{2,1},{3,0},{4,7},{5,6},{6,5},{7,4},{8,11},{9,10},{10,... | collective-permute-start | bytes 3194888 | tf_op jit(solution)/shard_map/ppermute | solution.py:906
  116.5 129.9 %collective-permute-start.1 = (bf16[5,208,512]{2,1,0:T(8,128)(2,1)}, bf16[5,208,512]{2,1,0:T(8,128)(2,1)}, u32[]{:S(2)}, u32[]{:S(2)}) collective-permute-start(bf16[5,208,512]{2,1,0:T(8,128)(2,1)} %get-tuple-element.35), channel_id=1, source_target_pairs={{0,2},{1,3},{2,0},{3,1},{4,6},{5,7},{6,4},{7,5},{8,10},{9,11},{10,... | collective-permute-start | bytes 3194888 | tf_op jit(solution)/shard_map/ppermute | solution.py:906
  117.9 128.4 %collective-permute-start = (bf16[5,208,512]{2,1,0:T(8,128)(2,1)}, bf16[5,208,512]{2,1,0:T(8,128)(2,1)}, u32[]{:S(2)}, u32[]{:S(2)}) collective-permute-start(bf16[5,208,512]{2,1,0:T(8,128)(2,1)} %get-tuple-element.35), channel_id=1, source_target_pairs={{0,1},{1,0},{2,3},{3,2},{4,5},{5,4},{6,7},{7,6},{8,9},{9,8},{10,11... | collective-permute-start | bytes 3194888 | tf_op jit(solution)/shard_map/ppermute | solution.py:906
  117.9 47.5 %collective-permute-start.5 = (s32[5,8,208]{2,1,0:T(8,128)S(1)}, s32[5,8,208]{2,1,0:T(8,128)S(1)}, u32[]{:S(2)}, u32[]{:S(2)}) collective-permute-start(s32[5,8,208]{2,1,0:T(8,128)S(1)} %copy-done.8), channel_id=1, source_target_pairs={{0,3},{1,2},{2,1},{3,0},{4,7},{5,6},{6,5},{7,4},{8,11},{9,10},{10,... | collective-permute-start | bytes 99848 | tf_op jit(solution)/shard_map/ppermute | solution.py:906
  118.6 48.0 %collective-permute-start.4 = (s32[5,8,208]{2,1,0:T(8,128)S(1)}, s32[5,8,208]{2,1,0:T(8,128)S(1)}, u32[]{:S(2)}, u32[]{:S(2)}) collective-permute-start(s32[5,8,208]{2,1,0:T(8,128)S(1)} %copy-done.8), channel_id=1, source_target_pairs={{0,2},{1,3},{2,0},{3,1},{4,6},{5,7},{6,4},{7,5},{8,10},{9,11},{10,... | collective-permute-start | bytes 99848 | tf_op jit(solution)/shard_map/ppermute | solution.py:906
  165.4 1.8 collective-permute-start.3
  288.3 17.2 %collective-permute-start.10 = (bf16[2,320,512]{2,1,0:T(8,128)(2,1)}, bf16[2,320,512]{2,1,0:T(8,128)(2,1)S(1)}, u32[]{:S(2)}, u32[]{:S(2)}) collective-permute-start(bf16[2,320,512]{2,1,0:T(8,128)(2,1)} %slice_bitcast_fusion.5), channel_id=1, source_target_pairs={{0,3},{1,2},{2,1},{3,0},{4,7},{5,6},{6,5},{7,4},{8,11},{9,10},{10,... | collective-permute-start | bytes 1966088 | tf_op jit(solution)/shard_map/ppermute | solution.py:906
  289.2 30.5 %collective-permute-start.9 = (bf16[2,320,512]{2,1,0:T(8,128)(2,1)}, bf16[2,320,512]{2,1,0:T(8,128)(2,1)}, u32[]{:S(2)}, u32[]{:S(2)}) collective-permute-start(bf16[2,320,512]{2,1,0:T(8,128)(2,1)} %get-tuple-element.92), channel_id=1, source_target_pairs={{0,2},{1,3},{2,0},{3,1},{4,6},{5,7},{6,4},{7,5},{8,10},{9,11},{10,... | collective-permute-start | bytes 1966088 | tf_op jit(solution)/shard_map/ppermute | solution.py:906
  289.8 29.9 %collective-permute-start.8 = (bf16[2,320,512]{2,1,0:T(8,128)(2,1)}, bf16[2,320,512]{2,1,0:T(8,128)(2,1)}, u32[]{:S(2)}, u32[]{:S(2)}) collective-permute-start(bf16[2,320,512]{2,1,0:T(8,128)(2,1)} %get-tuple-element.93), channel_id=1, source_target_pairs={{0,1},{1,0},{2,3},{3,2},{4,5},{5,4},{6,7},{7,6},{8,9},{9,8},{10,11... | collective-permute-start | bytes 1966088 | tf_op jit(solution)/shard_map/ppermute | solution.py:906
  335.1 51.4 %collective-permute-start.13 = (bf16[5,208,512]{2,1,0:T(8,128)(2,1)}, bf16[5,208,512]{2,1,0:T(8,128)(2,1)S(1)}, u32[]{:S(2)}, u32[]{:S(2)}) collective-permute-start(bf16[5,208,512]{2,1,0:T(8,128)(2,1)} %get-tuple-element.39), channel_id=1, source_target_pairs={{0,3},{1,2},{2,1},{3,0},{4,7},{5,6},{6,5},{7,4},{8,11},{9,10},{10,... | collective-permute-start | bytes 3194888 | tf_op jit(solution)/shard_map/ppermute | solution.py:906
  336.4 50.2 %collective-permute-start.12 = (bf16[5,208,512]{2,1,0:T(8,128)(2,1)}, bf16[5,208,512]{2,1,0:T(8,128)(2,1)S(1)}, u32[]{:S(2)}, u32[]{:S(2)}) collective-permute-start(bf16[5,208,512]{2,1,0:T(8,128)(2,1)} %get-tuple-element.39), channel_id=1, source_target_pairs={{0,2},{1,3},{2,0},{3,1},{4,6},{5,7},{6,4},{7,5},{8,10},{9,11},{10,... | collective-permute-start | bytes 3194888 | tf_op jit(solution)/shard_map/ppermute | solution.py:906
  336.9 49.7 %collective-permute-start.11 = (bf16[5,208,512]{2,1,0:T(8,128)(2,1)}, bf16[5,208,512]{2,1,0:T(8,128)(2,1)S(1)}, u32[]{:S(2)}, u32[]{:S(2)}) collective-permute-start(bf16[5,208,512]{2,1,0:T(8,128)(2,1)} %get-tuple-element.39), channel_id=1, source_target_pairs={{0,1},{1,0},{2,3},{3,2},{4,5},{5,4},{6,7},{7,6},{8,9},{9,8},{10,11... | collective-permute-start | bytes 3194888 | tf_op jit(solution)/shard_map/ppermute | solution.py:906
  337.1 47.6 %collective-permute-start.16 = (f32[5,8,208]{2,1,0:T(8,128)S(1)}, f32[5,8,208]{2,1,0:T(8,128)S(1)}, u32[]{:S(2)}, u32[]{:S(2)}) collective-permute-start(f32[5,8,208]{2,1,0:T(8,128)S(1)} %copy-done.7), channel_id=1, source_target_pairs={{0,3},{1,2},{2,1},{3,0},{4,7},{5,6},{6,5},{7,4},{8,11},{9,10},{10,... | collective-permute-start | bytes 99848 | tf_op jit(solution)/shard_map/ppermute | solution.py:906
  338.5 47.3 %collective-permute-start.15 = (f32[5,8,208]{2,1,0:T(8,128)S(1)}, f32[5,8,208]{2,1,0:T(8,128)S(1)}, u32[]{:S(2)}, u32[]{:S(2)}) collective-permute-start(f32[5,8,208]{2,1,0:T(8,128)S(1)} %copy-done.7), channel_id=1, source_target_pairs={{0,2},{1,3},{2,0},{3,1},{4,6},{5,7},{6,4},{7,5},{8,10},{9,11},{10,... | collective-permute-start | bytes 99848 | tf_op jit(solution)/shard_map/ppermute | solution.py:906
  437.0 16.8 %collective-permute-start.19 = (bf16[2,320,512]{2,1,0:T(8,128)(2,1)}, bf16[2,320,512]{2,1,0:T(8,128)(2,1)S(1)}, u32[]{:S(2)}, u32[]{:S(2)}) collective-permute-start(bf16[2,320,512]{2,1,0:T(8,128)(2,1)} %slice_bitcast_fusion.4), channel_id=1, source_target_pairs={{0,3},{1,2},{2,1},{3,0},{4,7},{5,6},{6,5},{7,4},{8,11},{9,10},{10,... | collective-permute-start | bytes 1966088 | tf_op jit(solution)/shard_map/ppermute | solution.py:906
  438.5 30.0 %collective-permute-start.18 = (bf16[2,320,512]{2,1,0:T(8,128)(2,1)}, bf16[2,320,512]{2,1,0:T(8,128)(2,1)}, u32[]{:S(2)}, u32[]{:S(2)}) collective-permute-start(bf16[2,320,512]{2,1,0:T(8,128)(2,1)} %get-tuple-element.89), channel_id=1, source_target_pairs={{0,2},{1,3},{2,0},{3,1},{4,6},{5,7},{6,4},{7,5},{8,10},{9,11},{10,... | collective-permute-start | bytes 1966088 | tf_op jit(solution)/shard_map/ppermute | solution.py:906
  439.0 29.4 %collective-permute-start.17 = (bf16[2,320,512]{2,1,0:T(8,128)(2,1)}, bf16[2,320,512]{2,1,0:T(8,128)(2,1)}, u32[]{:S(2)}, u32[]{:S(2)}) collective-permute-start(bf16[2,320,512]{2,1,0:T(8,128)(2,1)} %get-tuple-element.90), channel_id=1, source_target_pairs={{0,1},{1,0},{2,3},{3,2},{4,5},{5,4},{6,7},{7,6},{8,9},{9,8},{10,11... | collective-permute-start | bytes 1966088 | tf_op jit(solution)/shard_map/ppermute | solution.py:906
  (13 other events, 196.0 us)
Sparse Core Ops, SparseCore 0:
  13.9 79.0 all-gather.7
  94.8 34.2 all-gather.13
  131.5 35.3 all-gather.9
  168.6 35.2 all-gather.15
  206.2 35.2 all-gather.11

commit v3 on v2

--- a/solution.py
+++ b/solution.py
@@ -389,31 +389,114 @@
     return values * cumulative, cumulative + values * density
 
 
+def plane_gather(blocks, sems, base, dp_at, ex_at, near):
+    half = blocks.shape[1] // 2
+    first, second = pl.ds(0, half), pl.ds(half, half)
+    own = [
+        send(blocks.at[dp_at], blocks.at[dp_at], sems, base + k - 1, (near[k], ex_at)) for k in (1, 2)
+    ]
+    passed = [
+        send(blocks.at[near[1], first], blocks.at[near[1], first], sems, base + 2, (near[2], ex_at)),
+        send(blocks.at[near[2], second], blocks.at[near[2], second], sems, base + 3, (near[1], ex_at)),
+    ]
+    return own, passed
+
+
+def group_copies(images, step, buf, dest, tsem, lsem, dp_at, ex_at):
+    mate, across = flip(ex_at, 1), flip(ex_at, 2)
+    keep = pltpu.make_async_copy(buf.at[step], dest.at[0, step], lsem.at[step])
+    to_mate = send(buf.at[step], dest.at[1, step], tsem, step, (dp_at, mate))
+    to_chip = send(buf.at[step], dest.at[2, step], tsem, images + step, (dp_at, across))
+    onward = send(dest.at[2, step], dest.at[3, step], tsem, 2 * images + step, (dp_at, mate))
+    return keep, to_mate, to_chip, onward
+
+
 def forward_kernel(
-    real_rows,
-    experts,
-    tok_ref,
-    wqkv_ref,
-    wout_ref,
-    gain_ref,
-    router_ref,
-    router_t_ref,
-    cols_ref,
-    rows_ref,
-    qkv_ref,
-    probs_ref,
-    mixed_ref,
-    resid_ref,
-    act_ref,
-    gates_ref,
-    grow_ref,
+    images, real_rows, experts, tok_ref, qkvw_ref, outw_ref, extra_ref, cols_ref, rows_ref, codes_ref, win_ref, wex_ref,
+    qkv_ref, probs_ref, mixed_ref, resid_ref, gates_ref, dense_ref, ext_ref,
+    act_all, code_all, grow_all, win_all, wex_all, far_in,
+    dense, act_buf, grow_buf, d_send, d_recv, t_send, t_recv, r_send, r_recv, w_send, w_recv, local_sem,
 ):
+    step_at = pl.program_id(0)
+    dp_at, ex_at, near = place()
+    core, floor = lax.rem(ex_at, 2), ex_at // 2
+    dsem, tsem, rsem, wsem = (d_send, d_recv), (t_send, t_recv), (r_send, r_recv), (w_send, w_recv)
+    group_peers = [(dp_at, flip(ex_at, 1)), (dp_at, flip(ex_at, 2)), (dp_at, flip(flip(ex_at, 1), 2))]
+    floors = [floor, flip(floor, 1), flip(floor, 2), flip(flip(floor, 1), 2)]
+    columns = [dp_at] + near[1:]
+
+    codes_out = [send(codes_ref, code_all.at[k + 1], rsem, k, group_peers[k]) for k in range(3)]
+    grow_out = [send(grow_buf, grow_all.at[k + 1], rsem, 3 + k, group_peers[k]) for k in range(3)]
+    keeps = [
+        pltpu.make_async_copy(codes_ref, code_all.at[0], local_sem.at[images]),
+        pltpu.make_async_copy(win_ref, win_all.at[dp_at], local_sem.at[images + 1]),
+        pltpu.make_async_copy(wex_ref, wex_all.at[dp_at], local_sem.at[images + 2]),
+    ]
+    keep_grow = pltpu.make_async_copy(grow_buf, grow_all.at[0], local_sem.at[images + 3])
+    in_own, in_passed = plane_gather(win_all, wsem, 0, dp_at, ex_at, near)
+    ex_own, ex_passed = plane_gather(wex_all, wsem, 4, dp_at, ex_at, near)
+    to_far = send(win_ref, far_in, wsem, 8, (dp_at, flip(ex_at, 4)))
+    along_line = [
+        send(dense.at[dp_at, floor, core], dense.at[dp_at, floor, core], dsem, k - 1, (dp_at, 2 * floors[k] + core))
+        for k in (1, 2, 3)
+    ]
+    in_plane = [
+        [
+            send(
+                dense.at[dp_at, floors[k], core], dense.at[dp_at, floors[k], core], dsem, 3 + 3 * k + p - 1,
+                (near[p], ex_at),
+            )
+            for p in (1, 2, 3)
+        ]
+        for k in range(4)
+    ]
+    to_mate = [
+        send(dense.at[columns[p], :, core], dense.at[columns[p], :, core], dsem, 15 + p, group_peers[0])
+        for p in range(4)
+    ]
+
+    @pl.when(step_at == 0)
+    def _():
+        for copy in keeps:
+            copy.start()
+        width = outw_ref.shape[1]
+        dense[dp_at, floor, core, :, : 3 * width] = qkvw_ref[...]
+        dense[dp_at, floor, core, :, 3 * width : 4 * width] = outw_ref[...]
+        dense[dp_at, floor, core, :, 4 * width :] = extra_ref[...]
+        greet(
+            [(near[k], ex_at) for k in (1, 2, 3)]
+            + group_peers
+            + [(dp_at, flip(ex_at, 4)), (dp_at, flip(flip(ex_at, 2), 4))]
+        )
+        for copy in along_line + in_plane[0]:
+            copy.start()
+        for k in (1, 2, 3):
+            along_line[k - 1].wait_recv()
+            for copy in in_plane[k]:
+                copy.start()
+        to_mate[0].start()
+        for copy in codes_out:
+            copy.start()
+        for p in (1, 2, 3):
+            for k in range(4):
+                in_plane[k][p - 1].wait_recv()
+            to_mate[p].start()
+        for copy in keeps:
+            copy.wait()
+        for copy in in_own + ex_own + [to_far]:
+            copy.start()
+        for copy in to_mate:
+            copy.wait_recv()
+        full = dense[...].reshape(dense_ref.shape)
+        dense_ref[...] = full
+        ext_ref[...] = full[:, 4 * width :].astype(F32).T
+
     inputs = tok_ref[...].astype(F32)
     normed, _ = normalize(inputs)
-    act_one = (normed * gain_ref[0:1, :]).astype(BF16)
-    qkv = dot(act_one, wqkv_ref[...]).astype(BF16)
+    width = inputs.shape[1]
+    act_one = (normed * ext_ref[experts : experts + 1, :]).astype(BF16)
+    qkv = dot(act_one, dense_ref[:, : 3 * width]).astype(BF16)
     qkv_ref[...] = qkv
-    width = inputs.shape[1]
     rows = inputs.shape[0]
     low_half = lane_ids((1, 128)) < 64
     key_bias = jnp.where(lane_ids((1, rows)) < real_rows, 0.0, -1e30)
@@ -435,26 +518,78 @@
         parts.append(jnp.where(low_half, outs[0], outs[1]).astype(BF16))
     mixed = jnp.concatenate(parts, axis=1)
     mixed_ref[...] = mixed
-    resid = inputs + dot(mixed, wout_ref[...])
+    resid = inputs + dot(mixed, dense_ref[:, 3 * width : 4 * width])
     resid_ref[...] = resid
     normed_two, _ = normalize(resid)
-    act_two = (normed_two * gain_ref[1:2, :]).astype(BF16)
-    act_ref[...] = act_two
+    act_two = (normed_two * ext_ref[experts + 1 : experts + 2, :]).astype(BF16)
+    act_buf[step_at] = act_two
     lanes = lane_ids((1, 128))
-    logits = jnp.where(lanes < experts, dot(act_two, router_ref[...]), -1e30)
+    logits = jnp.where(lanes < experts, dot(act_two, dense_ref[:, 4 * width :]), -1e30)
     exped = jnp.exp(logits - jnp.max(logits, axis=-1, keepdims=True))
     gates = exped / jnp.sum(exped, axis=-1, keepdims=True)
     cols = cols_ref[...]
     first = jnp.sum(jnp.where(lanes == cols[:, 2:3], gates, 0.0), axis=-1, keepdims=True)
     second = jnp.sum(jnp.where(lanes == cols[:, 3:4], gates, 0.0), axis=-1, keepdims=True)
     gates_ref[...] = jnp.where(lanes == experts, first, jnp.where(lanes == experts + 1, second, gates))
-    logits_t = contract_cols(router_t_ref[...], act_two)[:experts]
+    logits_t = contract_cols(ext_ref[0:16, :].astype(BF16), act_two)[:experts]
     exped_t = jnp.exp(logits_t - jnp.max(logits_t, axis=0, keepdims=True))
     gates_t = exped_t / jnp.sum(exped_t, axis=0, keepdims=True)
     ids_t = row_ids(gates_t.shape)
     first_t = jnp.sum(jnp.where(ids_t == rows_ref[2:3, :], gates_t, 0.0), axis=0, keepdims=True)
     second_t = jnp.sum(jnp.where(ids_t == rows_ref[3:4, :], gates_t, 0.0), axis=0, keepdims=True)
-    grow_ref[...] = jnp.where(row_ids((8, rows)) == 0, first_t, second_t)
+    grow_buf[step_at] = jnp.where(row_ids((8, rows)) == 0, first_t, second_t)
+
+    for step in range(images):
+        keep, mate_copy, chip_copy, _ = group_copies(images, step, act_buf, act_all, tsem, local_sem, dp_at, ex_at)
+
+        @pl.when(step_at == step)
+        def _():
+            keep.start()
+            mate_copy.start()
+            chip_copy.start()
+
+    def pass_on(step):
+        _, _, chip_copy, onward = group_copies(images, step, act_buf, act_all, tsem, local_sem, dp_at, ex_at)
+        chip_copy.wait_recv()
+        onward.start()
+
+    for step in range(images - 2):
+
+        @pl.when(step_at == step + 2)
+        def _():
+            pass_on(step)
+
+    @pl.when(step_at == images - 2)
+    def _():
+        in_own[0].wait_recv()
+        in_passed[0].start()
+        in_own[1].wait_recv()
+        in_passed[1].start()
+
+    @pl.when(step_at == images - 1)
+    def _():
+        keep_grow.start()
+        for copy in grow_out:
+            copy.start()
+        ex_own[0].wait_recv()
+        ex_passed[0].start()
+        ex_own[1].wait_recv()
+        ex_passed[1].start()
+        for step in (images - 2, images - 1):
+            pass_on(step)
+        for step in range(images):
+            keep, mate_copy, chip_copy, onward = group_copies(
+                images, step, act_buf, act_all, tsem, local_sem, dp_at, ex_at
+            )
+            keep.wait()
+            mate_copy.wait()
+            chip_copy.wait_send()
+            onward.wait()
+        keep_grow.wait()
+        for copy in codes_out + grow_out + in_passed + ex_passed + [to_far]:
+            copy.wait()
+        for copy in along_line + to_mate + in_own + ex_own + [c for line in in_plane for c in line]:
+            copy.wait_send()
 
 
 def hot_rows(codes, start, count):
@@ -462,12 +597,65 @@
     return (slots == codes[0:1, :]) | (slots == codes[1:2, :])
 
 
+def return_copies(buf, back, q, half, sems, local, dp_at, ex_at):
+    peers = [None, (dp_at, flip(ex_at, 1)), (dp_at, flip(ex_at, 2)), (dp_at, flip(flip(ex_at, 1), 2))]
+    copies = []
+    for k in (2 * half, 2 * half + 1):
+        if k == 0:
+            copies.append(pltpu.make_async_copy(buf.at[q, 0], back.at[q, 0], local.at[q]))
+        else:
+            copies.append(send(buf.at[q, k], back.at[q, k], sems, 4 * q + k, peers[k]))
+    return copies
+
+
 def expert_forward_kernel(
-    cap, group, act_ref, codes_ref, win_ref, wout_ref, rows_out_ref, hidden_ref, slope_ref, out_ref
+    cap, group, act_ref, codes_ref, win_own, wex_own, win_far, wex_mine,
+    rows_out_ref, hidden_ref, slope_ref, back_ref, win_other, wex_other,
+    win_buf, wex_buf, out_buf, y_send, y_recv, w_send, w_recv, local_sem,
 ):
-    which, half = pl.program_id(0), pl.program_id(1)
+    which, half_step = pl.program_id(0), pl.program_id(1)
+    half = 1 - half_step
+    dp_at, ex_at, near = place()
+    ysem, wsem = (y_send, y_recv), (w_send, w_recv)
+    keep_in = pltpu.make_async_copy(win_far, win_other.at[dp_at], local_sem.at[2])
+    loads = [
+        pltpu.make_async_copy(win_own, win_buf.at[0], local_sem.at[3]),
+        pltpu.make_async_copy(wex_own, wex_buf.at[0], local_sem.at[4]),
+        pltpu.make_async_copy(win_other, win_buf.at[1], local_sem.at[5]),
+        pltpu.make_async_copy(wex_other, wex_buf.at[1], local_sem.at[6]),
+    ]
+    in_own, in_passed = plane_gather(win_other, wsem, 0, dp_at, ex_at, near)
+    ex_own, ex_passed = plane_gather(wex_other, wsem, 4, dp_at, ex_at, near)
+    to_far = send(wex_mine, wex_other.at[dp_at], wsem, 8, (dp_at, flip(ex_at, 4)))
+
+    def at(q, step):
+        return pl.when((which == q) & (half_step == step))
+
+    @at(0, 0)
+    def _():
+        keep_in.start()
+        loads[0].start()
+        loads[1].start()
+        greet(
+            [(near[k], ex_at) for k in (1, 2)]
+            + [(dp_at, flip(ex_at, 1)), (dp_at, flip(ex_at, 2)), (dp_at, flip(flip(ex_at, 1), 2)), (dp_at, flip(ex_at, 4))]
+        )
+        to_far.start()
+        keep_in.wait()
+        for copy in in_own:
+            copy.start()
+        loads[0].wait()
+        loads[1].wait()
+
+    @at(1, 0)
+    def _():
+        for copy in in_passed:
+            copy.wait_recv()
+        loads[2].start()
+        loads[2].wait()
+
     blocks, images = act_ref.shape[0], act_ref.shape[1]
-    hidden_width = win_ref.shape[1]
+    parts, width, hidden_width = win_buf.shape[1], act_ref.shape[3], win_buf.shape[3]
     pieces = []
     for block in range(blocks):
         start = (which * group + half * blocks + block) * cap
@@ -479,16 +667,59 @@
         pieces.append(total.astype(BF16))
     rows_in = jnp.concatenate(pieces, axis=0)
     rows_out_ref[...] = rows_in.reshape(rows_out_ref.shape)
-    step = 512
+    step = hidden_width // parts
+    for part in range(parts):
+        cut = slice(part * step, (part + 1) * step)
+        act, slope = gelu_pair(dot(rows_in, win_buf[which, :, :, cut].reshape(width, step)))
+        hidden_ref[:, :, cut] = act.astype(BF16).reshape(blocks, cap, step)
+        slope_ref[:, :, cut] = slope.astype(BF16).reshape(blocks, cap, step)
+
+    @at(1, 0)
+    def _():
+        for own, passed in zip(ex_own, ex_passed):
+            own.wait_recv()
+            passed.start()
+        for copy in ex_passed:
+            copy.wait_recv()
+        loads[3].start()
+        loads[3].wait()
+
     result = None
-    for offset in range(0, hidden_width, step):
-        act, slope = gelu_pair(dot(rows_in, win_ref[:, offset : offset + step]))
-        act = act.astype(BF16)
-        hidden_ref[:, :, offset : offset + step] = act.reshape(blocks, cap, step)
-        slope_ref[:, :, offset : offset + step] = slope.astype(BF16).reshape(blocks, cap, step)
-        term = dot(act, wout_ref[offset : offset + step, :])
+    for part in range(parts):
+        cut = slice(part * step, (part + 1) * step)
+        term = dot(hidden_ref[:, :, cut].reshape(blocks * cap, step), wex_buf[which, part])
         result = term if result is None else result + term
-    out_ref[...] = result.astype(BF16).reshape(out_ref.shape)
+    out_buf[which, pl.ds(half * blocks, blocks)] = result.astype(BF16).reshape(blocks, cap, width)
+
+    for q in range(2):
+        for step_at in range(2):
+
+            @at(q, step_at)
+            def _():
+                for copy in return_copies(out_buf, back_ref, q, 1 - step_at, ysem, local_sem, dp_at, ex_at):
+                    copy.start()
+
+    @at(0, 0)
+    def _():
+        in_own[0].wait_recv()
+        in_passed[0].start()
+        in_own[1].wait_recv()
+        in_passed[1].start()
+
+    @at(0, 1)
+    def _():
+        to_far.wait_recv()
+        for copy in ex_own:
+            copy.start()
+
+    @at(1, 1)
+    def _():
+        for q in range(2):
+            for step_at in range(2):
+                for copy in return_copies(out_buf, back_ref, q, 1 - step_at, ysem, local_sem, dp_at, ex_at):
+                    copy.wait()
+        for copy in in_own + in_passed + ex_own + ex_passed + [to_far]:
+            copy.wait_send()
 
 
 def hot_cols(codes, count):
@@ -496,9 +727,18 @@
 
 
 def combine_kernel(
-    experts, scale_ref, resid_ref, back_ref, cols_ref, gates_ref, target_ref, valid_ref,
-    out_ref, dout_ref, dlow_ref, dlogit_ref, loss_ref,
+    images, total_tokens, shard, experts, ext_ref, resid_ref, back_ref, cols_ref, gates_ref, target_ref, valid_ref,
+    out_ref, dout_ref, dlogit_ref, loss_ref, dlow_all,
+    dlow_buf, t_send, t_recv, local_sem,
 ):
+    step_at = pl.program_id(0)
+    dp_at, ex_at, _ = place()
+    tsem = (t_send, t_recv)
+
+    @pl.when(step_at == 0)
+    def _():
+        greet([(dp_at, flip(ex_at, 1)), (dp_at, flip(ex_at, 2))])
+
     count = back_ref.shape[0]
     cols = cols_ref[...]
     rows = cols.shape[0]
@@ -523,10 +763,12 @@
     def _():
         loss_ref[...] = jnp.zeros_like(loss_ref)
 
-    loss_ref[...] += jnp.sum(square)
-    dout = (scale_ref[0, 0] * valid[:, 0:1]) * residue
+    counts = jnp.sum(ext_ref[experts + 2 : experts + 4, :], axis=-1, keepdims=True)
+    count_all = (counts[0:1] * 128.0 + counts[1:2]) / shard
+    loss_ref[...] += jnp.sum(square) / count_all
+    dout = (total_tokens / count_all * valid[:, 0:1]) * residue
     dout_ref[...] = dout
-    dlow_ref[...] = dout.astype(BF16)
+    dlow_buf[step_at] = dout.astype(BF16)
     lanes = lane_ids((1, 128))
     grad = jnp.where(
         lanes == cols[:, 2:3], jnp.sum(dout * from_first, axis=-1, keepdims=True), 0.0
@@ -534,14 +776,74 @@
     real = jnp.where(lanes < experts, gates, 0.0)
     dlogit_ref[...] = real * (grad - jnp.sum(real * grad, axis=-1, keepdims=True))
 
+    def copies(step):
+        return group_copies(images, step, dlow_buf, dlow_all, tsem, local_sem, dp_at, ex_at)
+
+    for step in range(images):
+
+        @pl.when(step_at == step)
+        def _():
+            for copy in copies(step)[:3]:
+                copy.start()
+            if step >= 2:
+                copies(step - 2)[2].wait_recv()
+                copies(step - 2)[3].start()
+
+    @pl.when(step_at == images - 1)
+    def _():
+        for step in (images - 2, images - 1):
+            copies(step)[2].wait_recv()
+            copies(step)[3].start()
+        for step in range(images):
+            keep, to_mate, to_chip, onward = copies(step)
+            keep.wait()
+            to_mate.wait()
+            to_chip.wait_send()
+            onward.wait()
+
 
 def expert_back_kernel(
-    cap, group, dlow_ref, codes_ref, grow_ref, rows_ref, hidden_ref, slope_ref, win_ref, wout_ref,
-    back_ref, gin_ref, gout_ref, acc_in, acc_out,
+    cap, group, dlow_ref, codes_ref, grow_ref, rows_ref, hidden_ref, slope_ref, win_own, wex_own, win_other, wex_other,
+    back_ref, gin_ref, gex_ref, got_in, got_ex,
+    win_buf, wex_buf, acc_in, acc_out, low_in, low_ex, out_buf, y_send, y_recv, w_send, w_recv, local_sem,
 ):
-    which, half = pl.program_id(0), pl.program_id(1)
+    which_step, half_step = pl.program_id(0), pl.program_id(1)
+    which, half = 1 - which_step, 1 - half_step
+    dp_at, ex_at, near = place()
+    ysem, wsem = (y_send, y_recv), (w_send, w_recv)
+    loads = [
+        pltpu.make_async_copy(win_own, win_buf.at[0], local_sem.at[3]),
+        pltpu.make_async_copy(wex_own, wex_buf.at[0], local_sem.at[4]),
+        pltpu.make_async_copy(win_other, win_buf.at[1], local_sem.at[5]),
+        pltpu.make_async_copy(wex_other, wex_buf.at[1], local_sem.at[6]),
+    ]
+    stores = [
+        pltpu.make_async_copy(low_in.at[0], gin_ref.at[0], local_sem.at[7]),
+        pltpu.make_async_copy(low_ex.at[0], gex_ref.at[0], local_sem.at[8]),
+        pltpu.make_async_copy(low_in.at[1], gin_ref.at[1], local_sem.at[9]),
+        pltpu.make_async_copy(low_ex.at[1], gex_ref.at[1], local_sem.at[10]),
+    ]
+    spread = []
+    for t, (grad, got, first) in enumerate(((low_in, got_in, 1), (low_ex, got_ex, 2))):
+        for s, owner in enumerate((near[first], near[3])):
+            spread.append(send(grad.at[1, owner], got.at[s], wsem, 2 * t + s, (near[first], ex_at)))
+
+    def at(q, step):
+        return pl.when((which == q) & (half_step == step))
+
+    @at(1, 0)
+    def _():
+        for copy in (loads[2], loads[3], loads[0], loads[1]):
+            copy.start()
+        greet(
+            [(near[k], ex_at) for k in (1, 2)]
+            + [(dp_at, flip(ex_at, 1)), (dp_at, flip(ex_at, 2)), (dp_at, flip(flip(ex_at, 1), 2))]
+        )
+        for copy in loads:
+            copy.wait()
+
     blocks, images = dlow_ref.shape[0], dlow_ref.shape[1]
-    hidden_width = win_ref.shape[1]
+    parts, width, hidden_width = win_buf.shape[1], dlow_ref.shape[3], win_buf.shape[3]
     pieces = []
     for block in range(blocks):
         start = (which * group + half * blocks + block) * cap
@@ -563,34 +865,59 @@
     grads = jnp.concatenate(pieces, axis=0)
     grads_t = grads.T
     rows_in_t = rows_ref[...].reshape(blocks * cap, -1).T
-    step = 512
+    step = hidden_width // parts
     result = None
     for offset in range(0, hidden_width, step):
         cut = slice(offset, offset + step)
         hidden = hidden_ref[:, :, cut].reshape(blocks * cap, step)
         slope = slope_ref[:, :, cut].reshape(blocks * cap, step).astype(F32)
-        dpre = (contract_cols(grads, wout_ref[cut, :]) * slope).astype(BF16)
+        dpre = (contract_cols(grads, wex_buf[which, offset // step]) * slope).astype(BF16)
         gin = dot(rows_in_t, dpre)
         gout = dot(grads_t, hidden)
-        term = contract_cols(dpre, win_ref[:, cut])
+        term = contract_cols(dpre, win_buf[which, :, :, cut].reshape(width, step))
         result = term if result is None else result + term
 
-        @pl.when(half == 0)
+        @pl.when(half_step == 0)
         def _():
             acc_in[:, cut] = gin
             acc_out[:, cut] = gout
 
-        @pl.when(half == 1)
+        @pl.when(half_step == 1)
         def _():
-            gin_ref[:, cut] = (acc_in[:, cut] + gin).astype(BF16)
-            gout_ref[offset // step] = (acc_out[:, cut] + gout).astype(BF16)
-
-    back_ref[...] = result.astype(BF16).reshape(back_ref.shape)
+            total_in = (acc_in[:, cut] + gin).astype(BF16)
+            low_in[which, :, :, cut] = total_in.reshape(parts, width // parts, step)
+            low_ex[which, offset // step] = (acc_out[:, cut] + gout).astype(BF16)
+
+    out_buf[which, pl.ds(half * blocks, blocks)] = result.astype(BF16).reshape(blocks, cap, width)
+
+    for q in range(2):
+        for step_at in range(2):
+
+            @at(q, step_at)
+            def _():
+                for copy in return_copies(out_buf, back_ref, q, 1 - step_at, ysem, local_sem, dp_at, ex_at):
+                    copy.start()
+
+    @at(1, 1)
+    def _():
+        for copy in spread + stores[2:]:
+            copy.start()
+
+    @at(0, 1)
+    def _():
+        for copy in stores[:2]:
+            copy.start()
+        for q in range(2):
+            for step_at in range(2):
+                for copy in return_copies(out_buf, back_ref, q, 1 - step_at, ysem, local_sem, dp_at, ex_at):
+                    copy.wait()
+        for copy in spread + stores:
+            copy.wait()
 
 
 def back_kernel(
-    images, tok_ref, wqkv_ref, wout_ref, gain_ref, router_t_ref, cols_ref, back_ref, dlogit_ref, resid_ref,
-    dout_ref, qkv_ref, probs_ref, mixed_ref, loss_ref, gin_ref, gex_ref,
+    images, experts, tok_ref, dense_w, ext_ref, cols_ref, back_ref, dlogit_ref, resid_ref,
+    dout_ref, qkv_ref, probs_ref, mixed_ref, loss_ref, gin_ref, gex_ref, got_in_ref, got_ex_ref,
     tgrad_ref, dense_ref, misc_ref, gin_out, gex_out,
     acc, acc_misc, part_in, part_ex, got_in, got_ex, sum_in, sum_ex, more_in, more_ex, far_in, far_ex, came_in, came_ex,
     low, mate, low_mate, plane, low_plane, line, misc_got, local_sem, w_send, w_recv, d_send, d_recv, m_send, m_recv,
@@ -613,6 +940,8 @@
                     copies.append(
                         pltpu.make_async_copy(grad.at[q, owner], part.at[q, s], local_sem.at[4 * t + 2 * q + s])
                     )
+        copies.append(pltpu.make_async_copy(got_in_ref, got_in.at[1], local_sem.at[8]))
+        copies.append(pltpu.make_async_copy(got_ex_ref, got_ex.at[1], local_sem.at[9]))
         return copies
 
     def first_round(q):
@@ -638,8 +967,6 @@
         ]
 
     def add_first(q):
-        for copy in first_round(q):
-            copy.wait_recv()
         for _, part, got, passed, _, _, _, _, _, _ in tensors:
             passed[q] = (part[q, 1].astype(F32) + got[q, 1].astype(F32)).astype(BF16)
         for copy in second_round(q):
@@ -651,13 +978,16 @@
 
     @pl.when(step_at == 0)
     def _():
+        for copy in local_copies():
+            copy.start()
         greet(
             [(near[k], ex_at) for k in (1, 2, 3)]
             + [(dp_at, flip(ex_at, bit)) for bit in (1, 2, 4)]
             + [(dp_at, flip(flip(ex_at, 2), 4))]
         )
-        for copy in first_round(1) + first_round(0) + local_copies():
-            copy.start()
+        for copy in local_copies():
+            copy.wait()
+        add_first(1)
 
     count = back_ref.shape[0]
     cols = cols_ref[...]
@@ -665,12 +995,13 @@
     dlogits = dlogit_ref[...]
     dact = dot(hot.astype(BF16), back_ref[...])
     dlogits_high = dlogits.astype(BF16)
+    router_t = ext_ref[...].astype(BF16)
     dlogits_low = (dlogits - dlogits_high.astype(F32)).astype(BF16)
-    dact = dact + dot(dlogits_high, router_t_ref[...]) + dot(dlogits_low, router_t_ref[...])
+    dact = dact + dot(dlogits_high, router_t) + dot(dlogits_low, router_t)
 
     resid = resid_ref[...]
     normed_two, inverse_two = normalize(resid)
-    gain_two = gain_ref[1:2, :]
+    gain_two = ext_ref[experts + 1 : experts + 2, :]
     act_two = (normed_two * gain_two).astype(BF16)
     grouter = contract_rows(dlogits_high, act_two) + contract_rows(dlogits_low, act_two)
 
@@ -689,9 +1020,9 @@
     branch = dresid.astype(BF16)
     mixed = mixed_ref[...]
     gout = contract_rows(mixed, branch)
-    dmixed = contract_cols(branch, wout_ref[...]).astype(BF16)
+    width = branch.shape[1]
+    dmixed = contract_cols(branch, dense_w[:, 3 * width : 4 * width]).astype(BF16)
     qkv = qkv_ref[...]
-    width = dmixed.shape[1]
     low_half = lane_ids((1, 128)) < 64
     dqs, dks, dvs = [], [], []
     for pair in range(width // 128):
@@ -722,10 +1053,10 @@
     dqkv = jnp.concatenate(dqs + dks + dvs, axis=1)
     inputs = tok_ref[...].astype(F32)
     normed_one, inverse_one = normalize(inputs)
-    gain_one = gain_ref[0:1, :]
+    gain_one = ext_ref[experts : experts + 1, :]
     act_one = (normed_one * gain_one).astype(BF16)
     gqkv = contract_rows(act_one, dqkv)
-    dact_one = contract_cols(dqkv, wqkv_ref[...])
+    dact_one = contract_cols(dqkv, dense_w[:, : 3 * width])
     grad_one, ggain_one = norm_back(dact_one, normed_one, inverse_one, gain_one)
     tgrad_ref[...] = dresid + grad_one
     ids = row_ids((8, width))
@@ -735,8 +1066,6 @@
 
     @pl.when(step_at == 0)
     def _():
-        for copy in local_copies():
-            copy.wait()
         acc[:, : 3 * width] = gqkv
         acc[:, 3 * width :] = gout
         loss_row = jnp.where(row_ids((8, 128)) == 2, loss_ref[...], 0.0)
@@ -750,9 +1079,14 @@
         acc[:, 3 * width :] += gout
         acc_misc[...] += gmisc
 
-    @pl.when(step_at == images - 2)
-    def _():
-        add_first(1)
+    @pl.when(step_at == 1)
+    def _():
+        for copy in second_round(1):
+            copy.wait_recv()
+        for tensor in tensors:
+            tensor[5][...] = total_of(tensor, 1).astype(BF16)
+        for copy in far_round() + first_round(0):
+            copy.start()
 
     @pl.when(step_at == images - 1)
     def _():
@@ -766,14 +1100,6 @@
         ]
         misc = [send(acc_misc.at[...] if k == 0 else misc_got.at[5 + k - 1], misc_got.at[k], msem, k, misc_peers[k]) for k in range(5)]
         misc[0].start()
-        add_first(0)
-
-        for copy in second_round(1):
-            copy.wait_recv()
-        for tensor in tensors:
-            tensor[5][...] = total_of(tensor, 1).astype(BF16)
-        for copy in far_round():
-            copy.start()
 
         def misc_step(k):
             misc[k].wait_recv()
@@ -782,6 +1108,9 @@
             if k < 4:
                 misc[k + 1].start()
 
+        for copy in first_round(0):
+            copy.wait_recv()
+        add_first(0)
         to_mate.wait_recv()
         low_mate[...] = (low[:, :, core].astype(F32) + mate[...].astype(F32)).astype(BF16)
         to_plane = [send(low_mate.at[near[k]], plane.at[k - 1], dsem, k, (near[k], ex_at)) for k in (1, 2, 3)]
@@ -818,7 +1147,7 @@
             copy.wait_recv()
         for tensor in tensors:
             tensor[7][...] = total_of(tensor, 0) + tensor[6][...].astype(F32)
-        for copy in [to_mate] + misc + to_plane + to_line + first_round(0) + first_round(1):
+        for copy in [to_mate] + misc + to_plane + to_line + first_round(0):
             copy.wait_send()
         for copy in second_round(0) + second_round(1) + far_round():
             copy.wait_send()
@@ -867,44 +1196,20 @@
     count_high = jnp.floor(my_count / 128.0)
     count_low = my_count - 128.0 * count_high
     shard = qkv_weight.shape[0]
-    extra = jnp.concatenate(
+    small = jnp.concatenate(
         [
             router_weight,
             ln1_gain[:, None],
             ln2_gain[:, None],
             jnp.broadcast_to(count_high.astype(BF16), (shard, 1)),
             jnp.broadcast_to(count_low.astype(BF16), (shard, 1)),
-            jnp.zeros((shard, 128 - experts - 4), BF16),
         ],
         axis=1,
     )
-    dense = lax.all_gather(
-        jnp.concatenate([qkv_weight, out_weight, extra], axis=1), axes, axis=0, tiled=True
-    )
-    qkv_full = dense[:, : 3 * width]
-    out_full = dense[:, 3 * width : 4 * width]
-    extra_full = dense[:, 4 * width :]
-    router_full = jnp.where(lane_ids((1, 128)) < experts, extra_full, 0)
-    extra_t = extra_full.T
-    router_t = jnp.where(row_ids((128, 1)) < experts, extra_t, 0)
-    gains = extra_t[experts : experts + 2].astype(F32)
-    counts = extra_full[::shard].astype(F32)
-    valid_count = jnp.sum(counts[:, experts + 2] * 128.0 + counts[:, experts + 3])
-    scale = (total_tokens / valid_count).reshape(1, 1)
-
-    far = [(i, i ^ group) for i in range(experts)]
-    w_in = [expert_in[0]]
-    w_out = [expert_out[0]]
-    w_in.append(lax.ppermute(w_in[0], "expert", far))
-    w_out.append(lax.ppermute(w_out[0], "expert", far))
-    win_full = jnp.stack([lax.all_gather(w, "dp", axis=0, tiled=True) for w in w_in])
-    wout_full = jnp.stack([lax.all_gather(w, "dp", axis=0, tiled=True) for w in w_out])
-
-    def exchange(blocks):
-        out = [blocks[0]]
-        for k in range(1, group):
-            out.append(lax.ppermute(blocks[k], "expert", [(i, i ^ k) for i in range(experts)]))
-        return out
+    extra = jnp.pad(small, ((0, 0), (0, 128 - experts - 4)))
+    floors = experts // 2
+    in_part, ex_part = (width // dp, hidden_width), (hidden_width // dp, width)
+    any_space = pl.BlockSpec(memory_space=pl.ANY)
 
     code = jnp.where(slot_ids < capacity, (routes ^ me) * cap + slot_ids, -1)
     cols = pad_rows(jnp.concatenate([code, routes], axis=1), -1)
@@ -915,137 +1220,152 @@
     valid_p = pad_rows(jnp.broadcast_to(valid_f[:, None], (tok_rows, 8)))
 
     gate_lanes = 128
-    qkv_p, probs, mixed, resid, act_two, gates, grow = pl.pallas_call(
-        lambda *refs: forward_kernel(real_rows, experts, *refs),
+    dense_lanes = 4 * width + 128
+    (
+        qkv_p, probs, mixed, resid, gates, dense_full, ext, act_all, code_all, grow_all, win_own, wex_own, win_far,
+    ) = pl.pallas_call(
+        lambda *refs: forward_kernel(images, real_rows, experts, *refs),
         grid=(images,),
         in_specs=[
-            per_image(rows, width), whole((width, 3 * width)), whole((width, width)), whole((2, width)),
-            whole((width, 128)), whole((128, width)), per_image(rows, 8), per_image(8, rows),
+            per_image(rows, width), whole((shard, 3 * width)), whole((shard, width)), whole((shard, 128)),
+            per_image(rows, 8), per_image(8, rows), any_space, any_space, any_space,
         ],
         out_specs=[
             per_image(rows, 3 * width), per_image(HEADS, rows, rows), per_image(rows, width),
-            per_image(rows, width), per_image(rows, width), per_image(rows, gate_lanes), per_image(8, rows),
+            per_image(rows, width), per_image(rows, gate_lanes), whole((width, dense_lanes)), whole((128, width)),
+            *[any_space] * 6,
         ],
         out_shape=[
             shape((images, rows, 3 * width), BF16), shape((images, HEADS, rows, rows), BF16),
             shape((images, rows, width), BF16), shape((images, rows, width), F32),
-            shape((images, rows, width), BF16), shape((images, rows, gate_lanes), F32),
-            shape((images, 8, rows), F32),
-        ],
-        compiler_params=params(),
+            shape((images, rows, gate_lanes), F32), shape((width, dense_lanes), BF16), shape((128, width), F32),
+            shape((group, images, rows, width), BF16), shape((group, images, 8, rows), jnp.int32),
+            shape((group, images, 8, rows), F32), shape((dp, *in_part), BF16), shape((dp, *ex_part), BF16),
+            shape(in_part, BF16),
+        ],
+        scratch_shapes=[
+            pltpu.VMEM((dp, floors, 2, shard, dense_lanes), BF16), pltpu.VMEM((images, rows, width), BF16),
+            pltpu.VMEM((images, 8, rows), F32),
+            *sem_pairs(19), *sem_pairs(3 * images), *sem_pairs(6), *sem_pairs(9),
+            pltpu.SemaphoreType.DMA((images + 4,)),
+        ],
+        compiler_params=pltpu.CompilerParams(
+            vmem_limit_bytes=56 * MB, collective_id=2, has_side_effects=True
+        ),
         cost_estimate=pl.CostEstimate(flops=int(5e9), bytes_accessed=int(2e7), transcendentals=0),
         name="attention_forward",
-    )(tok_p, qkv_full, out_full, gains, router_full, router_t, cols, row_codes)
-
-    act_all = jnp.stack(exchange([act_two] * group))
-    code_all = jnp.stack(exchange([row_codes] * group))
+    )(tok_p, qkv_weight, out_weight, extra, cols, row_codes, row_codes, expert_in[0], expert_out[0])
 
     half_blocks = group // 2
     def by_half(*dims):
-        return pl.BlockSpec((half_blocks,) + dims, lambda q, h: (h,) + (0,) * len(dims))
-    def by_expert(*dims):
-        return pl.BlockSpec((None,) + dims, lambda q, h: (q,) + (0,) * len(dims))
-    def by_both(*dims):
-        return pl.BlockSpec((None, half_blocks) + dims, lambda q, h: (q, h) + (0,) * len(dims))
-
-    rows_in, hidden, slope, produced = pl.pallas_call(
+        return pl.BlockSpec((half_blocks,) + dims, lambda q, h: (1 - h,) + (0,) * len(dims))
+
+    def by_both(*dims, last_first=False):
+        if last_first:
+            return pl.BlockSpec((None, half_blocks) + dims, lambda q, h: (1 - q, 1 - h) + (0,) * len(dims))
+        return pl.BlockSpec((None, half_blocks) + dims, lambda q, h: (q, 1 - h) + (0,) * len(dims))
+
+    rows_in, hidden, slope, returned, win_other, wex_other = pl.pallas_call(
         lambda *refs: expert_forward_kernel(cap, group, *refs),
         grid=(2, 2),
-        in_specs=[
-            by_half(images, rows, width), by_half(images, 8, rows), by_expert(width, hidden_width),
-            by_expert(hidden_width, width),
-        ],
-        out_specs=[by_both(cap, width), by_both(cap, hidden_width), by_both(cap, hidden_width), by_both(cap, width)],
+        in_specs=[by_half(images, rows, width), by_half(images, 8, rows), *[any_space] * 4],
+        out_specs=[by_both(cap, width), by_both(cap, hidden_width), by_both(cap, hidden_width), *[any_space] * 3],
         out_shape=[
             shape((2, group, cap, width), BF16), shape((2, group, cap, hidden_width), BF16),
             shape((2, group, cap, hidden_width), BF16), shape((2, group, cap, width), BF16),
-        ],
-        compiler_params=params(),
+            shape((dp, *in_part), BF16), shape((dp, *ex_part), BF16),
+        ],
+        scratch_shapes=[
+            pltpu.VMEM((2, dp, *in_part), BF16), pltpu.VMEM((2, dp, *ex_part), BF16),
+            pltpu.VMEM((2, group, cap, width), BF16), *sem_pairs(8), *sem_pairs(9), pltpu.SemaphoreType.DMA((7,)),
+        ],
+        compiler_params=pltpu.CompilerParams(
+            vmem_limit_bytes=58 * MB, collective_id=3, has_side_effects=True
+        ),
         cost_estimate=pl.CostEstimate(flops=int(14e9), bytes_accessed=int(4e7), transcendentals=0),
         name="expert_forward",
-    )(act_all, code_all, win_full, wout_full)
-
-    def give_back(array):
-        came = exchange([array[:, k] for k in range(group)])
-        return jnp.stack(came, axis=1).reshape(2 * group * cap, width)
-
-    returned = give_back(produced)
-    block_out, dout, dlow, dlogits, loss_part = pl.pallas_call(
-        lambda *refs: combine_kernel(experts, *refs),
+    )(act_all, code_all, win_own, wex_own, win_far, expert_out[0])
+    returned = returned.reshape(2 * group * cap, width)
+
+    block_out, dout, dlogits, loss_part, dlow_all = pl.pallas_call(
+        lambda *refs: combine_kernel(images, total_tokens, shard, experts, *refs),
         grid=(images,),
         in_specs=[
-            pl.BlockSpec(memory_space=pltpu.SMEM), per_image(rows, width), whole((2 * group * cap, width)),
+            pl.BlockSpec((16, width), lambda i: (0, 0)), per_image(rows, width), whole((2 * group * cap, width)),
             per_image(rows, 8), per_image(rows, gate_lanes), per_image(rows, width), per_image(rows, 8),
         ],
         out_specs=[
-            per_image(rows, width), per_image(rows, width), per_image(rows, width), per_image(rows, gate_lanes),
-            whole((8, 128)),
+            per_image(rows, width), per_image(rows, width), per_image(rows, gate_lanes), whole((8, 128)), any_space,
         ],
         out_shape=[
             shape((images, rows, width), BF16), shape((images, rows, width), F32),
-            shape((images, rows, width), BF16), shape((images, rows, gate_lanes), F32), shape((8, 128), F32),
-        ],
-        compiler_params=params(),
+            shape((images, rows, gate_lanes), F32), shape((8, 128), F32), shape((group, images, rows, width), BF16),
+        ],
+        scratch_shapes=[
+            pltpu.VMEM((images, rows, width), BF16), *sem_pairs(3 * images), pltpu.SemaphoreType.DMA((images,)),
+        ],
+        compiler_params=pltpu.CompilerParams(
+            vmem_limit_bytes=56 * MB, collective_id=4, has_side_effects=True
+        ),
         cost_estimate=pl.CostEstimate(flops=int(5e9), bytes_accessed=int(1e7), transcendentals=0),
         name="combine_and_loss",
-    )(scale, resid, returned, cols, gates, target_p, valid_p)
-
-    dlow_all = jnp.stack(exchange([dlow] * group))
-    grow_all = jnp.stack(exchange([grow] * group))
-    drows, gin, gout_t = pl.pallas_call(
+    )(ext, resid, returned, cols, gates, target_p, valid_p)
+
+    flip_part = (width, hidden_width // dp)
+    drows, gin, gout_t, got_in, got_ex = pl.pallas_call(
         lambda *refs: expert_back_kernel(cap, group, *refs),
         grid=(2, 2),
         in_specs=[
             by_half(images, rows, width), by_half(images, 8, rows), by_half(images, 8, rows),
-            by_both(cap, width), by_both(cap, hidden_width), by_both(cap, hidden_width),
-            by_expert(width, hidden_width), by_expert(hidden_width, width),
-        ],
-        out_specs=[
-            by_both(cap, width), by_expert(width, hidden_width), by_expert(dp, width, hidden_width // dp),
-        ],
+            by_both(cap, width, last_first=True), by_both(cap, hidden_width, last_first=True),
+            by_both(cap, hidden_width, last_first=True), *[any_space] * 4,
+        ],
+        out_specs=[any_space] * 5,
         out_shape=[
-            shape((2, group, cap, width), BF16), shape((2, width, hidden_width), BF16),
-            shape((2, dp, width, hidden_width // dp), BF16),
-        ],
-        scratch_shapes=[pltpu.VMEM((width, hidden_width), F32), pltpu.VMEM((width, hidden_width), F32)],
-        compiler_params=params(),
+            shape((2, group, cap, width), BF16), shape((2, dp, *in_part), BF16), shape((2, dp, *flip_part), BF16),
+            shape((2, *in_part), BF16), shape((2, *flip_part), BF16),
+        ],
+        scratch_shapes=[
+            pltpu.VMEM((2, dp, *in_part), BF16), pltpu.VMEM((2, dp, *ex_part), BF16),
+            pltpu.VMEM((width, hidden_width), F32), pltpu.VMEM((width, hidden_width), F32),
+            pltpu.VMEM((2, dp, *in_part), BF16), pltpu.VMEM((2, dp, *flip_part), BF16),
+            pltpu.VMEM((2, group, cap, width), BF16), *sem_pairs(8), *sem_pairs(4), pltpu.SemaphoreType.DMA((11,)),
+        ],
+        compiler_params=pltpu.CompilerParams(
+            vmem_limit_bytes=60 * MB, collective_id=5, has_side_effects=True
+        ),
         cost_estimate=pl.CostEstimate(flops=int(24e9), bytes_accessed=int(4e7), transcendentals=0),
         name="expert_backward",
-    )(dlow_all, code_all, grow_all, rows_in, hidden, slope, win_full, wout_full)
-    grad_back = give_back(drows)
-
-    floors = experts // 2
-    in_part, ex_part = (width // dp, hidden_width), (width, hidden_width // dp)
-    any_space = pl.BlockSpec(memory_space=pl.ANY)
+    )(dlow_all, code_all, grow_all, rows_in, hidden, slope, win_own, wex_own, win_other, wex_other)
+    grad_back = drows.reshape(2 * group * cap, width)
 
     def vmem(*dims):
         return pltpu.VMEM(dims, BF16)
 
     tgrad, dense_grad, misc, gin_own, gex_own = pl.pallas_call(
-        lambda *refs: back_kernel(images, *refs),
+        lambda *refs: back_kernel(images, experts, *refs),
         grid=(images,),
         in_specs=[
-            per_image(rows, width), whole((width, 3 * width)), whole((width, width)), whole((2, width)),
-            whole((128, width)), per_image(rows, 8), whole((2 * group * cap, width)),
-            per_image(rows, gate_lanes), per_image(rows, width), per_image(rows, width),
+            per_image(rows, width), whole((width, dense_lanes)), whole((128, width)), per_image(rows, 8),
+            whole((2 * group * cap, width)), per_image(rows, gate_lanes), per_image(rows, width), per_image(rows, width),
             per_image(rows, 3 * width), per_image(HEADS, rows, rows), per_image(rows, width), whole((8, 128)),
-            any_space, any_space,
+            *[any_space] * 4,
         ],
         out_specs=[
-            per_image(rows, width), whole((shard, 4 * width)), whole((16, width)), whole(in_part), whole(ex_part),
+            per_image(rows, width), whole((shard, 4 * width)), whole((16, width)), whole(in_part), whole(flip_part),
         ],
         out_shape=[
             shape((images, rows, width), F32), shape((shard, 4 * width), F32), shape((16, width), F32),
-            shape(in_part, F32), shape(ex_part, F32),
+            shape(in_part, F32), shape(flip_part, F32),
         ],
         scratch_shapes=[
             pltpu.VMEM((width, 4 * width), F32), pltpu.VMEM((16, width), F32),
-            vmem(2, 2, *in_part), vmem(2, 2, *ex_part), vmem(2, 2, *in_part), vmem(2, 2, *ex_part),
-            vmem(2, *in_part), vmem(2, *ex_part), vmem(2, *in_part), vmem(2, *ex_part),
-            vmem(*in_part), vmem(*ex_part), vmem(*in_part), vmem(*ex_part),
+            vmem(2, 2, *in_part), vmem(2, 2, *flip_part), vmem(2, 2, *in_part), vmem(2, 2, *flip_part),
+            vmem(2, *in_part), vmem(2, *flip_part), vmem(2, *in_part), vmem(2, *flip_part),
+            vmem(*in_part), vmem(*flip_part), vmem(*in_part), vmem(*flip_part),
             vmem(dp, floors, 2, shard, 4 * width), vmem(dp, floors, shard, 4 * width), vmem(dp, floors, shard, 4 * width),
             vmem(3, floors, shard, 4 * width), vmem(floors, shard, 4 * width), vmem(3, shard, 4 * width),
-            pltpu.VMEM((10, 16, width), F32), pltpu.SemaphoreType.DMA((8,)),
+            pltpu.VMEM((10, 16, width), F32), pltpu.SemaphoreType.DMA((10,)),
             *sem_pairs(16), *sem_pairs(8), *sem_pairs(5),
         ],
         compiler_params=pltpu.CompilerParams(
@@ -1054,12 +1374,12 @@
         cost_estimate=pl.CostEstimate(flops=int(10e9), bytes_accessed=int(3e7), transcendentals=0),
         name="attention_backward",
     )(
-        tok_p, qkv_full, out_full, gains, router_t, cols, grad_back, dlogits, resid, dout, qkv_p, probs, mixed,
-        loss_part, gin.reshape(2, dp, *in_part), gout_t,
+        tok_p, dense_full, ext, cols, grad_back, dlogits, resid, dout, qkv_p, probs, mixed,
+        loss_part, gin, gout_t, got_in, got_ex,
     )
     flat = lax.axis_index("dp") * experts + me
     mine = lax.dynamic_slice_in_dim(misc, flat * shard, shard, axis=1)
-    loss_value = misc[10, 0] / valid_count
+    loss_value = misc[10, 0]
 
     def unpad(array):
         return array[:, :real_rows].reshape(tok_rows, width)

time: 616 us -> 352 us (0.57)
  waiting for transfers between devices: 285 us -> 0 us
  Pallas kernels: 224 us -> 328 us
  local copies, waits for them, and re-layouts: 46.2 us -> 21.5 us
  other arithmetic: 24.3 us -> 0.63 us
  starting transfers between devices: 17.4 us -> 0 us
  between operations: 18.5 us -> 2.16 us
    ppermute x20 -> x0, waiting for transfers between devices: 199 us -> none  [the longest x18 146 us: exchange(): lax.ppermute(blocks[k], 'expert', [(i, i ^ k) for i in range(experts)])]
    all_gather x5 -> x0, waiting for transfers between devices: 84.1 us -> none  [the longest x4 69.2 us: fast_shards(): lax.all_gather(w, 'dp', axis=0, tiled=True)]
    pallas_call x3, Pallas kernels: 148 us -> 196 us  [the longest x1 83 us: fast_shards(): pl.pallas_call(lambda *refs: back_kernel(images, experts, *refs), grid=(i...]
    pallas_call x1, Pallas kernels: 33.6 us -> 80.1 us  [fast_shards(): pl.pallas_call(lambda *refs: expert_forward_kernel(cap, group, *refs), gr...]
    another operation x8 -> x0, other arithmetic: 20.9 us -> none  [the longest x1 4.78 us: fast_shards(): jnp.stack([lax.all_gather(w, 'dp', axis=0, tiled=True) for w in w_out])]
    ppermute x20 -> x0, starting transfers between devices: 17.2 us -> none  [the longest x18 13.1 us: exchange(): lax.ppermute(blocks[k], 'expert', [(i, i ^ k) for i in range(experts)])]
    slice x7 -> x1, local copies, waits for them, and re-layouts: 12.5 us -> 1.19 us  [fast_shards(): loss_value = misc[10, 0]]
    pallas_call x1, Pallas kernels: 42.2 us -> 51.8 us  [fast_shards(): pl.pallas_call(lambda *refs: expert_back_kernel(cap, group, *refs), grid=...]
  transfers between devices with their start and end apart: 25 -> 0, of which waited for: 15 -> 0; matrix products, arithmetic and copies ran while one was open for 4% -> 0% of each run, Pallas kernels for 2% -> 0%
where the time goes in v3:
time: 352 us
  Pallas kernels  328 us (93%)
  local copies, waits for them, and re-layouts  21.5 us (6%)
    pallas_call x1, Pallas kernels, fast_shards(): pl.pallas_call(lambda *refs: back_kernel(images, experts, *refs), grid=(i...  83 us
    pallas_call x1, Pallas kernels, fast_shards(): pl.pallas_call(lambda *refs: forward_kernel(images, real_rows, experts, *...  80.1 us
    pallas_call x1, Pallas kernels, fast_shards(): pl.pallas_call(lambda *refs: expert_forward_kernel(cap, group, *refs), gr...  80.1 us
    pallas_call x1, Pallas kernels, fast_shards(): pl.pallas_call(lambda *refs: expert_back_kernel(cap, group, *refs), grid=...  51.8 us
    pallas_call x1, Pallas kernels, fast_shards(): pl.pallas_call(lambda *refs: combine_kernel(images, total_tokens, shard,...  32.9 us

profile of v3, /device:TPU:0, one launch (start us, length us, event | category | flops | bytes accessed | tf_op | source)
XLA Modules:
  0.0 352.1 jit_solution(15379335398570718857)
XLA Ops:
  0.7 1.5 reshape.48
  2.2 1.1 pad.27.refs_0_
  3.6 0.6 convert_reduce_fusion
  5.6 0.6 pad.28.refs_3_
  6.7 0.8 pad.30.refs_4_.refs_3_
  7.7 0.6 pad.31.clone.refs_5_.refs_6_
  8.4 80.1 %attention_forward.1 = (bf16[5,208,1536]{2,1,0:T(8,128)(2,1)}, bf16[5,8,208,208]{3,2,1,0:T(8,128)(2,1)}, bf16[5,208,512]{2,1,0:T(8,128)(2,1)}, f32[5,208,512]{2,...) custom-call(bf16[5,208,512]{2,1,0:T(8,128)(2,1)} %pad.27.refs_0_, ...), custom_call_target="tpu_custom_call" | custom-call | flops 5000000000 | bytes 20000000 | tf_op jit(solution)/shard_map/attention_forward/pallas_call | solution.py:1226
  88.5 80.1 %expert_forward.1 = (bf16[2,4,320,512]{3,2,1,0:T(8,128)(2,1)}, bf16[2,4,320,2048]{3,2,1,0:T(8,128)(2,1)}, bf16[2,4,320,2048]{3,2,1,0:T(8,128)(2,1)}, bf16[2,4,32...) custom-call(bf16[4,5,208,512]{3,2,1,0:T(8,128)(2,1)} %get-tuple-element.46.refs_0_, ...), custom_call_target="tpu_custom_call" | custom-call | flops 14000000000 | bytes 40000000 | tf_op jit(solution)/shard_map/expert_forward/pallas_call | solution.py:1268
  168.9 1.1 pad.32.refs_5_
  170.3 0.8 pad.33.refs_6_
  171.1 32.9 %combine_and_loss.1 = (bf16[5,208,512]{2,1,0:T(8,128)(2,1)}, f32[5,208,512]{2,1,0:T(8,128)}, f32[5,208,128]{2,1,0:T(8,128)}, f32[8,128]{1,0:T(8,128)}, bf16[4,5,208,512]{3,2,1,0:T(8,128)(2,1)}) custom-call(f32[128,512]{1,0:T(8,128)} %get-tuple-element.44.refs_0_.refs_2_, f32[5,208,512]{2,1,0:T(8,128)} %get-tuple-element.45.refs_1_.refs_6_, ...), custom_call_target="tpu_custom_call" | custom-call | flops 5000000000 | bytes 10000000 | tf_op jit(solution)/shard_map/combine_and_loss/pallas_call | solution.py:1290
  204.1 1.3 slice.24
  205.4 1.2 reshape.52
  206.6 51.8 %expert_backward.1 = (bf16[2,4,320,512]{3,2,1,0:T(8,128)(2,1)}, bf16[2,4,128,2048]{3,2,1,0:T(8,128)(2,1)}, bf16[2,4,512,512]{3,2,1,0:T(8,128)(2,1)}, bf16[2,128,2048]{2,1,0:T(8,128)(2,1)}, bf16[2,512,512]{2,1,0:T(8,128)(2,1)}) custom-call(bf16[4,5,208,512]{3,2,1,0:T(8,128)(2,1)} %get-tuple-element.55.refs_0_, s32[4,5,8,208]{3,2,1,0:T(8,128)} %get-tuple-element.47.refs_1_, ...), custom_call_target="tpu_custom_call" | custom-call | flops 24000000000 | bytes 40000000 | tf_op jit(solution)/shard_map/expert_backward/pallas_call | solution.py:1315
  258.4 83.0 %attention_backward.1 = (f32[5,208,512]{2,1,0:T(8,128)}, f32[16,2048]{1,0:T(8,128)}, f32[16,512]{1,0:T(8,128)}, f32[128,2048]{1,0:T(8,128)}, f32[512,512]{1,0:T(8,128)}) custom-call(bf16[5,208,512]{2,1,0:T(8,128)(2,1)} %pad.27.refs_0_, bf16[512,2176]{1,0:T(8,128)(2,1)} %get-tuple-element.54.refs_1_, f32[128,512]{1,0:T(8,128)} %get-tuple-element.44.refs_0_.refs_2_, ...), custom_call_target="tpu_custom_call" | custom-call | flops 10000000000 | bytes 30000000 | tf_op jit(solution)/shard_map/attention_backward/pallas_call | solution.py:1345
  341.4 1.2 slice.25
  342.6 1.7 slice.26
  344.3 1.5 reshape.54
  345.9 1.4 dynamic-slice_bitcast_fusion.1
  347.2 0.6 slice.28
  347.9 0.6 slice.29
  348.5 1.3 dynamic-slice_bitcast_fusion
  349.8 1.3 copy.35
  351.1 1.0 copy.38
  (36 shorter events, 1.6 us)
Async XLA Ops:
  0.6 2.7 copy-start.7
  0.7 2.8 copy-start.8
  0.7 2.8 copy-start.9
  0.7 2.9 copy-start.5
  0.7 5.6 %copy-start.4 = (s32[985,2]{0,1:T(2,128)S(1)}, s32[985,2]{0,1:T(2,128)}, u32[]{:S(2)}) copy-start(s32[985,2]{0,1:T(2,128)} %param.15) | copy-start | bytes 23644
  0.7 5.6 %copy-start.6 = (s32[985,2]{0,1:T(2,128)S(1)}, s32[985,2]{0,1:T(2,128)}, u32[]{:S(2)}) copy-start(s32[985,2]{0,1:T(2,128)} %param.16) | copy-start | bytes 23644
  88.5 80.1 %copy-start.2 = (bf16[985,512]{1,0:T(8,128)(2,1)S(1)}, bf16[985,512]{1,0:T(8,128)(2,1)}, u32[]{:S(2)}) copy-start(bf16[985,512]{1,0:T(8,128)(2,1)} %param.13) | copy-start | bytes 3025924
  344.3 2.9 copy-start.3
  344.3 5.5 %copy-start.1 = (f32[512,512]{1,0:T(8,128)S(1)}, f32[512,512]{1,0:T(8,128)}, u32[]{:S(2)}) copy-start(f32[512,512]{1,0:T(8,128)} %get-tuple-element.77) | copy-start | bytes 3145732
  345.9 5.3 %copy-start = (f32[128,2048]{1,0:T(8,128)S(1)}, f32[128,2048]{1,0:T(8,128)}, u32[]{:S(2)}) copy-start(f32[128,2048]{1,0:T(8,128)} %get-tuple-element.76) | copy-start | bytes 3145732

commit v4 on v3

--- a/solution.py
+++ b/solution.py
@@ -389,11 +389,11 @@
     return values * cumulative, cumulative + values * density
 
 
-def plane_gather(blocks, sems, base, dp_at, ex_at, near):
+def plane_gather(mine, blocks, sems, base, dp_at, ex_at, near):
     half = blocks.shape[1] // 2
     first, second = pl.ds(0, half), pl.ds(half, half)
     own = [
-        send(blocks.at[dp_at], blocks.at[dp_at], sems, base + k - 1, (near[k], ex_at)) for k in (1, 2)
+        send(mine, blocks.at[dp_at], sems, base + k - 1, (near[k], ex_at)) for k in (1, 2)
     ]
     passed = [
         send(blocks.at[near[1], first], blocks.at[near[1], first], sems, base + 2, (near[2], ex_at)),
@@ -433,8 +433,8 @@
         pltpu.make_async_copy(wex_ref, wex_all.at[dp_at], local_sem.at[images + 2]),
     ]
     keep_grow = pltpu.make_async_copy(grow_buf, grow_all.at[0], local_sem.at[images + 3])
-    in_own, in_passed = plane_gather(win_all, wsem, 0, dp_at, ex_at, near)
-    ex_own, ex_passed = plane_gather(wex_all, wsem, 4, dp_at, ex_at, near)
+    in_own, in_passed = plane_gather(win_ref, win_all, wsem, 0, dp_at, ex_at, near)
+    ex_own, ex_passed = plane_gather(wex_ref, wex_all, wsem, 4, dp_at, ex_at, near)
     to_far = send(win_ref, far_in, wsem, 8, (dp_at, flip(ex_at, 4)))
     along_line = [
         send(dense.at[dp_at, floor, core], dense.at[dp_at, floor, core], dsem, k - 1, (dp_at, 2 * floors[k] + core))
@@ -481,8 +481,6 @@
             for k in range(4):
                 in_plane[k][p - 1].wait_recv()
             to_mate[p].start()
-        for copy in keeps:
-            copy.wait()
         for copy in in_own + ex_own + [to_far]:
             copy.start()
         for copy in to_mate:
@@ -586,6 +584,8 @@
             chip_copy.wait_send()
             onward.wait()
         keep_grow.wait()
+        for copy in keeps:
+            copy.wait()
         for copy in codes_out + grow_out + in_passed + ex_passed + [to_far]:
             copy.wait()
         for copy in along_line + to_mate + in_own + ex_own + [c for line in in_plane for c in line]:
@@ -624,8 +624,8 @@
         pltpu.make_async_copy(win_other, win_buf.at[1], local_sem.at[5]),
         pltpu.make_async_copy(wex_other, wex_buf.at[1], local_sem.at[6]),
     ]
-    in_own, in_passed = plane_gather(win_other, wsem, 0, dp_at, ex_at, near)
-    ex_own, ex_passed = plane_gather(wex_other, wsem, 4, dp_at, ex_at, near)
+    in_own, in_passed = plane_gather(win_far, win_other, wsem, 0, dp_at, ex_at, near)
+    ex_own, ex_passed = plane_gather(wex_other.at[dp_at], wex_other, wsem, 4, dp_at, ex_at, near)
     to_far = send(wex_mine, wex_other.at[dp_at], wsem, 8, (dp_at, flip(ex_at, 4)))
 
     def at(q, step):
@@ -726,91 +726,20 @@
     return lane_ids((codes.shape[0], count)) == codes
 
 
-def combine_kernel(
-    images, total_tokens, shard, experts, ext_ref, resid_ref, back_ref, cols_ref, gates_ref, target_ref, valid_ref,
-    out_ref, dout_ref, dlogit_ref, loss_ref, dlow_all,
-    dlow_buf, t_send, t_recv, local_sem,
+def combine_back_kernel(
+    images, cap, group, total_tokens, shard, experts, ext_ref, resid_ref, came_ref, cols_ref, gates_ref, target_ref,
+    valid_ref, codes_ref, grow_ref, rows_ref, hidden_ref, slope_ref, win_own, wex_own, win_other, wex_other,
+    out_ref, dout_ref, dlogit_ref, loss_ref, back_ref, gin_ref, gex_ref, got_in, got_ex,
+    dlow, win_buf, wex_buf, acc_in, acc_out, low_in, low_ex, out_buf,
+    t_send, t_recv, y_send, y_recv, w_send, w_recv, local_sem,
 ):
     step_at = pl.program_id(0)
-    dp_at, ex_at, _ = place()
-    tsem = (t_send, t_recv)
-
-    @pl.when(step_at == 0)
-    def _():
-        greet([(dp_at, flip(ex_at, 1)), (dp_at, flip(ex_at, 2))])
-
-    count = back_ref.shape[0]
-    cols = cols_ref[...]
-    rows = cols.shape[0]
-    hot = jnp.concatenate(
-        [
-            jnp.where(hot_cols(cols[:, 0:1], count), 1.0, 0.0).astype(BF16),
-            jnp.where(hot_cols(cols[:, 1:2], count), 1.0, 0.0).astype(BF16),
-        ],
-        axis=0,
-    )
-    both = dot(hot, back_ref[...])
-    from_first, from_second = both[:rows], both[rows:]
-    gates = gates_ref[...]
-    first, second = gates[:, experts : experts + 1], gates[:, experts + 1 : experts + 2]
-    output = resid_ref[...] + first * from_first + second * from_second
-    out_ref[...] = output.astype(BF16)
-    residue = output - target_ref[...].astype(F32)
-    valid = valid_ref[...]
-    square = jnp.mean(residue * residue, axis=-1, keepdims=True) * valid[:, 0:1]
-
-    @pl.when(pl.program_id(0) == 0)
-    def _():
-        loss_ref[...] = jnp.zeros_like(loss_ref)
-
-    counts = jnp.sum(ext_ref[experts + 2 : experts + 4, :], axis=-1, keepdims=True)
-    count_all = (counts[0:1] * 128.0 + counts[1:2]) / shard
-    loss_ref[...] += jnp.sum(square) / count_all
-    dout = (total_tokens / count_all * valid[:, 0:1]) * residue
-    dout_ref[...] = dout
-    dlow_buf[step_at] = dout.astype(BF16)
-    lanes = lane_ids((1, 128))
-    grad = jnp.where(
-        lanes == cols[:, 2:3], jnp.sum(dout * from_first, axis=-1, keepdims=True), 0.0
-    ) + jnp.where(lanes == cols[:, 3:4], jnp.sum(dout * from_second, axis=-1, keepdims=True), 0.0)
-    real = jnp.where(lanes < experts, gates, 0.0)
-    dlogit_ref[...] = real * (grad - jnp.sum(real * grad, axis=-1, keepdims=True))
-
-    def copies(step):
-        return group_copies(images, step, dlow_buf, dlow_all, tsem, local_sem, dp_at, ex_at)
-
-    for step in range(images):
-
-        @pl.when(step_at == step)
-        def _():
-            for copy in copies(step)[:3]:
-                copy.start()
-            if step >= 2:
-                copies(step - 2)[2].wait_recv()
-                copies(step - 2)[3].start()
-
-    @pl.when(step_at == images - 1)
-    def _():
-        for step in (images - 2, images - 1):
-            copies(step)[2].wait_recv()
-            copies(step)[3].start()
-        for step in range(images):
-            keep, to_mate, to_chip, onward = copies(step)
-            keep.wait()
-            to_mate.wait()
-            to_chip.wait_send()
-            onward.wait()
-
-
-def expert_back_kernel(
-    cap, group, dlow_ref, codes_ref, grow_ref, rows_ref, hidden_ref, slope_ref, win_own, wex_own, win_other, wex_other,
-    back_ref, gin_ref, gex_ref, got_in, got_ex,
-    win_buf, wex_buf, acc_in, acc_out, low_in, low_ex, out_buf, y_send, y_recv, w_send, w_recv, local_sem,
-):
-    which_step, half_step = pl.program_id(0), pl.program_id(1)
-    which, half = 1 - which_step, 1 - half_step
     dp_at, ex_at, near = place()
-    ysem, wsem = (y_send, y_recv), (w_send, w_recv)
+    mate, across = (dp_at, flip(ex_at, 1)), (dp_at, flip(ex_at, 2))
+    tsem, ysem, wsem = (t_send, t_recv), (y_send, y_recv), (w_send, w_recv)
+    at_expert = jnp.maximum(step_at - images, 0)
+    which, half = 1 - at_expert // 2, lax.rem((at_expert + 1) // 2, 2)
+    order = [(1, 0), (1, 1), (0, 1), (0, 0)]
     loads = [
         pltpu.make_async_copy(win_own, win_buf.at[0], local_sem.at[3]),
         pltpu.make_async_copy(wex_own, wex_buf.at[0], local_sem.at[4]),
@@ -828,91 +757,164 @@
         for s, owner in enumerate((near[first], near[3])):
             spread.append(send(grad.at[1, owner], got.at[s], wsem, 2 * t + s, (near[first], ex_at)))
 
-    def at(q, step):
-        return pl.when((which == q) & (half_step == step))
-
-    @at(1, 0)
-    def _():
-        for copy in (loads[2], loads[3], loads[0], loads[1]):
+    def to_mate(step):
+        return send(dlow.at[0, step], dlow.at[1, step], tsem, step, mate)
+
+    def to_chip(step):
+        return send(dlow.at[0, step], dlow.at[2, step], tsem, images + step, across)
+
+    def onward(step):
+        return send(dlow.at[2, step], dlow.at[3, step], tsem, 2 * images + step, mate)
+
+    def returns(step):
+        q, side = order[step]
+        return return_copies(out_buf, back_ref, q, side, ysem, local_sem, dp_at, ex_at)
+
+    @pl.when(step_at == 0)
+    def _():
+        for copy in loads:
             copy.start()
         greet(
-            [(near[k], ex_at) for k in (1, 2)]
-            + [(dp_at, flip(ex_at, 1)), (dp_at, flip(ex_at, 2)), (dp_at, flip(flip(ex_at, 1), 2))]
+            [(near[k], ex_at) for k in (1, 2)] + [mate, across, (dp_at, flip(flip(ex_at, 1), 2))]
         )
+
+    @pl.when(step_at < images)
+    def _():
+        count = came_ref.shape[0]
+        cols = cols_ref[...]
+        rows = cols.shape[0]
+        hot = jnp.concatenate(
+            [
+                jnp.where(hot_cols(cols[:, 0:1], count), 1.0, 0.0).astype(BF16),
+                jnp.where(hot_cols(cols[:, 1:2], count), 1.0, 0.0).astype(BF16),
+            ],
+            axis=0,
+        )
+        both = dot(hot, came_ref[...])
+        from_first, from_second = both[:rows], both[rows:]
+        gates = gates_ref[...]
+        first, second = gates[:, experts : experts + 1], gates[:, experts + 1 : experts + 2]
+        output = resid_ref[...] + first * from_first + second * from_second
+        out_ref[...] = output.astype(BF16)
+        residue = output - target_ref[...].astype(F32)
+        valid = valid_ref[...]
+        square = jnp.mean(residue * residue, axis=-1, keepdims=True) * valid[:, 0:1]
+
+        @pl.when(step_at == 0)
+        def _():
+            loss_ref[...] = jnp.zeros_like(loss_ref)
+
+        counts = jnp.sum(ext_ref[experts + 2 : experts + 4, :], axis=-1, keepdims=True)
+        count_all = (counts[0:1] * 128.0 + counts[1:2]) / shard
+        loss_ref[...] += jnp.sum(square) / count_all
+        dout = (total_tokens / count_all * valid[:, 0:1]) * residue
+        dout_ref[...] = dout
+        dlow[0, step_at] = dout.astype(BF16)
+        lanes = lane_ids((1, 128))
+        grad = jnp.where(
+            lanes == cols[:, 2:3], jnp.sum(dout * from_first, axis=-1, keepdims=True), 0.0
+        ) + jnp.where(lanes == cols[:, 3:4], jnp.sum(dout * from_second, axis=-1, keepdims=True), 0.0)
+        real = jnp.where(lanes < experts, gates, 0.0)
+        dlogit_ref[...] = real * (grad - jnp.sum(real * grad, axis=-1, keepdims=True))
+
+    for step in range(images):
+
+        @pl.when(step_at == step)
+        def _():
+            to_chip(step).start()
+            to_mate(step).start()
+            if step >= 3:
+                to_chip(step - 3).wait_recv()
+                onward(step - 3).start()
+
+    @pl.when(step_at == images)
+    def _():
         for copy in loads:
             copy.wait()
-
-    blocks, images = dlow_ref.shape[0], dlow_ref.shape[1]
-    parts, width, hidden_width = win_buf.shape[1], dlow_ref.shape[3], win_buf.shape[3]
-    pieces = []
-    for block in range(blocks):
-        start = (which * group + half * blocks + block) * cap
-        total = None
-        slot_gate = None
-        for image in range(images):
-            codes = codes_ref[block, image]
-            slots = row_ids((cap, codes.shape[1])) + start
-            is_first = slots == codes[0:1, :]
-            is_second = slots == codes[1:2, :]
-            hot = jnp.where(is_first | is_second, 1.0, 0.0).astype(BF16)
-            term = dot(hot, dlow_ref[block, image])
-            gain = grow_ref[block, image]
-            picked = jnp.where(is_first, gain[0:1, :], jnp.where(is_second, gain[1:2, :], 0.0))
-            picked = jnp.sum(picked, axis=-1, keepdims=True)
-            total = term if total is None else total + term
-            slot_gate = picked if slot_gate is None else slot_gate + picked
-        pieces.append((total * slot_gate).astype(BF16))
-    grads = jnp.concatenate(pieces, axis=0)
-    grads_t = grads.T
-    rows_in_t = rows_ref[...].reshape(blocks * cap, -1).T
-    step = hidden_width // parts
-    result = None
-    for offset in range(0, hidden_width, step):
-        cut = slice(offset, offset + step)
-        hidden = hidden_ref[:, :, cut].reshape(blocks * cap, step)
-        slope = slope_ref[:, :, cut].reshape(blocks * cap, step).astype(F32)
-        dpre = (contract_cols(grads, wex_buf[which, offset // step]) * slope).astype(BF16)
-        gin = dot(rows_in_t, dpre)
-        gout = dot(grads_t, hidden)
-        term = contract_cols(dpre, win_buf[which, :, :, cut].reshape(width, step))
-        result = term if result is None else result + term
-
-        @pl.when(half_step == 0)
+        for step in range(images):
+            to_mate(step).wait_recv()
+
+    @pl.when(step_at == images + 1)
+    def _():
+        for step in range(images - 3, images):
+            to_chip(step).wait_recv()
+            onward(step).start()
+        for step in range(images):
+            onward(step).wait_recv()
+
+    @pl.when(step_at >= images)
+    def _():
+        blocks = group // 2
+        parts, width, hidden_width = win_buf.shape[1], dlow.shape[3], win_buf.shape[3]
+        pieces = []
+        for block in range(blocks):
+            start = (which * group + half * blocks + block) * cap
+            total = None
+            slot_gate = None
+            for image in range(images):
+                codes = codes_ref[half * blocks + block, image]
+                slots = row_ids((cap, codes.shape[1])) + start
+                is_first = slots == codes[0:1, :]
+                is_second = slots == codes[1:2, :]
+                hot = jnp.where(is_first | is_second, 1.0, 0.0).astype(BF16)
+                term = dot(hot, dlow[half * blocks + block, image])
+                gain = grow_ref[half * blocks + block, image]
+                picked = jnp.where(is_first, gain[0:1, :], jnp.where(is_second, gain[1:2, :], 0.0))
+                picked = jnp.sum(picked, axis=-1, keepdims=True)
+                total = term if total is None else total + term
+                slot_gate = picked if slot_gate is None else slot_gate + picked
+            pieces.append((total * slot_gate).astype(BF16))
+        grads = jnp.concatenate(pieces, axis=0)
+        grads_t = grads.T
+        rows_in_t = rows_ref[...].reshape(blocks * cap, -1).T
+        step = hidden_width // parts
+        result = None
+        for offset in range(0, hidden_width, step):
+            cut = slice(offset, offset + step)
+            hidden = hidden_ref[:, :, cut].reshape(blocks * cap, step)
+            slope = slope_ref[:, :, cut].reshape(blocks * cap, step).astype(F32)
+            dpre = (contract_cols(grads, wex_buf[which, offset // step]) * slope).astype(BF16)
+            gin = dot(rows_in_t, dpre)
+            gout = dot(grads_t, hidden)
+            term = contract_cols(dpre, win_buf[which, :, :, cut].reshape(width, step))
+            result = term if result is None else result + term
+
+            @pl.when(lax.rem(at_expert, 2) == 0)
+            def _():
+                acc_in[:, cut] = gin
+                acc_out[:, cut] = gout
+
+            @pl.when(lax.rem(at_expert, 2) == 1)
+            def _():
+                total_in = (acc_in[:, cut] + gin).astype(BF16)
+                low_in[which, :, :, cut] = total_in.reshape(parts, width // parts, step)
+                low_ex[which, offset // step] = (acc_out[:, cut] + gout).astype(BF16)
+
+        out_buf[which, pl.ds(half * blocks, blocks)] = result.astype(BF16).reshape(blocks, cap, width)
+
+    for step in range(4):
+
+        @pl.when(step_at == images + step)
         def _():
-            acc_in[:, cut] = gin
-            acc_out[:, cut] = gout
-
-        @pl.when(half_step == 1)
-        def _():
-            total_in = (acc_in[:, cut] + gin).astype(BF16)
-            low_in[which, :, :, cut] = total_in.reshape(parts, width // parts, step)
-            low_ex[which, offset // step] = (acc_out[:, cut] + gout).astype(BF16)
-
-    out_buf[which, pl.ds(half * blocks, blocks)] = result.astype(BF16).reshape(blocks, cap, width)
-
-    for q in range(2):
-        for step_at in range(2):
-
-            @at(q, step_at)
-            def _():
-                for copy in return_copies(out_buf, back_ref, q, 1 - step_at, ysem, local_sem, dp_at, ex_at):
+            for copy in returns(step):
+                copy.start()
+            if step == 1:
+                for copy in spread + stores[2:]:
                     copy.start()
 
-    @at(1, 1)
-    def _():
-        for copy in spread + stores[2:]:
-            copy.start()
-
-    @at(0, 1)
+    @pl.when(step_at == images + 3)
     def _():
         for copy in stores[:2]:
             copy.start()
-        for q in range(2):
-            for step_at in range(2):
-                for copy in return_copies(out_buf, back_ref, q, 1 - step_at, ysem, local_sem, dp_at, ex_at):
-                    copy.wait()
+        for step in range(4):
+            for copy in returns(step):
+                copy.wait()
         for copy in spread + stores:
             copy.wait()
+        for step in range(images):
+            to_mate(step).wait_send()
+            to_chip(step).wait_send()
+            onward(step).wait_send()
 
 
 def back_kernel(
@@ -1228,7 +1230,7 @@
         grid=(images,),
         in_specs=[
             per_image(rows, width), whole((shard, 3 * width)), whole((shard, width)), whole((shard, 128)),
-            per_image(rows, 8), per_image(8, rows), any_space, any_space, any_space,
+            per_image(rows, 8), per_image(8, rows), whole((images, 8, rows)), whole(in_part), whole(ex_part),
         ],
         out_specs=[
             per_image(rows, 3 * width), per_image(HEADS, rows, rows), per_image(rows, width),
@@ -1260,15 +1262,15 @@
     def by_half(*dims):
         return pl.BlockSpec((half_blocks,) + dims, lambda q, h: (1 - h,) + (0,) * len(dims))
 
-    def by_both(*dims, last_first=False):
-        if last_first:
-            return pl.BlockSpec((None, half_blocks) + dims, lambda q, h: (1 - q, 1 - h) + (0,) * len(dims))
+    def by_both(*dims):
         return pl.BlockSpec((None, half_blocks) + dims, lambda q, h: (q, 1 - h) + (0,) * len(dims))
 
     rows_in, hidden, slope, returned, win_other, wex_other = pl.pallas_call(
         lambda *refs: expert_forward_kernel(cap, group, *refs),
         grid=(2, 2),
-        in_specs=[by_half(images, rows, width), by_half(images, 8, rows), *[any_space] * 4],
+        in_specs=[
+            by_half(images, rows, width), by_half(images, 8, rows), any_space, any_space, whole(in_part), whole(ex_part),
+        ],
         out_specs=[by_both(cap, width), by_both(cap, hidden_width), by_both(cap, hidden_width), *[any_space] * 3],
         out_shape=[
             shape((2, group, cap, width), BF16), shape((2, group, cap, hidden_width), BF16),
@@ -1287,56 +1289,57 @@
     )(act_all, code_all, win_own, wex_own, win_far, expert_out[0])
     returned = returned.reshape(2 * group * cap, width)
 
-    block_out, dout, dlogits, loss_part, dlow_all = pl.pallas_call(
-        lambda *refs: combine_kernel(images, total_tokens, shard, experts, *refs),
-        grid=(images,),
+    flip_part = (width, hidden_width // dp)
+    last = images - 1
+
+    def early(*dims):
+        return pl.BlockSpec((None,) + dims, lambda i: (jnp.minimum(i, last),) + (0,) * len(dims))
+
+    def late(*dims):
+        def index(i):
+            step = jnp.maximum(i - images, 0)
+            return (1 - step // 2, lax.rem((step + 1) // 2, 2)) + (0,) * len(dims)
+
+        return pl.BlockSpec((None, half_blocks) + dims, index)
+
+    def once(dims):
+        return pl.BlockSpec(dims, lambda i: (0,) * len(dims), pipeline_mode=pl.Buffered(1))
+
+    block_out, dout, dlogits, loss_part, drows, gin, gout_t, got_in, got_ex = pl.pallas_call(
+        lambda *refs: combine_back_kernel(images, cap, group, total_tokens, shard, experts, *refs),
+        grid=(images + 4,),
         in_specs=[
-            pl.BlockSpec((16, width), lambda i: (0, 0)), per_image(rows, width), whole((2 * group * cap, width)),
-            per_image(rows, 8), per_image(rows, gate_lanes), per_image(rows, width), per_image(rows, 8),
+            once((16, width)), early(rows, width), once((2 * group * cap, width)), early(rows, 8),
+            early(rows, gate_lanes), early(rows, width), early(rows, 8), once((group, images, 8, rows)),
+            once((group, images, 8, rows)), late(cap, width), late(cap, hidden_width), late(cap, hidden_width),
+            *[any_space] * 4,
         ],
         out_specs=[
-            per_image(rows, width), per_image(rows, width), per_image(rows, gate_lanes), whole((8, 128)), any_space,
+            early(rows, width), early(rows, width), early(rows, gate_lanes), whole((8, 128)), *[any_space] * 5,
         ],
         out_shape=[
             shape((images, rows, width), BF16), shape((images, rows, width), F32),
-            shape((images, rows, gate_lanes), F32), shape((8, 128), F32), shape((group, images, rows, width), BF16),
-        ],
-        scratch_shapes=[
-            pltpu.VMEM((images, rows, width), BF16), *sem_pairs(3 * images), pltpu.SemaphoreType.DMA((images,)),
-        ],
-        compiler_params=pltpu.CompilerParams(
-            vmem_limit_bytes=56 * MB, collective_id=4, has_side_effects=True
-        ),
-        cost_estimate=pl.CostEstimate(flops=int(5e9), bytes_accessed=int(1e7), transcendentals=0),
-        name="combine_and_loss",
-    )(ext, resid, returned, cols, gates, target_p, valid_p)
-
-    flip_part = (width, hidden_width // dp)
-    drows, gin, gout_t, got_in, got_ex = pl.pallas_call(
-        lambda *refs: expert_back_kernel(cap, group, *refs),
-        grid=(2, 2),
-        in_specs=[
-            by_half(images, rows, width), by_half(images, 8, rows), by_half(images, 8, rows),
-            by_both(cap, width, last_first=True), by_both(cap, hidden_width, last_first=True),
-            by_both(cap, hidden_width, last_first=True), *[any_space] * 4,
-        ],
-        out_specs=[any_space] * 5,
-        out_shape=[
+            shape((images, rows, gate_lanes), F32), shape((8, 128), F32),
             shape((2, group, cap, width), BF16), shape((2, dp, *in_part), BF16), shape((2, dp, *flip_part), BF16),
             shape((2, *in_part), BF16), shape((2, *flip_part), BF16),
         ],
         scratch_shapes=[
+            pltpu.VMEM((group, images, rows, width), BF16),
             pltpu.VMEM((2, dp, *in_part), BF16), pltpu.VMEM((2, dp, *ex_part), BF16),
             pltpu.VMEM((width, hidden_width), F32), pltpu.VMEM((width, hidden_width), F32),
             pltpu.VMEM((2, dp, *in_part), BF16), pltpu.VMEM((2, dp, *flip_part), BF16),
-            pltpu.VMEM((2, group, cap, width), BF16), *sem_pairs(8), *sem_pairs(4), pltpu.SemaphoreType.DMA((11,)),
+            pltpu.VMEM((2, group, cap, width), BF16), *sem_pairs(3 * images), *sem_pairs(8), *sem_pairs(4),
+            pltpu.SemaphoreType.DMA((11,)),
         ],
         compiler_params=pltpu.CompilerParams(
-            vmem_limit_bytes=60 * MB, collective_id=5, has_side_effects=True
+            vmem_limit_bytes=62 * MB, collective_id=5, has_side_effects=True
         ),
         cost_estimate=pl.CostEstimate(flops=int(24e9), bytes_accessed=int(4e7), transcendentals=0),
-        name="expert_backward",
-    )(dlow_all, code_all, grow_all, rows_in, hidden, slope, win_own, wex_own, win_other, wex_other)
+        name="combine_expert_backward",
+    )(
+        ext, resid, returned, cols, gates, target_p, valid_p, code_all, grow_all, rows_in, hidden, slope,
+        win_own, wex_own, win_other, wex_other,
+    )
     grad_back = drows.reshape(2 * group * cap, width)
 
     def vmem(*dims):

time: 352 us -> 312 us (0.89)
  Pallas kernels: 328 us -> 287 us
    pallas_call x1, Pallas kernels: 80.1 us -> 63.8 us  [fast_shards(): pl.pallas_call(lambda *refs: forward_kernel(images, real_rows, experts, *...]
    pallas_call x1, Pallas kernels: 80.1 us -> 69 us  [fast_shards(): pl.pallas_call(lambda *refs: expert_forward_kernel(cap, group, *refs), gr...]
    pallas_call x2 -> x1, Pallas kernels: 84.7 us -> 74.5 us  [fast_shards(): pl.pallas_call(lambda *refs: combine_back_kernel(images, cap, group, tota...]
where the time goes in v4:
time: 312 us
  Pallas kernels  287 us (92%)
  local copies, waits for them, and re-layouts  20.1 us (6%)
    pallas_call x1, Pallas kernels, fast_shards(): pl.pallas_call(lambda *refs: back_kernel(images, experts, *refs), grid=(i...  80 us
    pallas_call x1, Pallas kernels, fast_shards(): pl.pallas_call(lambda *refs: combine_back_kernel(images, cap, group, tota...  74.5 us
    pallas_call x1, Pallas kernels, fast_shards(): pl.pallas_call(lambda *refs: expert_forward_kernel(cap, group, *refs), gr...  69 us
    pallas_call x1, Pallas kernels, fast_shards(): pl.pallas_call(lambda *refs: forward_kernel(images, real_rows, experts, *...  63.8 us

profile of v4, /device:TPU:0, one launch (start us, length us, event | category | flops | bytes accessed | tf_op | source)
XLA Modules:
  0.0 311.8 jit_solution(4432337960604648061)
XLA Ops:
  0.7 0.8 compare_select_fusion
  1.5 0.7 pad_add_fusion
  2.6 0.8 pad.30.refs_4_.refs_3_
  3.5 0.6 convert_reduce_fusion
  5.8 0.6 pad.28.refs_3_
  6.6 0.6 pad.31.clone.refs_5_.refs_6_
  7.5 1.1 pad.27.refs_0_
  8.6 63.8 %attention_forward.1 = (bf16[5,208,1536]{2,1,0:T(8,128)(2,1)}, bf16[5,8,208,208]{3,2,1,0:T(8,128)(2,1)}, bf16[5,208,512]{2,1,0:T(8,128)(2,1)}, f32[5,208,512]{2,...) custom-call(bf16[5,208,512]{2,1,0:T(8,128)(2,1)} %pad.27.refs_0_, ...), custom_call_target="tpu_custom_call" | custom-call | flops 5000000000 | bytes 20000000 | tf_op jit(solution)/shard_map/attention_forward/pallas_call | solution.py:1228
  72.5 69.0 %expert_forward.1 = (bf16[2,4,320,512]{3,2,1,0:T(8,128)(2,1)}, bf16[2,4,320,2048]{3,2,1,0:T(8,128)(2,1)}, bf16[2,4,320,2048]{3,2,1,0:T(8,128)(2,1)}, bf16[2,4,32...) custom-call(bf16[4,5,208,512]{3,2,1,0:T(8,128)(2,1)} %get-tuple-element.45.refs_0_, ...), custom_call_target="tpu_custom_call" | custom-call | flops 14000000000 | bytes 40000000 | tf_op jit(solution)/shard_map/expert_forward/pallas_call | solution.py:1268
  141.8 1.1 pad.32.refs_5_
  143.1 0.8 pad.33.refs_6_
  144.0 74.5 %combine_expert_backward.1 = (bf16[5,208,512]{2,1,0:T(8,128)(2,1)}, f32[5,208,512]{2,1,0:T(8,128)}, f32[5,208,128]{2,1,0:T(8,128)}, f32[8,128]{1,0:T(8,128)}, bf...) custom-call(f32[128,512]{1,0:T(8,128)} %get-tuple-element.43.refs_0_, ...), custom_call_target="tpu_custom_call" | custom-call | flops 24000000000 | bytes 40000000 | tf_op jit(solution)/shard_map/combine_expert_backward/pallas_call | solution.py:1308
  218.5 80.0 %attention_backward.1 = (f32[5,208,512]{2,1,0:T(8,128)}, f32[16,2048]{1,0:T(8,128)}, f32[16,512]{1,0:T(8,128)}, f32[128,2048]{1,0:T(8,128)}, f32[512,512]{1,0:T(8,128)}) custom-call(bf16[5,208,512]{2,1,0:T(8,128)(2,1)} %pad.27.refs_0_, bf16[512,2176]{1,0:T(8,128)(2,1)} %get-tuple-element.59.refs_1_, f32[128,512]{1,0:T(8,128)} %get-tuple-element.43.refs_0_.refs_2_, ...), custom_call_target="tpu_custom_call" | custom-call | flops 10000000000 | bytes 30000000 | tf_op jit(solution)/shard_map/attention_backward/pallas_call | solution.py:1348
  298.5 1.7 slice.26
  300.3 1.5 reshape.54
  301.8 1.3 copy.35
  303.1 0.6 slice.28
  303.8 0.6 slice.29
  304.4 1.3 dynamic-slice_bitcast_fusion
  305.7 1.3 dynamic-slice_bitcast_fusion.1
  307.1 1.2 slice.25
  308.3 1.3 slice.24
  309.6 1.2 reshape.52
  310.8 1.0 copy.38
  (33 shorter events, 1.9 us)
Async XLA Ops:
  0.6 2.8 copy-start.5
  0.7 4.7 %copy-start.6 = (bf16[16,8]{0,1:T(8,128)(2,1)S(1)}, bf16[16,8]{0,1:T(8,128)(2,1)}, u32[]{:S(2)}) copy-start(bf16[16,8]{0,1:T(8,128)(2,1)} %param.21) | copy-start | bytes 772
  0.7 4.8 %copy-start.7 = (bf16[16]{0:T(256)(128)(2,1)S(1)}, bf16[16]{0:T(256)(128)(2,1)}, u32[]{:S(2)}) copy-start(bf16[16]{0:T(256)(128)(2,1)} %param.17) | copy-start | bytes 100
  0.7 4.9 %copy-start.8 = (bf16[16]{0:T(256)(128)(2,1)S(1)}, bf16[16]{0:T(256)(128)(2,1)}, u32[]{:S(2)}) copy-start(bf16[16]{0:T(256)(128)(2,1)} %param.20) | copy-start | bytes 100
  0.7 6.6 %copy-start.2 = (bf16[985,512]{1,0:T(8,128)(2,1)S(1)}, bf16[985,512]{1,0:T(8,128)(2,1)}, u32[]{:S(2)}) copy-start(bf16[985,512]{1,0:T(8,128)(2,1)} %param.12) | copy-start | bytes 3025924
  72.5 69.0 %copy-start.3 = (bf16[985,512]{1,0:T(8,128)(2,1)S(1)}, bf16[985,512]{1,0:T(8,128)(2,1)}, u32[]{:S(2)}) copy-start(bf16[985,512]{1,0:T(8,128)(2,1)} %param.13) | copy-start | bytes 3025924
  300.3 1.6 copy-start.1
  300.3 2.9 copy-start.4
  303.8 7.0 %copy-start = (f32[128,2048]{1,0:T(8,128)S(1)}, f32[128,2048]{1,0:T(8,128)}, u32[]{:S(2)}) copy-start(f32[128,2048]{1,0:T(8,128)} %get-tuple-element.74) | copy-start | bytes 3145732

commit v5 on v4

--- a/solution.py
+++ b/solution.py
@@ -389,53 +389,70 @@
     return values * cumulative, cumulative + values * density
 
 
-def plane_gather(mine, blocks, sems, base, dp_at, ex_at, near):
-    half = blocks.shape[1] // 2
+def plane_gather(mine, blocks, q, sems, base, dp_at, ex_at, near):
+    half = blocks.shape[2] // 2
     first, second = pl.ds(0, half), pl.ds(half, half)
-    own = [
-        send(mine, blocks.at[dp_at], sems, base + k - 1, (near[k], ex_at)) for k in (1, 2)
-    ]
+    own = [send(mine, blocks.at[q, dp_at], sems, base + k - 1, (near[k], ex_at)) for k in (1, 2)]
     passed = [
-        send(blocks.at[near[1], first], blocks.at[near[1], first], sems, base + 2, (near[2], ex_at)),
-        send(blocks.at[near[2], second], blocks.at[near[2], second], sems, base + 3, (near[1], ex_at)),
+        send(blocks.at[q, near[1], first], blocks.at[q, near[1], first], sems, base + 2, (near[2], ex_at)),
+        send(blocks.at[q, near[2], second], blocks.at[q, near[2], second], sems, base + 3, (near[1], ex_at)),
     ]
     return own, passed
 
 
-def group_copies(images, step, buf, dest, tsem, lsem, dp_at, ex_at):
-    mate, across = flip(ex_at, 1), flip(ex_at, 2)
-    keep = pltpu.make_async_copy(buf.at[step], dest.at[0, step], lsem.at[step])
-    to_mate = send(buf.at[step], dest.at[1, step], tsem, step, (dp_at, mate))
-    to_chip = send(buf.at[step], dest.at[2, step], tsem, images + step, (dp_at, across))
-    onward = send(dest.at[2, step], dest.at[3, step], tsem, 2 * images + step, (dp_at, mate))
-    return keep, to_mate, to_chip, onward
-
-
-def forward_kernel(
-    images, real_rows, experts, tok_ref, qkvw_ref, outw_ref, extra_ref, cols_ref, rows_ref, codes_ref, win_ref, wex_ref,
-    qkv_ref, probs_ref, mixed_ref, resid_ref, gates_ref, dense_ref, ext_ref,
-    act_all, code_all, grow_all, win_all, wex_all, far_in,
-    dense, act_buf, grow_buf, d_send, d_recv, t_send, t_recv, r_send, r_recv, w_send, w_recv, local_sem,
+def hot_rows(codes, start, count):
+    slots = row_ids((count, codes.shape[1])) + start
+    return (slots == codes[0:1, :]) | (slots == codes[1:2, :])
+
+
+def return_copies(buf, back, q, half, sems, local, dp_at, ex_at):
+    peers = [None, (dp_at, flip(ex_at, 1)), (dp_at, flip(ex_at, 2)), (dp_at, flip(flip(ex_at, 1), 2))]
+    copies = []
+    for k in (2 * half, 2 * half + 1):
+        if k == 0:
+            copies.append(pltpu.make_async_copy(buf.at[q, 0], back.at[q, 0], local.at[q]))
+        else:
+            copies.append(send(buf.at[q, k], back.at[q, k], sems, 4 * q + k, peers[k]))
+    return copies
+
+
+def front_kernel(
+    images, real_rows, experts, cap, group,
+    tok_ref, qkvw_ref, outw_ref, extra_ref, cols_ref, rows_ref, codes_ref, win_ref, wex_ref,
+    qkv_ref, probs_ref, mixed_ref, resid_ref, gates_ref, dense_ref, ext_ref, rows_out_ref, hidden_ref, slope_ref,
+    back_ref, code_out, grow_out, win_out, wex_out,
+    dense, act, code_buf, grow_buf, win_buf, wex_buf, out_buf, kept,
+    d_send, d_recv, t_send, t_recv, r_send, r_recv, w_send, w_recv, y_send, y_recv, local_sem,
 ):
     step_at = pl.program_id(0)
     dp_at, ex_at, near = place()
     core, floor = lax.rem(ex_at, 2), ex_at // 2
-    dsem, tsem, rsem, wsem = (d_send, d_recv), (t_send, t_recv), (r_send, r_recv), (w_send, w_recv)
-    group_peers = [(dp_at, flip(ex_at, 1)), (dp_at, flip(ex_at, 2)), (dp_at, flip(flip(ex_at, 1), 2))]
+    dsem, tsem, rsem, wsem, ysem = (d_send, d_recv), (t_send, t_recv), (r_send, r_recv), (w_send, w_recv), (y_send, y_recv)
+    mate, across, beyond = (dp_at, flip(ex_at, 1)), (dp_at, flip(ex_at, 2)), (dp_at, flip(flip(ex_at, 1), 2))
+    far = (dp_at, flip(ex_at, 4))
+    group_peers = [mate, across, beyond]
     floors = [floor, flip(floor, 1), flip(floor, 2), flip(flip(floor, 1), 2)]
     columns = [dp_at] + near[1:]
-
-    codes_out = [send(codes_ref, code_all.at[k + 1], rsem, k, group_peers[k]) for k in range(3)]
-    grow_out = [send(grow_buf, grow_all.at[k + 1], rsem, 3 + k, group_peers[k]) for k in range(3)]
-    keeps = [
-        pltpu.make_async_copy(codes_ref, code_all.at[0], local_sem.at[images]),
-        pltpu.make_async_copy(win_ref, win_all.at[dp_at], local_sem.at[images + 1]),
-        pltpu.make_async_copy(wex_ref, wex_all.at[dp_at], local_sem.at[images + 2]),
+    at_expert = jnp.maximum(step_at - images, 0)
+    which, half = at_expert // 2, lax.rem((at_expert + 1) // 2, 2)
+    order = [(0, 0), (0, 1), (1, 1), (1, 0)]
+
+    codes_sent = [send(codes_ref, code_buf.at[k + 1], rsem, k, group_peers[k]) for k in range(3)]
+    grow_sent = [send(grow_buf.at[0], grow_buf.at[k + 1], rsem, 3 + k, group_peers[k]) for k in range(3)]
+    stores = [
+        pltpu.make_async_copy(code_buf, code_out, local_sem.at[2]),
+        pltpu.make_async_copy(grow_buf, grow_out, local_sem.at[3]),
+        pltpu.make_async_copy(win_buf, win_out, local_sem.at[4]),
+        pltpu.make_async_copy(wex_buf, wex_out, local_sem.at[5]),
     ]
-    keep_grow = pltpu.make_async_copy(grow_buf, grow_all.at[0], local_sem.at[images + 3])
-    in_own, in_passed = plane_gather(win_ref, win_all, wsem, 0, dp_at, ex_at, near)
-    ex_own, ex_passed = plane_gather(wex_ref, wex_all, wsem, 4, dp_at, ex_at, near)
-    to_far = send(win_ref, far_in, wsem, 8, (dp_at, flip(ex_at, 4)))
+    in_own, in_passed = plane_gather(win_ref, win_buf, 0, wsem, 0, dp_at, ex_at, near)
+    ex_own, ex_passed = plane_gather(wex_ref, wex_buf, 0, wsem, 4, dp_at, ex_at, near)
+    in_far, in_far_passed = plane_gather(win_buf.at[1, dp_at], win_buf, 1, wsem, 8, dp_at, ex_at, near)
+    ex_far, ex_far_passed = plane_gather(wex_buf.at[1, dp_at], wex_buf, 1, wsem, 12, dp_at, ex_at, near)
+    to_far = [
+        send(win_ref, win_buf.at[1, dp_at], wsem, 16, far),
+        send(wex_ref, wex_buf.at[1, dp_at], wsem, 17, far),
+    ]
     along_line = [
         send(dense.at[dp_at, floor, core], dense.at[dp_at, floor, core], dsem, k - 1, (dp_at, 2 * floors[k] + core))
         for k in (1, 2, 3)
@@ -450,276 +467,241 @@
         ]
         for k in range(4)
     ]
-    to_mate = [
-        send(dense.at[columns[p], :, core], dense.at[columns[p], :, core], dsem, 15 + p, group_peers[0])
-        for p in range(4)
+    dense_mate = [
+        send(dense.at[columns[p], :, core], dense.at[columns[p], :, core], dsem, 15 + p, mate) for p in range(4)
     ]
 
+    def to_mate(step):
+        return send(act.at[0, step], act.at[1, step], tsem, step, mate)
+
+    def to_chip(step):
+        return send(act.at[0, step], act.at[2, step], tsem, images + step, across)
+
+    def onward(step):
+        return send(act.at[2, step], act.at[3, step], tsem, 2 * images + step, mate)
+
+    def returns(step):
+        q, side = order[step]
+        return return_copies(out_buf, back_ref, q, side, ysem, local_sem, dp_at, ex_at)
+
+    def pass_on(own, passed):
+        for first, second in zip(own, passed):
+            first.wait_recv()
+            second.start()
+
     @pl.when(step_at == 0)
     def _():
-        for copy in keeps:
-            copy.start()
         width = outw_ref.shape[1]
         dense[dp_at, floor, core, :, : 3 * width] = qkvw_ref[...]
         dense[dp_at, floor, core, :, 3 * width : 4 * width] = outw_ref[...]
         dense[dp_at, floor, core, :, 4 * width :] = extra_ref[...]
-        greet(
-            [(near[k], ex_at) for k in (1, 2, 3)]
-            + group_peers
-            + [(dp_at, flip(ex_at, 4)), (dp_at, flip(flip(ex_at, 2), 4))]
-        )
+        code_buf[0] = codes_ref[...]
+        greet([(near[k], ex_at) for k in (1, 2, 3)] + group_peers + [far, (dp_at, flip(flip(ex_at, 2), 4))])
         for copy in along_line + in_plane[0]:
             copy.start()
+        win_buf[0, dp_at] = win_ref[...]
+        wex_buf[0, dp_at] = wex_ref[...]
         for k in (1, 2, 3):
             along_line[k - 1].wait_recv()
             for copy in in_plane[k]:
                 copy.start()
-        to_mate[0].start()
-        for copy in codes_out:
+        dense_mate[0].start()
+        for copy in to_far + codes_sent:
             copy.start()
         for p in (1, 2, 3):
             for k in range(4):
                 in_plane[k][p - 1].wait_recv()
-            to_mate[p].start()
-        for copy in in_own + ex_own + [to_far]:
-            copy.start()
-        for copy in to_mate:
+            dense_mate[p].start()
+        for copy in in_own + ex_own:
+            copy.start()
+        for copy in dense_mate:
             copy.wait_recv()
         full = dense[...].reshape(dense_ref.shape)
         dense_ref[...] = full
         ext_ref[...] = full[:, 4 * width :].astype(F32).T
 
-    inputs = tok_ref[...].astype(F32)
-    normed, _ = normalize(inputs)
-    width = inputs.shape[1]
-    act_one = (normed * ext_ref[experts : experts + 1, :]).astype(BF16)
-    qkv = dot(act_one, dense_ref[:, : 3 * width]).astype(BF16)
-    qkv_ref[...] = qkv
-    rows = inputs.shape[0]
-    low_half = lane_ids((1, 128)) < 64
-    key_bias = jnp.where(lane_ids((1, rows)) < real_rows, 0.0, -1e30)
-    parts = []
-    for pair in range(width // 128):
-        lanes = slice(128 * pair, 128 * (pair + 1))
-        queries = qkv[:, lanes]
-        key_rows = qkv[:, width + 128 * pair : width + 128 * (pair + 1)]
-        values = qkv[:, 2 * width + 128 * pair : 2 * width + 128 * (pair + 1)]
-        outs = []
-        for side in range(2):
-            mask = low_half if side == 0 else jnp.logical_not(low_half)
-            masked = jnp.where(mask, queries, jnp.zeros_like(queries))
-            scores = contract_cols(masked, key_rows) * 0.125 + key_bias
-            exped = jnp.exp(scores - jnp.max(scores, axis=-1, keepdims=True))
-            probs = (exped * (1.0 / jnp.sum(exped, axis=-1, keepdims=True))).astype(BF16)
-            probs_ref[2 * pair + side] = probs
-            outs.append(dot(probs, values))
-        parts.append(jnp.where(low_half, outs[0], outs[1]).astype(BF16))
-    mixed = jnp.concatenate(parts, axis=1)
-    mixed_ref[...] = mixed
-    resid = inputs + dot(mixed, dense_ref[:, 3 * width : 4 * width])
-    resid_ref[...] = resid
-    normed_two, _ = normalize(resid)
-    act_two = (normed_two * ext_ref[experts + 1 : experts + 2, :]).astype(BF16)
-    act_buf[step_at] = act_two
-    lanes = lane_ids((1, 128))
-    logits = jnp.where(lanes < experts, dot(act_two, dense_ref[:, 4 * width :]), -1e30)
-    exped = jnp.exp(logits - jnp.max(logits, axis=-1, keepdims=True))
-    gates = exped / jnp.sum(exped, axis=-1, keepdims=True)
-    cols = cols_ref[...]
-    first = jnp.sum(jnp.where(lanes == cols[:, 2:3], gates, 0.0), axis=-1, keepdims=True)
-    second = jnp.sum(jnp.where(lanes == cols[:, 3:4], gates, 0.0), axis=-1, keepdims=True)
-    gates_ref[...] = jnp.where(lanes == experts, first, jnp.where(lanes == experts + 1, second, gates))
-    logits_t = contract_cols(ext_ref[0:16, :].astype(BF16), act_two)[:experts]
-    exped_t = jnp.exp(logits_t - jnp.max(logits_t, axis=0, keepdims=True))
-    gates_t = exped_t / jnp.sum(exped_t, axis=0, keepdims=True)
-    ids_t = row_ids(gates_t.shape)
-    first_t = jnp.sum(jnp.where(ids_t == rows_ref[2:3, :], gates_t, 0.0), axis=0, keepdims=True)
-    second_t = jnp.sum(jnp.where(ids_t == rows_ref[3:4, :], gates_t, 0.0), axis=0, keepdims=True)
-    grow_buf[step_at] = jnp.where(row_ids((8, rows)) == 0, first_t, second_t)
+    @pl.when(step_at < images)
+    def _():
+        inputs = tok_ref[...].astype(F32)
+        normed, _ = normalize(inputs)
+        width = inputs.shape[1]
+        act_one = (normed * ext_ref[experts : experts + 1, :]).astype(BF16)
+        qkv = dot(act_one, dense_ref[:, : 3 * width]).astype(BF16)
+        qkv_ref[...] = qkv
+        rows = inputs.shape[0]
+        low_half = lane_ids((1, 128)) < 64
+        key_bias = jnp.where(lane_ids((1, rows)) < real_rows, 0.0, -1e30)
+        parts = []
+        for pair in range(width // 128):
+            lanes = slice(128 * pair, 128 * (pair + 1))
+            queries = qkv[:, lanes]
+            key_rows = qkv[:, width + 128 * pair : width + 128 * (pair + 1)]
+            values = qkv[:, 2 * width + 128 * pair : 2 * width + 128 * (pair + 1)]
+            outs = []
+            for side in range(2):
+                mask = low_half if side == 0 else jnp.logical_not(low_half)
+                masked = jnp.where(mask, queries, jnp.zeros_like(queries))
+                scores = contract_cols(masked, key_rows) * 0.125 + key_bias
+                exped = jnp.exp(scores - jnp.max(scores, axis=-1, keepdims=True))
+                probs = (exped * (1.0 / jnp.sum(exped, axis=-1, keepdims=True))).astype(BF16)
+                probs_ref[2 * pair + side] = probs
+                outs.append(dot(probs, values))
+            parts.append(jnp.where(low_half, outs[0], outs[1]).astype(BF16))
+        mixed = jnp.concatenate(parts, axis=1)
+        mixed_ref[...] = mixed
+        resid = inputs + dot(mixed, dense_ref[:, 3 * width : 4 * width])
+        resid_ref[...] = resid
+        normed_two, _ = normalize(resid)
+        act_two = (normed_two * ext_ref[experts + 1 : experts + 2, :]).astype(BF16)
+        act[0, step_at] = act_two
+        lanes = lane_ids((1, 128))
+        logits = jnp.where(lanes < experts, dot(act_two, dense_ref[:, 4 * width :]), -1e30)
+        exped = jnp.exp(logits - jnp.max(logits, axis=-1, keepdims=True))
+        gates = exped / jnp.sum(exped, axis=-1, keepdims=True)
+        cols = cols_ref[...]
+        first = jnp.sum(jnp.where(lanes == cols[:, 2:3], gates, 0.0), axis=-1, keepdims=True)
+        second = jnp.sum(jnp.where(lanes == cols[:, 3:4], gates, 0.0), axis=-1, keepdims=True)
+        gates_ref[...] = jnp.where(lanes == experts, first, jnp.where(lanes == experts + 1, second, gates))
+        logits_t = contract_cols(ext_ref[0:16, :].astype(BF16), act_two)[:experts]
+        exped_t = jnp.exp(logits_t - jnp.max(logits_t, axis=0, keepdims=True))
+        gates_t = exped_t / jnp.sum(exped_t, axis=0, keepdims=True)
+        ids_t = row_ids(gates_t.shape)
+        first_t = jnp.sum(jnp.where(ids_t == rows_ref[2:3, :], gates_t, 0.0), axis=0, keepdims=True)
+        second_t = jnp.sum(jnp.where(ids_t == rows_ref[3:4, :], gates_t, 0.0), axis=0, keepdims=True)
+        grow_buf[0, step_at] = jnp.where(row_ids((8, rows)) == 0, first_t, second_t)
 
     for step in range(images):
-        keep, mate_copy, chip_copy, _ = group_copies(images, step, act_buf, act_all, tsem, local_sem, dp_at, ex_at)
 
         @pl.when(step_at == step)
         def _():
-            keep.start()
-            mate_copy.start()
-            chip_copy.start()
-
-    def pass_on(step):
-        _, _, chip_copy, onward = group_copies(images, step, act_buf, act_all, tsem, local_sem, dp_at, ex_at)
-        chip_copy.wait_recv()
-        onward.start()
-
-    for step in range(images - 2):
-
-        @pl.when(step_at == step + 2)
-        def _():
-            pass_on(step)
+            to_chip(step).start()
+            to_mate(step).start()
+            if step >= 3:
+                to_chip(step - 3).wait_recv()
+                onward(step - 3).start()
 
     @pl.when(step_at == images - 2)
     def _():
-        in_own[0].wait_recv()
-        in_passed[0].start()
-        in_own[1].wait_recv()
-        in_passed[1].start()
+        pass_on(in_own, in_passed)
 
     @pl.when(step_at == images - 1)
     def _():
-        keep_grow.start()
-        for copy in grow_out:
-            copy.start()
-        ex_own[0].wait_recv()
-        ex_passed[0].start()
-        ex_own[1].wait_recv()
-        ex_passed[1].start()
-        for step in (images - 2, images - 1):
-            pass_on(step)
+        for copy in grow_sent:
+            copy.start()
+
+    @pl.when(step_at == images)
+    def _():
+        pass_on(ex_own, ex_passed)
+        to_far[0].wait_recv()
+        for copy in in_far:
+            copy.start()
+        for copy in in_passed + codes_sent:
+            copy.wait_recv()
         for step in range(images):
-            keep, mate_copy, chip_copy, onward = group_copies(
-                images, step, act_buf, act_all, tsem, local_sem, dp_at, ex_at
-            )
-            keep.wait()
-            mate_copy.wait()
-            chip_copy.wait_send()
-            onward.wait()
-        keep_grow.wait()
-        for copy in keeps:
-            copy.wait()
-        for copy in codes_out + grow_out + in_passed + ex_passed + [to_far]:
-            copy.wait()
-        for copy in along_line + to_mate + in_own + ex_own + [c for line in in_plane for c in line]:
-            copy.wait_send()
-
-
-def hot_rows(codes, start, count):
-    slots = row_ids((count, codes.shape[1])) + start
-    return (slots == codes[0:1, :]) | (slots == codes[1:2, :])
-
-
-def return_copies(buf, back, q, half, sems, local, dp_at, ex_at):
-    peers = [None, (dp_at, flip(ex_at, 1)), (dp_at, flip(ex_at, 2)), (dp_at, flip(flip(ex_at, 1), 2))]
-    copies = []
-    for k in (2 * half, 2 * half + 1):
-        if k == 0:
-            copies.append(pltpu.make_async_copy(buf.at[q, 0], back.at[q, 0], local.at[q]))
-        else:
-            copies.append(send(buf.at[q, k], back.at[q, k], sems, 4 * q + k, peers[k]))
-    return copies
-
-
-def expert_forward_kernel(
-    cap, group, act_ref, codes_ref, win_own, wex_own, win_far, wex_mine,
-    rows_out_ref, hidden_ref, slope_ref, back_ref, win_other, wex_other,
-    win_buf, wex_buf, out_buf, y_send, y_recv, w_send, w_recv, local_sem,
-):
-    which, half_step = pl.program_id(0), pl.program_id(1)
-    half = 1 - half_step
-    dp_at, ex_at, near = place()
-    ysem, wsem = (y_send, y_recv), (w_send, w_recv)
-    keep_in = pltpu.make_async_copy(win_far, win_other.at[dp_at], local_sem.at[2])
-    loads = [
-        pltpu.make_async_copy(win_own, win_buf.at[0], local_sem.at[3]),
-        pltpu.make_async_copy(wex_own, wex_buf.at[0], local_sem.at[4]),
-        pltpu.make_async_copy(win_other, win_buf.at[1], local_sem.at[5]),
-        pltpu.make_async_copy(wex_other, wex_buf.at[1], local_sem.at[6]),
-    ]
-    in_own, in_passed = plane_gather(win_far, win_other, wsem, 0, dp_at, ex_at, near)
-    ex_own, ex_passed = plane_gather(wex_other.at[dp_at], wex_other, wsem, 4, dp_at, ex_at, near)
-    to_far = send(wex_mine, wex_other.at[dp_at], wsem, 8, (dp_at, flip(ex_at, 4)))
-
-    def at(q, step):
-        return pl.when((which == q) & (half_step == step))
-
-    @at(0, 0)
-    def _():
-        keep_in.start()
-        loads[0].start()
-        loads[1].start()
-        greet(
-            [(near[k], ex_at) for k in (1, 2)]
-            + [(dp_at, flip(ex_at, 1)), (dp_at, flip(ex_at, 2)), (dp_at, flip(flip(ex_at, 1), 2)), (dp_at, flip(ex_at, 4))]
-        )
-        to_far.start()
-        keep_in.wait()
-        for copy in in_own:
-            copy.start()
-        loads[0].wait()
-        loads[1].wait()
-
-    @at(1, 0)
-    def _():
-        for copy in in_passed:
+            to_mate(step).wait_recv()
+
+    @pl.when(step_at == images + 1)
+    def _():
+        for step in range(images - 3, images):
+            to_chip(step).wait_recv()
+            onward(step).start()
+        for step in range(images):
+            onward(step).wait_recv()
+
+    @pl.when(step_at == images + 2)
+    def _():
+        for copy in in_far_passed:
             copy.wait_recv()
-        loads[2].start()
-        loads[2].wait()
-
-    blocks, images = act_ref.shape[0], act_ref.shape[1]
-    parts, width, hidden_width = win_buf.shape[1], act_ref.shape[3], win_buf.shape[3]
-    pieces = []
-    for block in range(blocks):
-        start = (which * group + half * blocks + block) * cap
-        total = None
-        for image in range(images):
-            hot = jnp.where(hot_rows(codes_ref[block, image], start, cap), 1.0, 0.0).astype(BF16)
-            term = dot(hot, act_ref[block, image])
-            total = term if total is None else total + term
-        pieces.append(total.astype(BF16))
-    rows_in = jnp.concatenate(pieces, axis=0)
-    rows_out_ref[...] = rows_in.reshape(rows_out_ref.shape)
-    step = hidden_width // parts
-    for part in range(parts):
-        cut = slice(part * step, (part + 1) * step)
-        act, slope = gelu_pair(dot(rows_in, win_buf[which, :, :, cut].reshape(width, step)))
-        hidden_ref[:, :, cut] = act.astype(BF16).reshape(blocks, cap, step)
-        slope_ref[:, :, cut] = slope.astype(BF16).reshape(blocks, cap, step)
-
-    @at(1, 0)
-    def _():
-        for own, passed in zip(ex_own, ex_passed):
-            own.wait_recv()
-            passed.start()
+
+    blocks = group // 2
+    parts, width, hidden_width = win_buf.shape[1], act.shape[3], win_buf.shape[3]
+    step_width = hidden_width // parts
+
+    @pl.when(step_at >= images)
+    def _():
+        pieces = []
+        for block in range(blocks):
+            start = (which * group + half * blocks + block) * cap
+            total = None
+            for image in range(images):
+                hot = hot_rows(code_buf[half * blocks + block, image], start, cap)
+                term = dot(jnp.where(hot, 1.0, 0.0).astype(BF16), act[half * blocks + block, image])
+                total = term if total is None else total + term
+            pieces.append(total.astype(BF16))
+        rows_in = jnp.concatenate(pieces, axis=0)
+        rows_out_ref[...] = rows_in.reshape(rows_out_ref.shape)
+        for part in range(parts):
+            if part == 1:
+
+                @pl.when(step_at == images + 1)
+                def _():
+                    pass_on(in_far, in_far_passed)
+                    to_far[1].wait_recv()
+                    for copy in ex_far:
+                        copy.start()
+
+            cut = slice(part * step_width, (part + 1) * step_width)
+            hidden, slope = gelu_pair(dot(rows_in, win_buf[which, :, :, cut].reshape(width, step_width)))
+            hidden_ref[:, :, cut] = hidden.astype(BF16).reshape(blocks, cap, step_width)
+            slope_ref[:, :, cut] = slope.astype(BF16).reshape(blocks, cap, step_width)
+
+    def second_product(source, q, side):
+        result = None
+        for part in range(parts):
+            cut = slice(part * step_width, (part + 1) * step_width)
+            term = dot(source[:, :, cut].reshape(blocks * cap, step_width), wex_buf[q, part])
+            result = term if result is None else result + term
+        out_buf[q, pl.ds(side * blocks, blocks)] = result.astype(BF16).reshape(blocks, cap, width)
+
+    @pl.when(step_at == images)
+    def _():
         for copy in ex_passed:
             copy.wait_recv()
-        loads[3].start()
-        loads[3].wait()
-
-    result = None
-    for part in range(parts):
-        cut = slice(part * step, (part + 1) * step)
-        term = dot(hidden_ref[:, :, cut].reshape(blocks * cap, step), wex_buf[which, part])
-        result = term if result is None else result + term
-    out_buf[which, pl.ds(half * blocks, blocks)] = result.astype(BF16).reshape(blocks, cap, width)
-
-    for q in range(2):
-        for step_at in range(2):
-
-            @at(q, step_at)
-            def _():
-                for copy in return_copies(out_buf, back_ref, q, 1 - step_at, ysem, local_sem, dp_at, ex_at):
-                    copy.start()
-
-    @at(0, 0)
-    def _():
-        in_own[0].wait_recv()
-        in_passed[0].start()
-        in_own[1].wait_recv()
-        in_passed[1].start()
-
-    @at(0, 1)
-    def _():
-        to_far.wait_recv()
-        for copy in ex_own:
-            copy.start()
-
-    @at(1, 1)
-    def _():
-        for q in range(2):
-            for step_at in range(2):
-                for copy in return_copies(out_buf, back_ref, q, 1 - step_at, ysem, local_sem, dp_at, ex_at):
-                    copy.wait()
-        for copy in in_own + in_passed + ex_own + ex_passed + [to_far]:
+
+    @pl.when(step_at == images + 2)
+    def _():
+        kept[...] = hidden_ref[...]
+
+    @pl.when(step_at == images + 3)
+    def _():
+        pass_on(ex_far, ex_far_passed)
+        for copy in grow_sent:
+            copy.wait_recv()
+        for copy in ex_far_passed:
+            copy.wait_recv()
+        for copy in stores:
+            copy.start()
+        second_product(kept, 1, 1)
+        for copy in returns(2):
+            copy.start()
+
+    @pl.when((step_at >= images) & (step_at != images + 2))
+    def _():
+        second_product(hidden_ref, which, half)
+
+    for step in (0, 1, 3):
+
+        @pl.when(step_at == images + step)
+        def _():
+            for copy in returns(step):
+                copy.start()
+
+    @pl.when(step_at == images + 3)
+    def _():
+        for step in range(4):
+            for copy in returns(step):
+                copy.wait()
+        for copy in stores:
+            copy.wait()
+        for step in range(images):
+            to_mate(step).wait_send()
+            to_chip(step).wait_send()
+            onward(step).wait_send()
+        for copy in along_line + dense_mate + codes_sent + grow_sent + to_far + [c for line in in_plane for c in line]:
             copy.wait_send()
+        for own, passed in ((in_own, in_passed), (ex_own, ex_passed), (in_far, in_far_passed), (ex_far, ex_far_passed)):
+            for copy in own + passed:
+                copy.wait_send()
 
 
 def hot_cols(codes, count):
@@ -728,9 +710,10 @@
 
 def combine_back_kernel(
     images, cap, group, total_tokens, shard, experts, ext_ref, resid_ref, came_ref, cols_ref, gates_ref, target_ref,
-    valid_ref, codes_ref, grow_ref, rows_ref, hidden_ref, slope_ref, win_own, wex_own, win_other, wex_other,
-    out_ref, dout_ref, dlogit_ref, loss_ref, back_ref, gin_ref, gex_ref, got_in, got_ex,
+    valid_ref, codes_ref, grow_ref, rows_ref, hidden_ref, slope_ref, win_all, wex_all,
+    out_ref, dout_ref, dlogit_ref, loss_ref, back_ref, gin_ref, gex_ref, far_in, far_ex,
     dlow, win_buf, wex_buf, acc_in, acc_out, low_in, low_ex, out_buf,
+    got_in, got_ex, sum_in, sum_ex, more_in, more_ex,
     t_send, t_recv, y_send, y_recv, w_send, w_recv, local_sem,
 ):
     step_at = pl.program_id(0)
@@ -741,21 +724,19 @@
     which, half = 1 - at_expert // 2, lax.rem((at_expert + 1) // 2, 2)
     order = [(1, 0), (1, 1), (0, 1), (0, 0)]
     loads = [
-        pltpu.make_async_copy(win_own, win_buf.at[0], local_sem.at[3]),
-        pltpu.make_async_copy(wex_own, wex_buf.at[0], local_sem.at[4]),
-        pltpu.make_async_copy(win_other, win_buf.at[1], local_sem.at[5]),
-        pltpu.make_async_copy(wex_other, wex_buf.at[1], local_sem.at[6]),
+        pltpu.make_async_copy(win_all, win_buf, local_sem.at[3]),
+        pltpu.make_async_copy(wex_all, wex_buf, local_sem.at[4]),
     ]
     stores = [
-        pltpu.make_async_copy(low_in.at[0], gin_ref.at[0], local_sem.at[7]),
-        pltpu.make_async_copy(low_ex.at[0], gex_ref.at[0], local_sem.at[8]),
-        pltpu.make_async_copy(low_in.at[1], gin_ref.at[1], local_sem.at[9]),
-        pltpu.make_async_copy(low_ex.at[1], gex_ref.at[1], local_sem.at[10]),
+        pltpu.make_async_copy(low_in.at[0], gin_ref, local_sem.at[7]),
+        pltpu.make_async_copy(low_ex.at[0], gex_ref, local_sem.at[8]),
     ]
-    spread = []
-    for t, (grad, got, first) in enumerate(((low_in, got_in, 1), (low_ex, got_ex, 2))):
+    tensors = [(low_in, got_in, sum_in, more_in, far_in, 1, 2), (low_ex, got_ex, sum_ex, more_ex, far_ex, 2, 1)]
+    spread, second_round = [], []
+    for t, (grad, got, passed, more, _, first, second) in enumerate(tensors):
         for s, owner in enumerate((near[first], near[3])):
-            spread.append(send(grad.at[1, owner], got.at[s], wsem, 2 * t + s, (near[first], ex_at)))
+            spread.append(send(grad.at[1, owner], got.at[s], wsem, 3 * t + s, (near[first], ex_at)))
+        second_round.append(send(passed, more, wsem, 3 * t + 2, (near[second], ex_at)))
 
     def to_mate(step):
         return send(dlow.at[0, step], dlow.at[1, step], tsem, step, mate)
@@ -899,18 +880,30 @@
             for copy in returns(step):
                 copy.start()
             if step == 1:
-                for copy in spread + stores[2:]:
+                for copy in spread:
                     copy.start()
 
     @pl.when(step_at == images + 3)
     def _():
-        for copy in stores[:2]:
+        for copy in stores:
+            copy.start()
+        for copy in spread:
+            copy.wait_recv()
+        for grad, got, passed, _, _, _, second in tensors:
+            passed[...] = (grad[1, near[second]].astype(F32) + got[1].astype(F32)).astype(BF16)
+        for copy in second_round:
             copy.start()
         for step in range(4):
             for copy in returns(step):
                 copy.wait()
-        for copy in spread + stores:
+        for copy in second_round:
+            copy.wait_recv()
+        for grad, got, _, more, far, _, _ in tensors:
+            far[...] = (grad[1, dp_at].astype(F32) + got[0].astype(F32) + more[...].astype(F32)).astype(BF16)
+        for copy in stores:
             copy.wait()
+        for copy in spread + second_round:
+            copy.wait_send()
         for step in range(images):
             to_mate(step).wait_send()
             to_chip(step).wait_send()
@@ -919,9 +912,9 @@
 
 def back_kernel(
     images, experts, tok_ref, dense_w, ext_ref, cols_ref, back_ref, dlogit_ref, resid_ref,
-    dout_ref, qkv_ref, probs_ref, mixed_ref, loss_ref, gin_ref, gex_ref, got_in_ref, got_ex_ref,
+    dout_ref, qkv_ref, probs_ref, mixed_ref, loss_ref, gin_ref, gex_ref, far_in, far_ex,
     tgrad_ref, dense_ref, misc_ref, gin_out, gex_out,
-    acc, acc_misc, part_in, part_ex, got_in, got_ex, sum_in, sum_ex, more_in, more_ex, far_in, far_ex, came_in, came_ex,
+    acc, acc_misc, part_in, part_ex, got_in, got_ex, sum_in, sum_ex, more_in, more_ex, came_in, came_ex,
     low, mate, low_mate, plane, low_plane, line, misc_got, local_sem, w_send, w_recv, d_send, d_recv, m_send, m_recv,
 ):
     step_at = pl.program_id(0)
@@ -932,64 +925,27 @@
         (gin_ref, part_in, got_in, sum_in, more_in, far_in, came_in, gin_out, 1, 2),
         (gex_ref, part_ex, got_ex, sum_ex, more_ex, far_ex, came_ex, gex_out, 2, 1),
     ]
-
-    def local_copies():
-        copies = []
-        for t, (grad, part, _, _, _, _, _, _, _, second) in enumerate(tensors):
-            for q in range(2):
-                for s in range(2):
-                    owner = dp_at if s == 0 else near[second]
-                    copies.append(
-                        pltpu.make_async_copy(grad.at[q, owner], part.at[q, s], local_sem.at[4 * t + 2 * q + s])
-                    )
-        copies.append(pltpu.make_async_copy(got_in_ref, got_in.at[1], local_sem.at[8]))
-        copies.append(pltpu.make_async_copy(got_ex_ref, got_ex.at[1], local_sem.at[9]))
-        return copies
-
-    def first_round(q):
-        copies = []
-        for t, (grad, _, got, _, _, _, _, _, first, _) in enumerate(tensors):
-            for s in range(2):
-                owner = near[first] if s == 0 else near[3]
-                copies.append(
-                    send(grad.at[q, owner], got.at[q, s], wsem, 8 * q + 4 * t + s, (near[first], ex_at))
-                )
-        return copies
-
-    def second_round(q):
-        return [
-            send(passed.at[q], more.at[q], wsem, 8 * q + 4 * t + 2, (near[second], ex_at))
-            for t, (_, _, _, passed, more, _, _, _, _, second) in enumerate(tensors)
-        ]
-
-    def far_round():
-        return [
-            send(far, came, wsem, 4 * t + 3, (dp_at, flip(ex_at, 4)))
-            for t, (_, _, _, _, _, far, came, _, _, _) in enumerate(tensors)
-        ]
-
-    def add_first(q):
-        for _, part, got, passed, _, _, _, _, _, _ in tensors:
-            passed[q] = (part[q, 1].astype(F32) + got[q, 1].astype(F32)).astype(BF16)
-        for copy in second_round(q):
-            copy.start()
-
-    def total_of(tensor, q):
-        _, part, got, _, more, _, _, _, _, _ = tensor
-        return part[q, 0].astype(F32) + got[q, 0].astype(F32) + more[q].astype(F32)
+    local_copies, first_round, second_round, far_round = [], [], [], []
+    for t, (grad, part, got, passed, more, far, came, _, first, second) in enumerate(tensors):
+        for s in range(2):
+            mine = dp_at if s == 0 else near[second]
+            theirs = near[first] if s == 0 else near[3]
+            local_copies.append(pltpu.make_async_copy(grad.at[mine], part.at[s], local_sem.at[2 * t + s]))
+            first_round.append(send(grad.at[theirs], got.at[s], wsem, 4 * t + s, (near[first], ex_at)))
+        second_round.append(send(passed, more, wsem, 4 * t + 2, (near[second], ex_at)))
+        far_round.append(send(far, came, wsem, 4 * t + 3, (dp_at, flip(ex_at, 4))))
 
     @pl.when(step_at == 0)
     def _():
-        for copy in local_copies():
+        for copy in local_copies:
             copy.start()
         greet(
             [(near[k], ex_at) for k in (1, 2, 3)]
             + [(dp_at, flip(ex_at, bit)) for bit in (1, 2, 4)]
             + [(dp_at, flip(flip(ex_at, 2), 4))]
         )
-        for copy in local_copies():
-            copy.wait()
-        add_first(1)
+        for copy in first_round + far_round:
+            copy.start()
 
     count = back_ref.shape[0]
     cols = cols_ref[...]
@@ -1081,13 +1037,15 @@
         acc[:, 3 * width :] += gout
         acc_misc[...] += gmisc
 
-    @pl.when(step_at == 1)
-    def _():
-        for copy in second_round(1):
+    @pl.when(step_at == images - 2)
+    def _():
+        for copy in local_copies:
+            copy.wait()
+        for copy in first_round:
             copy.wait_recv()
-        for tensor in tensors:
-            tensor[5][...] = total_of(tensor, 1).astype(BF16)
-        for copy in far_round() + first_round(0):
+        for _, part, got, passed, _, _, _, _, _, _ in tensors:
+            passed[...] = (part[1].astype(F32) + got[1].astype(F32)).astype(BF16)
+        for copy in second_round:
             copy.start()
 
     @pl.when(step_at == images - 1)
@@ -1110,9 +1068,6 @@
             if k < 4:
                 misc[k + 1].start()
 
-        for copy in first_round(0):
-            copy.wait_recv()
-        add_first(0)
         to_mate.wait_recv()
         low_mate[...] = (low[:, :, core].astype(F32) + mate[...].astype(F32)).astype(BF16)
         to_plane = [send(low_mate.at[near[k]], plane.at[k - 1], dsem, k, (near[k], ex_at)) for k in (1, 2, 3)]
@@ -1143,15 +1098,13 @@
             result = result + line[k].astype(F32)
         dense_ref[...] = result
 
-        for copy in second_round(0):
+        for copy in second_round + far_round:
             copy.wait_recv()
-        for copy in far_round():
-            copy.wait_recv()
-        for tensor in tensors:
-            tensor[7][...] = total_of(tensor, 0) + tensor[6][...].astype(F32)
-        for copy in [to_mate] + misc + to_plane + to_line + first_round(0):
-            copy.wait_send()
-        for copy in second_round(0) + second_round(1) + far_round():
+        for _, part, got, _, more, _, came, out, _, _ in tensors:
+            out[...] = (
+                part[0].astype(F32) + got[0].astype(F32) + more[...].astype(F32) + came[...].astype(F32)
+            )
+        for copy in [to_mate] + misc + to_plane + to_line + first_round + second_round + far_round:
             copy.wait_send()
 
 
@@ -1223,113 +1176,92 @@
 
     gate_lanes = 128
     dense_lanes = 4 * width + 128
+    half_blocks = group // 2
+    last = images - 1
+
+    def early(*dims):
+        return pl.BlockSpec((None,) + dims, lambda i: (jnp.minimum(i, last),) + (0,) * len(dims))
+
+    def late(far_first, *dims):
+        def index(i):
+            step = jnp.maximum(i - images, 0)
+            which = 1 - step // 2 if far_first else step // 2
+            return (which, lax.rem((step + 1) // 2, 2)) + (0,) * len(dims)
+
+        return pl.BlockSpec((None, half_blocks) + dims, index)
+
+    def once(dims):
+        return pl.BlockSpec(dims, lambda i: (0,) * len(dims), pipeline_mode=pl.Buffered(1))
+
     (
-        qkv_p, probs, mixed, resid, gates, dense_full, ext, act_all, code_all, grow_all, win_own, wex_own, win_far,
+        qkv_p, probs, mixed, resid, gates, dense_full, ext, rows_in, hidden, slope, returned, code_all, grow_all,
+        win_all, wex_all,
     ) = pl.pallas_call(
-        lambda *refs: forward_kernel(images, real_rows, experts, *refs),
-        grid=(images,),
+        lambda *refs: front_kernel(images, real_rows, experts, cap, group, *refs),
+        grid=(images + 4,),
         in_specs=[
-            per_image(rows, width), whole((shard, 3 * width)), whole((shard, width)), whole((shard, 128)),
-            per_image(rows, 8), per_image(8, rows), whole((images, 8, rows)), whole(in_part), whole(ex_part),
+            early(rows, width), once((shard, 3 * width)), once((shard, width)), once((shard, 128)),
+            early(rows, 8), early(8, rows), once((images, 8, rows)), once(in_part), once(ex_part),
         ],
         out_specs=[
-            per_image(rows, 3 * width), per_image(HEADS, rows, rows), per_image(rows, width),
-            per_image(rows, width), per_image(rows, gate_lanes), whole((width, dense_lanes)), whole((128, width)),
-            *[any_space] * 6,
+            early(rows, 3 * width), early(HEADS, rows, rows), early(rows, width), early(rows, width),
+            early(rows, gate_lanes), whole((width, dense_lanes)), whole((128, width)),
+            late(False, cap, width), late(False, cap, hidden_width), late(False, cap, hidden_width),
+            *[any_space] * 5,
         ],
         out_shape=[
             shape((images, rows, 3 * width), BF16), shape((images, HEADS, rows, rows), BF16),
             shape((images, rows, width), BF16), shape((images, rows, width), F32),
             shape((images, rows, gate_lanes), F32), shape((width, dense_lanes), BF16), shape((128, width), F32),
-            shape((group, images, rows, width), BF16), shape((group, images, 8, rows), jnp.int32),
-            shape((group, images, 8, rows), F32), shape((dp, *in_part), BF16), shape((dp, *ex_part), BF16),
-            shape(in_part, BF16),
+            shape((2, group, cap, width), BF16), shape((2, group, cap, hidden_width), BF16),
+            shape((2, group, cap, hidden_width), BF16), shape((2, group, cap, width), BF16),
+            shape((group, images, 8, rows), jnp.int32), shape((group, images, 8, rows), F32),
+            shape((2, dp, *in_part), BF16), shape((2, dp, *ex_part), BF16),
         ],
         scratch_shapes=[
-            pltpu.VMEM((dp, floors, 2, shard, dense_lanes), BF16), pltpu.VMEM((images, rows, width), BF16),
-            pltpu.VMEM((images, 8, rows), F32),
-            *sem_pairs(19), *sem_pairs(3 * images), *sem_pairs(6), *sem_pairs(9),
-            pltpu.SemaphoreType.DMA((images + 4,)),
+            pltpu.VMEM((dp, floors, 2, shard, dense_lanes), BF16), pltpu.VMEM((group, images, rows, width), BF16),
+            pltpu.VMEM((group, images, 8, rows), jnp.int32), pltpu.VMEM((group, images, 8, rows), F32),
+            pltpu.VMEM((2, dp, *in_part), BF16), pltpu.VMEM((2, dp, *ex_part), BF16),
+            pltpu.VMEM((2, group, cap, width), BF16), pltpu.VMEM((half_blocks, cap, hidden_width), BF16),
+            *sem_pairs(19), *sem_pairs(3 * images), *sem_pairs(6), *sem_pairs(18), *sem_pairs(8),
+            pltpu.SemaphoreType.DMA((6,)),
         ],
         compiler_params=pltpu.CompilerParams(
-            vmem_limit_bytes=56 * MB, collective_id=2, has_side_effects=True
+            vmem_limit_bytes=60 * MB, collective_id=2, has_side_effects=True
         ),
-        cost_estimate=pl.CostEstimate(flops=int(5e9), bytes_accessed=int(2e7), transcendentals=0),
-        name="attention_forward",
+        cost_estimate=pl.CostEstimate(flops=int(20e9), bytes_accessed=int(6e7), transcendentals=0),
+        name="attention_expert_forward",
     )(tok_p, qkv_weight, out_weight, extra, cols, row_codes, row_codes, expert_in[0], expert_out[0])
-
-    half_blocks = group // 2
-    def by_half(*dims):
-        return pl.BlockSpec((half_blocks,) + dims, lambda q, h: (1 - h,) + (0,) * len(dims))
-
-    def by_both(*dims):
-        return pl.BlockSpec((None, half_blocks) + dims, lambda q, h: (q, 1 - h) + (0,) * len(dims))
-
-    rows_in, hidden, slope, returned, win_other, wex_other = pl.pallas_call(
-        lambda *refs: expert_forward_kernel(cap, group, *refs),
-        grid=(2, 2),
-        in_specs=[
-            by_half(images, rows, width), by_half(images, 8, rows), any_space, any_space, whole(in_part), whole(ex_part),
-        ],
-        out_specs=[by_both(cap, width), by_both(cap, hidden_width), by_both(cap, hidden_width), *[any_space] * 3],
-        out_shape=[
-            shape((2, group, cap, width), BF16), shape((2, group, cap, hidden_width), BF16),
-            shape((2, group, cap, hidden_width), BF16), shape((2, group, cap, width), BF16),
-            shape((dp, *in_part), BF16), shape((dp, *ex_part), BF16),
-        ],
-        scratch_shapes=[
-            pltpu.VMEM((2, dp, *in_part), BF16), pltpu.VMEM((2, dp, *ex_part), BF16),
-            pltpu.VMEM((2, group, cap, width), BF16), *sem_pairs(8), *sem_pairs(9), pltpu.SemaphoreType.DMA((7,)),
-        ],
-        compiler_params=pltpu.CompilerParams(
-            vmem_limit_bytes=58 * MB, collective_id=3, has_side_effects=True
-        ),
-        cost_estimate=pl.CostEstimate(flops=int(14e9), bytes_accessed=int(4e7), transcendentals=0),
-        name="expert_forward",
-    )(act_all, code_all, win_own, wex_own, win_far, expert_out[0])
     returned = returned.reshape(2 * group * cap, width)
 
     flip_part = (width, hidden_width // dp)
-    last = images - 1
-
-    def early(*dims):
-        return pl.BlockSpec((None,) + dims, lambda i: (jnp.minimum(i, last),) + (0,) * len(dims))
-
-    def late(*dims):
-        def index(i):
-            step = jnp.maximum(i - images, 0)
-            return (1 - step // 2, lax.rem((step + 1) // 2, 2)) + (0,) * len(dims)
-
-        return pl.BlockSpec((None, half_blocks) + dims, index)
-
-    def once(dims):
-        return pl.BlockSpec(dims, lambda i: (0,) * len(dims), pipeline_mode=pl.Buffered(1))
-
-    block_out, dout, dlogits, loss_part, drows, gin, gout_t, got_in, got_ex = pl.pallas_call(
+    block_out, dout, dlogits, loss_part, drows, gin, gout_t, far_in, far_ex = pl.pallas_call(
         lambda *refs: combine_back_kernel(images, cap, group, total_tokens, shard, experts, *refs),
         grid=(images + 4,),
         in_specs=[
             once((16, width)), early(rows, width), once((2 * group * cap, width)), early(rows, 8),
             early(rows, gate_lanes), early(rows, width), early(rows, 8), once((group, images, 8, rows)),
-            once((group, images, 8, rows)), late(cap, width), late(cap, hidden_width), late(cap, hidden_width),
-            *[any_space] * 4,
+            once((group, images, 8, rows)), late(True, cap, width), late(True, cap, hidden_width),
+            late(True, cap, hidden_width), any_space, any_space,
         ],
         out_specs=[
-            early(rows, width), early(rows, width), early(rows, gate_lanes), whole((8, 128)), *[any_space] * 5,
+            early(rows, width), early(rows, width), early(rows, gate_lanes), whole((8, 128)), *[any_space] * 3,
+            once(in_part), once(flip_part),
         ],
         out_shape=[
             shape((images, rows, width), BF16), shape((images, rows, width), F32),
             shape((images, rows, gate_lanes), F32), shape((8, 128), F32),
-            shape((2, group, cap, width), BF16), shape((2, dp, *in_part), BF16), shape((2, dp, *flip_part), BF16),
-            shape((2, *in_part), BF16), shape((2, *flip_part), BF16),
+            shape((2, group, cap, width), BF16), shape((dp, *in_part), BF16), shape((dp, *flip_part), BF16),
+            shape(in_part, BF16), shape(flip_part, BF16),
         ],
         scratch_shapes=[
             pltpu.VMEM((group, images, rows, width), BF16),
             pltpu.VMEM((2, dp, *in_part), BF16), pltpu.VMEM((2, dp, *ex_part), BF16),
             pltpu.VMEM((width, hidden_width), F32), pltpu.VMEM((width, hidden_width), F32),
             pltpu.VMEM((2, dp, *in_part), BF16), pltpu.VMEM((2, dp, *flip_part), BF16),
-            pltpu.VMEM((2, group, cap, width), BF16), *sem_pairs(3 * images), *sem_pairs(8), *sem_pairs(4),
-            pltpu.SemaphoreType.DMA((11,)),
+            pltpu.VMEM((2, group, cap, width), BF16),
+            *[pltpu.VMEM(dims, BF16) for dims in ((2, *in_part), (2, *flip_part), in_part, flip_part, in_part, flip_part)],
+            *sem_pairs(3 * images), *sem_pairs(8), *sem_pairs(6), pltpu.SemaphoreType.DMA((9,)),
         ],
         compiler_params=pltpu.CompilerParams(
             vmem_limit_bytes=62 * MB, collective_id=5, has_side_effects=True
@@ -1338,7 +1270,7 @@
         name="combine_expert_backward",
     )(
         ext, resid, returned, cols, gates, target_p, valid_p, code_all, grow_all, rows_in, hidden, slope,
-        win_own, wex_own, win_other, wex_other,
+        win_all, wex_all,
     )
     grad_back = drows.reshape(2 * group * cap, width)
 
@@ -1363,13 +1295,12 @@
         ],
         scratch_shapes=[
             pltpu.VMEM((width, 4 * width), F32), pltpu.VMEM((16, width), F32),
-            vmem(2, 2, *in_part), vmem(2, 2, *flip_part), vmem(2, 2, *in_part), vmem(2, 2, *flip_part),
             vmem(2, *in_part), vmem(2, *flip_part), vmem(2, *in_part), vmem(2, *flip_part),
-            vmem(*in_part), vmem(*flip_part), vmem(*in_part), vmem(*flip_part),
+            vmem(*in_part), vmem(*flip_part), vmem(*in_part), vmem(*flip_part), vmem(*in_part), vmem(*flip_part),
             vmem(dp, floors, 2, shard, 4 * width), vmem(dp, floors, shard, 4 * width), vmem(dp, floors, shard, 4 * width),
             vmem(3, floors, shard, 4 * width), vmem(floors, shard, 4 * width), vmem(3, shard, 4 * width),
-            pltpu.VMEM((10, 16, width), F32), pltpu.SemaphoreType.DMA((10,)),
-            *sem_pairs(16), *sem_pairs(8), *sem_pairs(5),
+            pltpu.VMEM((10, 16, width), F32), pltpu.SemaphoreType.DMA((4,)),
+            *sem_pairs(8), *sem_pairs(8), *sem_pairs(5),
         ],
         compiler_params=pltpu.CompilerParams(
             vmem_limit_bytes=60 * MB, collective_id=1, has_side_effects=True
@@ -1378,7 +1309,7 @@
         name="attention_backward",
     )(
         tok_p, dense_full, ext, cols, grad_back, dlogits, resid, dout, qkv_p, probs, mixed,
-        loss_part, gin, gout_t, got_in, got_ex,
+        loss_part, gin, gout_t, far_in, far_ex,
     )
     flat = lax.axis_index("dp") * experts + me
     mine = lax.dynamic_slice_in_dim(misc, flat * shard, shard, axis=1)

time: 312 us -> 293 us (0.939)
  Pallas kernels: 287 us -> 269 us
    pallas_call x2 -> x1, Pallas kernels: 133 us -> 119 us  [fast_shards(): pl.pallas_call(lambda *refs: front_kernel(images, real_rows, experts, cap...]
    pallas_call x1, Pallas kernels: 80 us -> 66.8 us  [fast_shards(): pl.pallas_call(lambda *refs: back_kernel(images, experts, *refs), grid=(i...]
    pallas_call x1, Pallas kernels: 74.5 us -> 82.8 us  [fast_shards(): pl.pallas_call(lambda *refs: combine_back_kernel(images, cap, group, tota...]
where the time goes in v5:
time: 293 us; the launch traced here: 292 us
  Pallas kernels  269 us (92%)
  local copies, waits for them, and re-layouts  19 us (6%)
    pallas_call x1, Pallas kernels, fast_shards(): pl.pallas_call(lambda *refs: front_kernel(images, real_rows, experts, cap...  119 us
    pallas_call x1, Pallas kernels, fast_shards(): pl.pallas_call(lambda *refs: combine_back_kernel(images, cap, group, tota...  82.8 us
    pallas_call x1, Pallas kernels, fast_shards(): pl.pallas_call(lambda *refs: back_kernel(images, experts, *refs), grid=(i...  66.8 us

profile of v5, /device:TPU:0, one launch (start us, length us, event | category | flops | bytes accessed | tf_op | source)
XLA Modules:
  0.0 292.3 jit_solution(17765811008194336114)
XLA Ops:
  0.7 0.8 compare_select_fusion
  1.5 0.7 pad_add_fusion
  2.6 0.8 pad.30.refs_4_.refs_3_
  3.5 0.6 convert_reduce_fusion
  5.8 0.6 pad.28.refs_3_
  6.6 0.6 pad.31.clone.refs_5_.refs_6_
  7.3 0.3 reshape.48
  7.5 1.1 pad.27.refs_0_
  8.6 119.5 %attention_expert_forward.1 = (bf16[5,208,1536]{2,1,0:T(8,128)(2,1)}, bf16[5,8,208,208]{3,2,1,0:T(8,128)(2,1)}, bf16[5,208,512]{2,1,0:T(8,128)(2,1)}, f32[5,208,...) custom-call(bf16[5,208,512]{2,1,0:T(8,128)(2,1)} %pad.27.refs_0_, ...), custom_call_target="tpu_custom_call" | custom-call | flops 20000000000 | bytes 60000000 | tf_op jit(solution)/shard_map/attention_expert_forward/pallas_call | solution.py:1199
  128.1 0.3 reshape.51
  128.4 1.1 pad.32.refs_5_
  129.8 0.8 pad.33.refs_6_
  130.6 82.8 %combine_expert_backward.1 = (bf16[5,208,512]{2,1,0:T(8,128)(2,1)}, f32[5,208,512]{2,1,0:T(8,128)}, f32[5,208,128]{2,1,0:T(8,128)}, f32[8,128]{1,0:T(8,128)}, bf...) custom-call(f32[128,512]{1,0:T(8,128)} %get-tuple-element.39.refs_0_, ...), custom_call_target="tpu_custom_call" | custom-call | flops 24000000000 | bytes 40000000 | tf_op jit(solution)/shard_map/combine_expert_backward/pallas_call | solution.py:1238
  213.4 66.8 %attention_backward.1 = (f32[5,208,512]{2,1,0:T(8,128)}, f32[16,2048]{1,0:T(8,128)}, f32[16,512]{1,0:T(8,128)}, f32[128,2048]{1,0:T(8,128)}, f32[512,512]{1,0:T(8,128)}) custom-call(bf16[5,208,512]{2,1,0:T(8,128)(2,1)} %pad.27.refs_0_, bf16[512,2176]{1,0:T(8,128)(2,1)} %get-tuple-element.51.refs_1_, f32[128,512]{1,0:T(8,128)} %get-tuple-element.39.refs_0_.refs_2_, ...), custom_call_target="tpu_custom_call" | custom-call | flops 10000000000 | bytes 30000000 | tf_op jit(solution)/shard_map/attention_backward/pallas_call | solution.py:1280
  280.3 1.7 slice.26
  282.0 1.5 reshape.54
  283.6 1.3 copy.35
  284.9 0.6 slice.28
  285.5 0.6 slice.29
  286.2 1.3 dynamic-slice_bitcast_fusion
  287.5 1.3 dynamic-slice_bitcast_fusion.1
  288.8 1.2 slice.25
  290.1 1.2 reshape.52
  291.3 1.0 copy.38
  (34 shorter events, 1.4 us)
Async XLA Ops:
  0.6 2.8 copy-start.6
  0.7 4.7 %copy-start.7 = (bf16[16,8]{0,1:T(8,128)(2,1)S(1)}, bf16[16,8]{0,1:T(8,128)(2,1)}, u32[]{:S(2)}) copy-start(bf16[16,8]{0,1:T(8,128)(2,1)} %param.21) | copy-start | bytes 772
  0.7 4.8 %copy-start.8 = (bf16[16]{0:T(256)(128)(2,1)S(1)}, bf16[16]{0:T(256)(128)(2,1)}, u32[]{:S(2)}) copy-start(bf16[16]{0:T(256)(128)(2,1)} %param.17) | copy-start | bytes 100
  0.7 4.9 %copy-start.9 = (bf16[16]{0:T(256)(128)(2,1)S(1)}, bf16[16]{0:T(256)(128)(2,1)}, u32[]{:S(2)}) copy-start(bf16[16]{0:T(256)(128)(2,1)} %param.20) | copy-start | bytes 100
  0.7 6.6 %copy-start.2 = (bf16[985,512]{1,0:T(8,128)(2,1)S(1)}, bf16[985,512]{1,0:T(8,128)(2,1)}, u32[]{:S(2)}) copy-start(bf16[985,512]{1,0:T(8,128)(2,1)} %param.12) | copy-start | bytes 3025924
  8.6 119.5 %copy-start.3 = (bf16[985,512]{1,0:T(8,128)(2,1)S(1)}, bf16[985,512]{1,0:T(8,128)(2,1)}, u32[]{:S(2)}) copy-start(bf16[985,512]{1,0:T(8,128)(2,1)} %param.13) | copy-start | bytes 3025924
  282.0 1.6 copy-start.1
  282.0 2.9 copy-start.5
  283.6 6.4 %copy-start.4 = (bf16[5,208,512]{2,1,0:T(8,128)(2,1)S(1)}, bf16[5,208,512]{2,1,0:T(8,128)(2,1)}, u32[]{:S(2)}) copy-start(bf16[5,208,512]{2,1,0:T(8,128)(2,1)} %get-tuple-element.50) | copy-start | bytes 3194884
  285.5 5.8 %copy-start = (f32[128,2048]{1,0:T(8,128)S(1)}, f32[128,2048]{1,0:T(8,128)}, u32[]{:S(2)}) copy-start(f32[128,2048]{1,0:T(8,128)} %get-tuple-element.66) | copy-start | bytes 3145732

commit v6 on v5

--- a/solution.py
+++ b/solution.py
@@ -418,7 +418,7 @@
 
 def front_kernel(
     images, real_rows, experts, cap, group,
-    tok_ref, qkvw_ref, outw_ref, extra_ref, cols_ref, rows_ref, codes_ref, win_ref, wex_ref,
+    tok_ref, qkvw_ref, outw_ref, extra_ref, cols_ref, rows_ref, codes_ref, all_cols_ref, win_ref, wex_ref,
     qkv_ref, probs_ref, mixed_ref, resid_ref, gates_ref, dense_ref, ext_ref, rows_out_ref, hidden_ref, slope_ref,
     back_ref, code_out, grow_out, win_out, wex_out,
     dense, act, code_buf, grow_buf, win_buf, wex_buf, out_buf, kept,
@@ -494,7 +494,15 @@
         width = outw_ref.shape[1]
         dense[dp_at, floor, core, :, : 3 * width] = qkvw_ref[...]
         dense[dp_at, floor, core, :, 3 * width : 4 * width] = outw_ref[...]
-        dense[dp_at, floor, core, :, 4 * width :] = extra_ref[...]
+        valid = jnp.maximum(all_cols_ref[...], 0).astype(F32)
+        per_lane = jnp.sum(jnp.sum(valid, axis=0), axis=0, keepdims=True)
+        my_count = jnp.sum(jnp.where(lane_ids((1, 8)) == 4, per_lane, 0.0), axis=-1, keepdims=True)
+        count_high = jnp.floor(my_count * (1.0 / 128.0))
+        lanes = lane_ids((1, 128))
+        counts = jnp.where(lanes == experts + 2, count_high, 0.0) + jnp.where(
+            lanes == experts + 3, my_count - 128.0 * count_high, 0.0
+        )
+        dense[dp_at, floor, core, :, 4 * width :] = (extra_ref[...].astype(F32) + counts).astype(BF16)
         code_buf[0] = codes_ref[...]
         greet([(near[k], ex_at) for k in (1, 2, 3)] + group_peers + [far, (dp_at, flip(flip(ex_at, 2), 4))])
         for copy in along_line + in_plane[0]:
@@ -710,7 +718,7 @@
 
 def combine_back_kernel(
     images, cap, group, total_tokens, shard, experts, ext_ref, resid_ref, came_ref, cols_ref, gates_ref, target_ref,
-    valid_ref, codes_ref, grow_ref, rows_ref, hidden_ref, slope_ref, win_all, wex_all,
+    codes_ref, grow_ref, rows_ref, hidden_ref, slope_ref, win_all, wex_all,
     out_ref, dout_ref, dlogit_ref, loss_ref, back_ref, gin_ref, gex_ref, far_in, far_ex,
     dlow, win_buf, wex_buf, acc_in, acc_out, low_in, low_ex, out_buf,
     got_in, got_ex, sum_in, sum_ex, more_in, more_ex,
@@ -778,8 +786,8 @@
         output = resid_ref[...] + first * from_first + second * from_second
         out_ref[...] = output.astype(BF16)
         residue = output - target_ref[...].astype(F32)
-        valid = valid_ref[...]
-        square = jnp.mean(residue * residue, axis=-1, keepdims=True) * valid[:, 0:1]
+        valid = jnp.maximum(cols[:, 4:5], 0).astype(F32)
+        square = jnp.mean(residue * residue, axis=-1, keepdims=True) * valid
 
         @pl.when(step_at == 0)
         def _():
@@ -788,7 +796,7 @@
         counts = jnp.sum(ext_ref[experts + 2 : experts + 4, :], axis=-1, keepdims=True)
         count_all = (counts[0:1] * 128.0 + counts[1:2]) / shard
         loss_ref[...] += jnp.sum(square) / count_all
-        dout = (total_tokens / count_all * valid[:, 0:1]) * residue
+        dout = (total_tokens / count_all * valid) * residue
         dout_ref[...] = dout
         dlow[0, step_at] = dout.astype(BF16)
         lanes = lane_ids((1, 128))
@@ -911,11 +919,11 @@
 
 
 def back_kernel(
-    images, experts, tok_ref, dense_w, ext_ref, cols_ref, back_ref, dlogit_ref, resid_ref,
+    images, real_rows, experts, tok_ref, dense_w, ext_ref, cols_ref, back_ref, dlogit_ref, resid_ref,
     dout_ref, qkv_ref, probs_ref, mixed_ref, loss_ref, gin_ref, gex_ref, far_in, far_ex,
     tgrad_ref, dense_ref, misc_ref, gin_out, gex_out,
     acc, acc_misc, part_in, part_ex, got_in, got_ex, sum_in, sum_ex, more_in, more_ex, came_in, came_ex,
-    low, mate, low_mate, plane, low_plane, line, misc_got, local_sem, w_send, w_recv, d_send, d_recv, m_send, m_recv,
+    low, mate, low_mate, plane, low_plane, line, misc_got, misc_t, local_sem, w_send, w_recv, d_send, d_recv, m_send, m_recv,
 ):
     step_at = pl.program_id(0)
     dp_at, ex_at, near = place()
@@ -1016,7 +1024,13 @@
     gqkv = contract_rows(act_one, dqkv)
     dact_one = contract_cols(dqkv, dense_w[:, : 3 * width])
     grad_one, ggain_one = norm_back(dact_one, normed_one, inverse_one, gain_one)
-    tgrad_ref[...] = dresid + grad_one
+    tgrad = dresid + grad_one
+    for image in range(images):
+
+        @pl.when(step_at == image)
+        def _():
+            tgrad_ref[image * real_rows : (image + 1) * real_rows, :] = tgrad[:real_rows]
+
     ids = row_ids((8, width))
     gmisc = jnp.concatenate(
         [grouter[:8], jnp.where(ids == 0, ggain_one, jnp.where(ids == 1, ggain_two, 0.0))], axis=0
@@ -1090,7 +1104,10 @@
             copy.start()
         misc_step(3)
         misc_step(4)
-        misc_ref[...] = misc_got[9]
+        flat = (dp_at * (2 * low.shape[1]) + ex_at) * shard
+        rows_t = jnp.concatenate([misc_got[9], jnp.zeros((112, misc_got.shape[2]), F32)], axis=0).T
+        misc_t[...] = rows_t
+        misc_ref[...] = misc_t[pl.ds(pl.multiple_of(flat, shard), shard), :]
         for copy in to_line:
             copy.wait_recv()
         result = low_plane[floor].astype(F32)
@@ -1106,6 +1123,75 @@
             )
         for copy in [to_mate] + misc + to_plane + to_line + first_round + second_round + far_round:
             copy.wait_send()
+
+
+def prepare_kernel(
+    images, capacity, cap, tok_ref, target_ref, routes_ref, slots_ref, valid_ref, router_ref, gain_one_ref, gain_two_ref,
+    tok_out, target_out, cols_out, rows_out, extra_out,
+    wide, line,
+):
+    total, width = tok_ref.shape
+    real_rows, rows = total // images, tok_out.shape[1]
+    for source, out in ((tok_ref, tok_out), (target_ref, target_out)):
+        wide[:total, :] = source[...].astype(F32)
+        for image in range(images):
+            piece = wide[image * real_rows : image * real_rows + rows, :]
+            piece = jnp.where(row_ids((rows, 1)) < real_rows, piece, 0.0)
+            out[image] = piece.astype(BF16)
+    me = lax.axis_index("expert")
+    routes, slots = routes_ref[...], slots_ref[...]
+    code = jnp.where(slots < capacity, jnp.bitwise_xor(routes, me) * cap + slots, -1)
+    line[0:2, :total] = code.astype(F32)
+    line[2:4, :total] = routes.astype(F32)
+    line[4:5, :total] = valid_ref[...].astype(F32)
+    lanes = line.shape[1]
+    packed = line[...]
+    for image in range(images):
+        piece = packed[:, image * real_rows : image * real_rows + rows]
+        keep = (lane_ids((8, rows)) < real_rows) & (row_ids((8, rows)) < 5)
+        piece = jnp.where(keep, piece, -1.0)
+        rows_out[image] = piece.astype(jnp.int32)
+        square = jnp.concatenate(
+            [
+                jnp.concatenate([piece, jnp.full((8, round_up(rows, 128) - rows), -1.0, F32)], axis=1),
+                jnp.full((120, round_up(rows, 128)), -1.0, F32),
+            ],
+            axis=0,
+        )
+        cols_out[image] = square.T[:rows, :8].astype(jnp.int32)
+    experts, shard = router_ref.shape
+    tall = jnp.concatenate(
+        [
+            router_ref[...].astype(F32), gain_one_ref[...].astype(F32), gain_two_ref[...].astype(F32),
+            jnp.zeros((126 - experts, shard), F32),
+        ],
+        axis=0,
+    )
+    tall = jnp.concatenate([tall, jnp.zeros((128, 128 - shard), F32)], axis=1)
+    extra_out[...] = tall.T[:shard].astype(BF16)
+
+
+def finish_kernel(
+    real_rows, experts, padded_ref, tgrad_in, dense_ref, misc_ref, gin_in, gex_in,
+    out_ref, loss_ref, tgrad_ref, gain_one_ref, gqkv_ref, gout_ref, gain_two_ref, grouter_ref, gin_ref, gex_ref,
+    joined,
+):
+    images, width = padded_ref.shape[0], padded_ref.shape[2]
+    for image in range(images):
+        joined[image * real_rows : (image + 1) * real_rows, :] = padded_ref[image].astype(F32)[:real_rows]
+    out_ref[...] = joined[: images * real_rows, :].astype(BF16)
+    tgrad_ref[...] = tgrad_in[...]
+    gqkv_ref[...] = dense_ref[:, : 3 * width]
+    gout_ref[...] = dense_ref[:, 3 * width :]
+    own = misc_ref[...]
+    shard = own.shape[0]
+    turned = jnp.concatenate([own, jnp.zeros((128 - shard, 128), F32)], axis=0).T
+    gain_one_ref[...] = turned[8:9, :shard]
+    gain_two_ref[...] = turned[9:10, :shard]
+    grouter_ref[...] = own[:, :experts]
+    loss_ref[...] = own[0:1, 10:11]
+    gin_ref[...] = gin_in[...]
+    gex_ref[...] = gex_in[...].T
 
 
 def shape(dims, kind):
@@ -1140,39 +1226,25 @@
     images = IMG_DEV
     real_rows = tok_rows // images
     rows = round_up(real_rows, 16)
-    me = lax.axis_index("expert")
-
-    def pad_rows(array, value=0):
-        array = array.reshape(images, real_rows, -1)
-        return jnp.pad(array, ((0, 0), (0, rows - real_rows), (0, 0)), constant_values=value)
-
-    valid_f = valid_mask.astype(F32)
-    my_count = jnp.sum(valid_f)
-    count_high = jnp.floor(my_count / 128.0)
-    count_low = my_count - 128.0 * count_high
     shard = qkv_weight.shape[0]
-    small = jnp.concatenate(
-        [
-            router_weight,
-            ln1_gain[:, None],
-            ln2_gain[:, None],
-            jnp.broadcast_to(count_high.astype(BF16), (shard, 1)),
-            jnp.broadcast_to(count_low.astype(BF16), (shard, 1)),
-        ],
-        axis=1,
-    )
-    extra = jnp.pad(small, ((0, 0), (0, 128 - experts - 4)))
+    tok_p, target_p, cols, row_codes, extra = pl.pallas_call(
+        lambda *refs: prepare_kernel(images, capacity, cap, *refs),
+        out_shape=[
+            shape((images, rows, width), BF16), shape((images, rows, width), BF16), shape((images, rows, 8), jnp.int32),
+            shape((images, 8, rows), jnp.int32), shape((shard, 128), BF16),
+        ],
+        scratch_shapes=[
+            pltpu.VMEM((round_up(tok_rows + rows - real_rows, 8), width), F32),
+            pltpu.VMEM((8, round_up(tok_rows + rows - real_rows, 128)), F32),
+        ],
+        compiler_params=params(),
+        name="prepare",
+    )(
+        tokens, targets, routes.T, slot_ids.T, valid_mask[None], router_weight.T, ln1_gain[None], ln2_gain[None],
+    )
     floors = experts // 2
     in_part, ex_part = (width // dp, hidden_width), (hidden_width // dp, width)
     any_space = pl.BlockSpec(memory_space=pl.ANY)
-
-    code = jnp.where(slot_ids < capacity, (routes ^ me) * cap + slot_ids, -1)
-    cols = pad_rows(jnp.concatenate([code, routes], axis=1), -1)
-    row_codes = jnp.pad(cols.transpose(0, 2, 1), ((0, 0), (0, 4), (0, 0)))
-    cols = jnp.pad(cols, ((0, 0), (0, 0), (0, 4)))
-    tok_p = pad_rows(tokens)
-    target_p = pad_rows(targets)
-    valid_p = pad_rows(jnp.broadcast_to(valid_f[:, None], (tok_rows, 8)))
 
     gate_lanes = 128
     dense_lanes = 4 * width + 128
@@ -1201,7 +1273,7 @@
         grid=(images + 4,),
         in_specs=[
             early(rows, width), once((shard, 3 * width)), once((shard, width)), once((shard, 128)),
-            early(rows, 8), early(8, rows), once((images, 8, rows)), once(in_part), once(ex_part),
+            early(rows, 8), early(8, rows), once((images, 8, rows)), once((images, rows, 8)), once(in_part), once(ex_part),
         ],
         out_specs=[
             early(rows, 3 * width), early(HEADS, rows, rows), early(rows, width), early(rows, width),
@@ -1231,7 +1303,7 @@
         ),
         cost_estimate=pl.CostEstimate(flops=int(20e9), bytes_accessed=int(6e7), transcendentals=0),
         name="attention_expert_forward",
-    )(tok_p, qkv_weight, out_weight, extra, cols, row_codes, row_codes, expert_in[0], expert_out[0])
+    )(tok_p, qkv_weight, out_weight, extra, cols, row_codes, row_codes, cols, expert_in[0], expert_out[0])
     returned = returned.reshape(2 * group * cap, width)
 
     flip_part = (width, hidden_width // dp)
@@ -1240,7 +1312,7 @@
         grid=(images + 4,),
         in_specs=[
             once((16, width)), early(rows, width), once((2 * group * cap, width)), early(rows, 8),
-            early(rows, gate_lanes), early(rows, width), early(rows, 8), once((group, images, 8, rows)),
+            early(rows, gate_lanes), early(rows, width), once((group, images, 8, rows)),
             once((group, images, 8, rows)), late(True, cap, width), late(True, cap, hidden_width),
             late(True, cap, hidden_width), any_space, any_space,
         ],
@@ -1269,7 +1341,7 @@
         cost_estimate=pl.CostEstimate(flops=int(24e9), bytes_accessed=int(4e7), transcendentals=0),
         name="combine_expert_backward",
     )(
-        ext, resid, returned, cols, gates, target_p, valid_p, code_all, grow_all, rows_in, hidden, slope,
+        ext, resid, returned, cols, gates, target_p, code_all, grow_all, rows_in, hidden, slope,
         win_all, wex_all,
     )
     grad_back = drows.reshape(2 * group * cap, width)
@@ -1278,7 +1350,7 @@
         return pltpu.VMEM(dims, BF16)
 
     tgrad, dense_grad, misc, gin_own, gex_own = pl.pallas_call(
-        lambda *refs: back_kernel(images, experts, *refs),
+        lambda *refs: back_kernel(images, real_rows, experts, *refs),
         grid=(images,),
         in_specs=[
             per_image(rows, width), whole((width, dense_lanes)), whole((128, width)), per_image(rows, 8),
@@ -1287,10 +1359,10 @@
             *[any_space] * 4,
         ],
         out_specs=[
-            per_image(rows, width), whole((shard, 4 * width)), whole((16, width)), whole(in_part), whole(flip_part),
+            once((tok_rows, width)), whole((shard, 4 * width)), whole((shard, 128)), whole(in_part), whole(flip_part),
         ],
         out_shape=[
-            shape((images, rows, width), F32), shape((shard, 4 * width), F32), shape((16, width), F32),
+            shape((tok_rows, width), F32), shape((shard, 4 * width), F32), shape((shard, 128), F32),
             shape(in_part, F32), shape(flip_part, F32),
         ],
         scratch_shapes=[
@@ -1299,7 +1371,8 @@
             vmem(*in_part), vmem(*flip_part), vmem(*in_part), vmem(*flip_part), vmem(*in_part), vmem(*flip_part),
             vmem(dp, floors, 2, shard, 4 * width), vmem(dp, floors, shard, 4 * width), vmem(dp, floors, shard, 4 * width),
             vmem(3, floors, shard, 4 * width), vmem(floors, shard, 4 * width), vmem(3, shard, 4 * width),
-            pltpu.VMEM((10, 16, width), F32), pltpu.SemaphoreType.DMA((4,)),
+            pltpu.VMEM((10, 16, width), F32), pltpu.VMEM((width, 128), F32),
+            pltpu.SemaphoreType.DMA((4,)),
             *sem_pairs(8), *sem_pairs(8), *sem_pairs(5),
         ],
         compiler_params=pltpu.CompilerParams(
@@ -1311,24 +1384,28 @@
         tok_p, dense_full, ext, cols, grad_back, dlogits, resid, dout, qkv_p, probs, mixed,
         loss_part, gin, gout_t, far_in, far_ex,
     )
-    flat = lax.axis_index("dp") * experts + me
-    mine = lax.dynamic_slice_in_dim(misc, flat * shard, shard, axis=1)
-    loss_value = misc[10, 0]
-
-    def unpad(array):
-        return array[:, :real_rows].reshape(tok_rows, width)
-
+    out, loss, tokens_grad, gain_one_grad, qkv_grad, out_grad, gain_two_grad, router_grad, in_grad, ex_grad = pl.pallas_call(
+        lambda *refs: finish_kernel(real_rows, experts, *refs),
+        out_shape=[
+            shape((tok_rows, width), BF16), shape((1, 1), F32), shape((tok_rows, width), F32), shape((1, shard), F32),
+            shape((shard, 3 * width), F32), shape((shard, width), F32), shape((1, shard), F32),
+            shape((shard, experts), F32), shape(in_part, F32), shape(ex_part, F32),
+        ],
+        scratch_shapes=[pltpu.VMEM((round_up(tok_rows, 8), width), F32)],
+        compiler_params=params(),
+        name="finish",
+    )(block_out, tgrad, dense_grad, misc, gin_own, gex_own)
     return (
-        unpad(block_out),
-        loss_value,
-        unpad(tgrad),
-        mine[8],
-        dense_grad[:, : 3 * width],
-        dense_grad[:, 3 * width :],
-        mine[9],
-        mine[:experts].T,
-        gin_own[None],
-        gex_own.T[None],
+        out,
+        loss.reshape(()),
+        tokens_grad,
+        gain_one_grad.reshape(shard),
+        qkv_grad,
+        out_grad,
+        gain_two_grad.reshape(shard),
+        router_grad,
+        in_grad[None],
+        ex_grad[None],
     )
 
 

time: 293 us -> 281 us (0.959)
  local copies, waits for them, and re-layouts: 19 us -> 1.36 us
  Pallas kernels: 269 us -> 279 us
    pallas_call x1 -> x3, Pallas kernels: 66.8 us -> 76.8 us  [the longest x1 67.6 us: fast_shards(): pl.pallas_call(lambda *refs: back_kernel(images, real_rows, experts, *ref...]
    pad x6 -> x0, local copies, waits for them, and re-layouts: 5.12 us -> none  [the longest x3 3.04 us: pad_rows(): jnp.pad(array, ((0, 0), (0, rows - real_rows), (0, 0)), constant_values=v...]
    slice x5 -> x0, local copies, waits for them, and re-layouts: 4.27 us -> none  [the longest x2 1.82 us: unpad(): return array[:, :real_rows].reshape(tok_rows, width)]
    reshape x6 -> x0, local copies, waits for them, and re-layouts: 3.65 us -> none  [the longest x2 2.77 us: unpad(): return array[:, :real_rows].reshape(tok_rows, width)]
where the time goes in v6:
time: 281 us
  Pallas kernels  279 us (99%)
    pallas_call x1, Pallas kernels, fast_shards(): pl.pallas_call(lambda *refs: front_kernel(images, real_rows, experts, cap...  120 us
    pallas_call x1, Pallas kernels, fast_shards(): pl.pallas_call(lambda *refs: combine_back_kernel(images, cap, group, tota...  82.7 us
    pallas_call x1, Pallas kernels, fast_shards(): pl.pallas_call(lambda *refs: back_kernel(images, real_rows, experts, *ref...  67.6 us

profile of v6, /device:TPU:0, one launch (start us, length us, event | category | flops | bytes accessed | tf_op | source)
XLA Modules:
  0.0 281.2 jit_solution(5741904542060179328)
XLA Ops:
  0.6 3.7 %prepare.1 = (bf16[5,208,512]{2,1,0:T(8,128)(2,1)}, bf16[5,208,512]{2,1,0:T(8,128)(2,1)}, s32[5,208,8]{2,1,0:T(8,128)}, s32[5,8,208]{2,1,0:T(8,128)}, bf16[16,128]{1,0:T(8,128)(2,1)}) custom-call(bf16[985,512]{1,0:T(8,128)(2,1)} %refs_0_.1, bf16[985,512]{1,0:T(8,128)(2,1)} %refs_1_.2, s32[2,985]{1,0:T(2,128)} %bitcast.15, s32[2,985]{1,0:T(2,128)} %bitcast.16, ...), custom_call_target="tpu_custom_call" | custom-call | tf_op jit(solution)/shard_map/prepare/pallas_call | solution.py:1230
  4.4 119.6 %attention_expert_forward.1 = (bf16[5,208,1536]{2,1,0:T(8,128)(2,1)}, bf16[5,8,208,208]{3,2,1,0:T(8,128)(2,1)}, bf16[5,208,512]{2,1,0:T(8,128)(2,1)}, f32[5,208,...) custom-call(bf16[5,208,512]{2,1,0:T(8,128)(2,1)} %get-tuple-element., ...), custom_call_target="tpu_custom_call" | custom-call | flops 20000000000 | bytes 60000000 | tf_op jit(solution)/shard_map/attention_expert_forward/pallas_call | solution.py:1271
  124.0 82.7 %combine_expert_backward.1 = (bf16[5,208,512]{2,1,0:T(8,128)(2,1)}, f32[5,208,512]{2,1,0:T(8,128)}, f32[5,208,128]{2,1,0:T(8,128)}, f32[8,128]{1,0:T(8,128)}, bf...) custom-call(f32[128,512]{1,0:T(8,128)} %get-tuple-element.58.refs_0_, ...), custom_call_target="tpu_custom_call" | custom-call | flops 24000000000 | bytes 40000000 | tf_op jit(solution)/shard_map/combine_expert_backward/pallas_call | solution.py:1310
  206.8 67.6 %attention_backward.1 = (f32[985,512]{1,0:T(8,128)}, f32[16,2048]{1,0:T(8,128)}, f32[16,128]{1,0:T(8,128)}, f32[128,2048]{1,0:T(8,128)}, f32[512,512]{1,0:T(8,128)}) custom-call(bf16[5,208,512]{2,1,0:T(8,128)(2,1)} %get-tuple-element.54.refs_0_, bf16[512,2176]{1,0:T(8,128)(2,1)} %get-tuple-element.71.refs_1_, f32[128,512]{1,0:T(8,128)} %get-tuple-element.58.refs_0_.refs_2_, ...), custom_call_target="tpu_custom_call" | custom-call | flops 10000000000 | bytes 30000000 | tf_op jit(solution)/shard_map/attention_backward/pallas_call | solution.py:1352
  274.4 5.5 %finish.1 = (bf16[985,512]{1,0:T(8,128)(2,1)}, f32[1,1]{1,0:T(1,128)}, f32[985,512]{1,0:T(8,128)}, f32[1,16]{1,0:T(1,128)}, f32[16,1536]{1,0:T(8,128)}, /*index=...) custom-call(bf16[5,208,512]{2,1,0:T(8,128)(2,1)} %get-tuple-element.70.refs_0_, ...), custom_call_target="tpu_custom_call" | custom-call | tf_op jit(solution)/shard_map/finish/pallas_call | solution.py:1387
  279.9 1.4 copy.22

commit v7 on v6

--- a/solution.py
+++ b/solution.py
@@ -740,11 +740,22 @@
         pltpu.make_async_copy(low_ex.at[0], gex_ref, local_sem.at[8]),
     ]
     tensors = [(low_in, got_in, sum_in, more_in, far_in, 1, 2), (low_ex, got_ex, sum_ex, more_ex, far_ex, 2, 1)]
-    spread, second_round = [], []
-    for t, (grad, got, passed, more, _, first, second) in enumerate(tensors):
-        for s, owner in enumerate((near[first], near[3])):
-            spread.append(send(grad.at[1, owner], got.at[s], wsem, 3 * t + s, (near[first], ex_at)))
-        second_round.append(send(passed, more, wsem, 3 * t + 2, (near[second], ex_at)))
+    parts, width, hidden_width = win_buf.shape[1], dlow.shape[3], win_buf.shape[3]
+    step_width = hidden_width // parts
+    spread_in, spread_ex = [], []
+    for s, owner in enumerate((near[1], near[3])):
+        for part in range(parts):
+            cut = slice(part * step_width, (part + 1) * step_width)
+            spread_in.append(
+                send(low_in.at[1, owner, :, cut], got_in.at[s, :, cut], wsem, 4 + parts * s + part, (near[1], ex_at))
+            )
+    for s, owner in enumerate((near[2], near[3])):
+        spread_ex.append(send(low_ex.at[1, owner], got_ex.at[s], wsem, s, (near[2], ex_at)))
+    spread = spread_in + spread_ex
+    second_round = [
+        send(passed, more, wsem, 2 + t, (near[second], ex_at))
+        for t, (_, _, passed, more, _, _, second) in enumerate(tensors)
+    ]
 
     def to_mate(step):
         return send(dlow.at[0, step], dlow.at[1, step], tsem, step, mate)
@@ -879,6 +890,19 @@
                 low_in[which, :, :, cut] = total_in.reshape(parts, width // parts, step)
                 low_ex[which, offset // step] = (acc_out[:, cut] + gout).astype(BF16)
 
+            part = offset // step
+
+            @pl.when(at_expert == 1)
+            def _():
+                for s in range(2):
+                    spread_in[parts * s + part].start()
+
+            for s, owner in enumerate((near[2], near[3])):
+
+                @pl.when((at_expert == 1) & (owner == part))
+                def _():
+                    spread_ex[s].start()
+
         out_buf[which, pl.ds(half * blocks, blocks)] = result.astype(BF16).reshape(blocks, cap, width)
 
     for step in range(4):
@@ -887,9 +911,6 @@
         def _():
             for copy in returns(step):
                 copy.start()
-            if step == 1:
-                for copy in spread:
-                    copy.start()
 
     @pl.when(step_at == images + 3)
     def _():
@@ -1188,7 +1209,7 @@
     turned = jnp.concatenate([own, jnp.zeros((128 - shard, 128), F32)], axis=0).T
     gain_one_ref[...] = turned[8:9, :shard]
     gain_two_ref[...] = turned[9:10, :shard]
-    grouter_ref[...] = own[:, :experts]
+    grouter_ref[...] = turned[:experts, :shard]
     loss_ref[...] = own[0:1, 10:11]
     gin_ref[...] = gin_in[...]
     gex_ref[...] = gex_in[...].T
@@ -1333,7 +1354,7 @@
             pltpu.VMEM((2, dp, *in_part), BF16), pltpu.VMEM((2, dp, *flip_part), BF16),
             pltpu.VMEM((2, group, cap, width), BF16),
             *[pltpu.VMEM(dims, BF16) for dims in ((2, *in_part), (2, *flip_part), in_part, flip_part, in_part, flip_part)],
-            *sem_pairs(3 * images), *sem_pairs(8), *sem_pairs(6), pltpu.SemaphoreType.DMA((9,)),
+            *sem_pairs(3 * images), *sem_pairs(8), *sem_pairs(4 + 2 * dp), pltpu.SemaphoreType.DMA((9,)),
         ],
         compiler_params=pltpu.CompilerParams(
             vmem_limit_bytes=62 * MB, collective_id=5, has_side_effects=True
@@ -1389,7 +1410,7 @@
         out_shape=[
             shape((tok_rows, width), BF16), shape((1, 1), F32), shape((tok_rows, width), F32), shape((1, shard), F32),
             shape((shard, 3 * width), F32), shape((shard, width), F32), shape((1, shard), F32),
-            shape((shard, experts), F32), shape(in_part, F32), shape(ex_part, F32),
+            shape((experts, shard), F32), shape(in_part, F32), shape(ex_part, F32),
         ],
         scratch_shapes=[pltpu.VMEM((round_up(tok_rows, 8), width), F32)],
         compiler_params=params(),
@@ -1403,7 +1424,7 @@
         qkv_grad,
         out_grad,
         gain_two_grad.reshape(shard),
-        router_grad,
+        router_grad.T,
         in_grad[None],
         ex_grad[None],
     )

time: 281 us -> 279 us (level)
  no operation moved by 1% of the time
where the time goes in v7:
time: 279 us
  Pallas kernels  278 us (100%)
    pallas_call x1, Pallas kernels, fast_shards(): pl.pallas_call(lambda *refs: front_kernel(images, real_rows, experts, cap...  120 us
    pallas_call x1, Pallas kernels, fast_shards(): pl.pallas_call(lambda *refs: combine_back_kernel(images, cap, group, tota...  81 us
    pallas_call x1, Pallas kernels, fast_shards(): pl.pallas_call(lambda *refs: back_kernel(images, real_rows, experts, *ref...  68.2 us

profile of v7, /device:TPU:0, one launch (start us, length us, event | category | flops | bytes accessed | tf_op | source)
XLA Modules:
  0.0 278.7 jit_solution(13027789761926890896)
XLA Ops:
  0.6 3.7 %prepare.1 = (bf16[5,208,512]{2,1,0:T(8,128)(2,1)}, bf16[5,208,512]{2,1,0:T(8,128)(2,1)}, s32[5,208,8]{2,1,0:T(8,128)}, s32[5,8,208]{2,1,0:T(8,128)}, bf16[16,128]{1,0:T(8,128)(2,1)}) custom-call(bf16[985,512]{1,0:T(8,128)(2,1)} %refs_0_.1, bf16[985,512]{1,0:T(8,128)(2,1)} %refs_1_.2, s32[2,985]{1,0:T(2,128)} %bitcast.16, s32[2,985]{1,0:T(2,128)} %bitcast.17, ...), custom_call_target="tpu_custom_call" | custom-call | tf_op jit(solution)/shard_map/prepare/pallas_call | solution.py:1251
  4.4 119.6 %attention_expert_forward.1 = (bf16[5,208,1536]{2,1,0:T(8,128)(2,1)}, bf16[5,8,208,208]{3,2,1,0:T(8,128)(2,1)}, bf16[5,208,512]{2,1,0:T(8,128)(2,1)}, f32[5,208,...) custom-call(bf16[5,208,512]{2,1,0:T(8,128)(2,1)} %get-tuple-element., ...), custom_call_target="tpu_custom_call" | custom-call | flops 20000000000 | bytes 60000000 | tf_op jit(solution)/shard_map/attention_expert_forward/pallas_call | solution.py:1292
  124.0 81.0 %combine_expert_backward.1 = (bf16[5,208,512]{2,1,0:T(8,128)(2,1)}, f32[5,208,512]{2,1,0:T(8,128)}, f32[5,208,128]{2,1,0:T(8,128)}, f32[8,128]{1,0:T(8,128)}, bf...) custom-call(f32[128,512]{1,0:T(8,128)} %get-tuple-element.58.refs_0_, ...), custom_call_target="tpu_custom_call" | custom-call | flops 24000000000 | bytes 40000000 | tf_op jit(solution)/shard_map/combine_expert_backward/pallas_call | solution.py:1331
  205.0 68.2 %attention_backward.1 = (f32[985,512]{1,0:T(8,128)}, f32[16,2048]{1,0:T(8,128)}, f32[16,128]{1,0:T(8,128)}, f32[128,2048]{1,0:T(8,128)}, f32[512,512]{1,0:T(8,128)}) custom-call(bf16[5,208,512]{2,1,0:T(8,128)(2,1)} %get-tuple-element.54.refs_0_, bf16[512,2176]{1,0:T(8,128)(2,1)} %get-tuple-element.71.refs_1_, f32[128,512]{1,0:T(8,128)} %get-tuple-element.58.refs_0_.refs_2_, ...), custom_call_target="tpu_custom_call" | custom-call | flops 10000000000 | bytes 30000000 | tf_op jit(solution)/shard_map/attention_backward/pallas_call | solution.py:1373
  273.2 5.5 %finish.1 = (bf16[985,512]{1,0:T(8,128)(2,1)}, f32[1,1]{1,0:T(1,128)}, f32[985,512]{1,0:T(8,128)}, f32[1,16]{1,0:T(1,128)}, f32[16,1536]{1,0:T(8,128)}, /*index=...) custom-call(bf16[5,208,512]{2,1,0:T(8,128)(2,1)} %get-tuple-element.70.refs_0_, ...), custom_call_target="tpu_custom_call" | custom-call | tf_op jit(solution)/shard_map/finish/pallas_call | solution.py:1408

commit v8 on v7

--- a/solution.py
+++ b/solution.py
@@ -677,10 +677,15 @@
             copy.wait_recv()
         for copy in ex_far_passed:
             copy.wait_recv()
+        for block, copy in reversed(list(enumerate(returns(2)))):
+            result = None
+            for part in range(parts):
+                cut = slice(part * step_width, (part + 1) * step_width)
+                term = dot(kept[block, :, cut], wex_buf[1, part])
+                result = term if result is None else result + term
+            out_buf[1, blocks + block] = result.astype(BF16)
+            copy.start()
         for copy in stores:
-            copy.start()
-        second_product(kept, 1, 1)
-        for copy in returns(2):
             copy.start()
 
     @pl.when((step_at >= images) & (step_at != images + 2))
@@ -870,6 +875,17 @@
         step = hidden_width // parts
         result = None
         for offset in range(0, hidden_width, step):
+            if offset == hidden_width - step:
+
+                @pl.when(at_expert == 3)
+                def _():
+                    for copy in spread:
+                        copy.wait_recv()
+                    for grad, got, passed, _, _, _, second in tensors:
+                        passed[...] = (grad[1, near[second]].astype(F32) + got[1].astype(F32)).astype(BF16)
+                    for copy in second_round:
+                        copy.start()
+
             cut = slice(offset, offset + step)
             hidden = hidden_ref[:, :, cut].reshape(blocks * cap, step)
             slope = slope_ref[:, :, cut].reshape(blocks * cap, step).astype(F32)
@@ -915,12 +931,6 @@
     @pl.when(step_at == images + 3)
     def _():
         for copy in stores:
-            copy.start()
-        for copy in spread:
-            copy.wait_recv()
-        for grad, got, passed, _, _, _, second in tensors:
-            passed[...] = (grad[1, near[second]].astype(F32) + got[1].astype(F32)).astype(BF16)
-        for copy in second_round:
             copy.start()
         for step in range(4):
             for copy in returns(step):

time: 279 us -> 279 us (level)
  no operation moved by 1% of the time
where the time goes in v8:
time: 279 us
  Pallas kernels  278 us (100%)
    pallas_call x1, Pallas kernels, fast_shards(): pl.pallas_call(lambda *refs: front_kernel(images, real_rows, experts, cap...  119 us
    pallas_call x1, Pallas kernels, fast_shards(): pl.pallas_call(lambda *refs: combine_back_kernel(images, cap, group, tota...  81 us
    pallas_call x1, Pallas kernels, fast_shards(): pl.pallas_call(lambda *refs: back_kernel(images, real_rows, experts, *ref...  68.2 us

profile of v8, /device:TPU:0, one launch (start us, length us, event | category | flops | bytes accessed | tf_op | source)
XLA Modules:
  0.0 278.5 jit_solution(2461669337855689269)
XLA Ops:
  0.6 3.7 %prepare.1 = (bf16[5,208,512]{2,1,0:T(8,128)(2,1)}, bf16[5,208,512]{2,1,0:T(8,128)(2,1)}, s32[5,208,8]{2,1,0:T(8,128)}, s32[5,8,208]{2,1,0:T(8,128)}, bf16[16,128]{1,0:T(8,128)(2,1)}) custom-call(bf16[985,512]{1,0:T(8,128)(2,1)} %refs_0_.1, bf16[985,512]{1,0:T(8,128)(2,1)} %refs_1_.2, s32[2,985]{1,0:T(2,128)} %bitcast.16, s32[2,985]{1,0:T(2,128)} %bitcast.17, ...), custom_call_target="tpu_custom_call" | custom-call | tf_op jit(solution)/shard_map/prepare/pallas_call | solution.py:1261
  4.4 119.4 %attention_expert_forward.1 = (bf16[5,208,1536]{2,1,0:T(8,128)(2,1)}, bf16[5,8,208,208]{3,2,1,0:T(8,128)(2,1)}, bf16[5,208,512]{2,1,0:T(8,128)(2,1)}, f32[5,208,...) custom-call(bf16[5,208,512]{2,1,0:T(8,128)(2,1)} %get-tuple-element., ...), custom_call_target="tpu_custom_call" | custom-call | flops 20000000000 | bytes 60000000 | tf_op jit(solution)/shard_map/attention_expert_forward/pallas_call | solution.py:1302
  123.8 81.0 %combine_expert_backward.1 = (bf16[5,208,512]{2,1,0:T(8,128)(2,1)}, f32[5,208,512]{2,1,0:T(8,128)}, f32[5,208,128]{2,1,0:T(8,128)}, f32[8,128]{1,0:T(8,128)}, bf...) custom-call(f32[128,512]{1,0:T(8,128)} %get-tuple-element.58.refs_0_, ...), custom_call_target="tpu_custom_call" | custom-call | flops 24000000000 | bytes 40000000 | tf_op jit(solution)/shard_map/combine_expert_backward/pallas_call | solution.py:1341
  204.8 68.2 %attention_backward.1 = (f32[985,512]{1,0:T(8,128)}, f32[16,2048]{1,0:T(8,128)}, f32[16,128]{1,0:T(8,128)}, f32[128,2048]{1,0:T(8,128)}, f32[512,512]{1,0:T(8,128)}) custom-call(bf16[5,208,512]{2,1,0:T(8,128)(2,1)} %get-tuple-element.54.refs_0_, bf16[512,2176]{1,0:T(8,128)(2,1)} %get-tuple-element.71.refs_1_, f32[128,512]{1,0:T(8,128)} %get-tuple-element.58.refs_0_.refs_2_, ...), custom_call_target="tpu_custom_call" | custom-call | flops 10000000000 | bytes 30000000 | tf_op jit(solution)/shard_map/attention_backward/pallas_call | solution.py:1383
  273.0 5.5 %finish.1 = (bf16[985,512]{1,0:T(8,128)(2,1)}, f32[1,1]{1,0:T(1,128)}, f32[985,512]{1,0:T(8,128)}, f32[1,16]{1,0:T(1,128)}, f32[16,1536]{1,0:T(8,128)}, /*index=...) custom-call(bf16[5,208,512]{2,1,0:T(8,128)(2,1)} %get-tuple-element.70.refs_0_, ...), custom_call_target="tpu_custom_call" | custom-call | tf_op jit(solution)/shard_map/finish/pallas_call | solution.py:1418
